TPU v7x, 256 devices: a whole 4x4x8 slice. The times are simulated.
256 devices in a mesh: owner: 64 (over y, z, core), help: 4 (over x).
Axes of the slice: x: 4, y: 4, z: 8, core: 2. Of those that a mesh axis runs over, the one named last changes fastest.
Arguments:
- embeddings: bfloat16 [262144, 768], P(('owner', 'help')), may hold values from -8 to 8
- cluster_ids: int32 [262144, 1], P(('owner', 'help')), may hold values from 0 to 127; in each aligned block of 1024 rows (0 to 1023, 1024 to 2047, ...) at most 16 rows name the same one
Outputs:
- nearest: float32 [262144], P(('owner', 'help'))
- centre_cosine: float32 [262144], P(('owner', 'help'))
- centroids: float32 [128, 768], P('owner')
Inputs may be any that keep to these rules, and one draw needn't show every extreme that they name: `cluster_ids`: within the rows of one device no cluster is named more than 16 times, a bound that some block reaches; every cluster is named by some row.
All inputs are finite; a program needn't handle non-finite values.
Results may differ from a plain program's by a relative error of at most 0.0003.
Values may be sent and summed in bfloat16 or wider, within the bound.
No kernel may reach another device: no remote copies, remote signals or barrier semaphores. Data moves between devices by JAX's collectives and lax.ppermute only.
A program may use at most 64 MiB of HBM per device.

v0:
```python
import jax
import jax.numpy as jnp
from jax import lax
from jax.sharding import PartitionSpec as P

CL_OWN = 2


EPS = 1e-06


def inverse_norms(block, width):
    squares = jnp.einsum("ksd,ksd->ks", block, block, preferred_element_type=jnp.float32)
    return lax.rsqrt(squares / width + EPS)


def cosines(mine, mine_inv, other, other_inv, width):
    dots = jnp.einsum("ksd,kpd->ksp", mine, other, preferred_element_type=jnp.float32)
    return dots * mine_inv[:, :, None] * other_inv[:, None, :] / width


def shards(embeddings, cluster_ids):
    rows, width = embeddings.shape
    owners = lax.axis_size("owner")
    clusters = CL_OWN * owners
    cap = rows // owners
    ids = cluster_ids[:, 0]
    onehot = (ids[:, None] == jnp.arange(clusters, dtype=jnp.int32)[None, :]).astype(jnp.int32)
    rank = jnp.sum((jnp.cumsum(onehot, axis=0) - onehot) * onehot, axis=1)
    position = (ids % CL_OWN * owners + ids // CL_OWN) * cap + rank
    send = jnp.zeros((CL_OWN * owners * cap, width), jnp.bfloat16).at[position].set(embeddings)
    flags = jnp.zeros((CL_OWN * owners * cap,), jnp.bfloat16).at[position].set(1.0)
    send = send.reshape(CL_OWN, owners, cap, width)
    flags = flags.reshape(CL_OWN, owners, cap)
    got, got_flags = (
        lax.all_to_all(send, "owner", split_axis=1, concat_axis=1, tiled=True),
        lax.all_to_all(flags, "owner", split_axis=1, concat_axis=1, tiled=True),
    )
    members = owners * cap
    block = got.reshape(CL_OWN, members, width)
    alive = got_flags.reshape(CL_OWN, members)
    inv = inverse_norms(block, width)
    base = lax.axis_index("help") * members
    mine_index = base + jnp.arange(members, dtype=jnp.int32)
    start_best = jnp.full((CL_OWN, members), -1.0, jnp.float32)
    other = lax.all_gather(block, "help", axis=1, tiled=True)
    other_live = lax.all_gather(alive, "help", axis=1, tiled=True)
    count = other.shape[1]
    cosine = cosines(block, inv, other, inverse_norms(other, width), width)
    other_index = jnp.arange(count, dtype=jnp.int32)
    keep = (other_live[:, None, :] > 0) & (other_index[None, None, :] != mine_index[None, :, None])
    best = jnp.maximum(start_best, jnp.max(jnp.where(keep, cosine, -1.0), axis=2))
    partial_totals = jnp.einsum("ks,ksd->kd", alive, block, preferred_element_type=jnp.float32)
    partial_counts = jnp.sum(alive.astype(jnp.float32), axis=1)
    totals, counts = lax.psum((partial_totals, partial_counts), "help")
    means = totals / counts[:, None]
    toward = jnp.einsum(
        "ksd,kd->ks", block.astype(jnp.float32), totals, precision=lax.Precision.HIGHEST
    )
    scale = lax.rsqrt(jnp.sum(totals * totals, axis=1) / width + EPS)
    centre = toward * inv * scale[:, None] / width
    back_best, back_centre = (
        lax.all_to_all(
            best.reshape(CL_OWN, owners, cap), "owner", split_axis=1, concat_axis=1, tiled=True
        ),
        lax.all_to_all(
            centre.reshape(CL_OWN, owners, cap), "owner", split_axis=1, concat_axis=1, tiled=True
        ),
    )
    nearest = back_best.reshape(-1)[position]
    centre_cosine = back_centre.reshape(-1)[position]
    return (nearest, centre_cosine, means)


def solution(mesh):
    placed = (P(("owner", "help"), None), P(("owner", "help"), None))
    return jax.shard_map(
        shards,
        mesh=mesh,
        in_specs=placed,
        out_specs=(P(("owner", "help")), P(("owner", "help")), P("owner", None)),
        check_vma=False,
    )
```

profile of v0, /device:TPU:2, one launch (start us, length us, event | category | flops | bytes accessed | tf_op | source)
XLA Modules:
  0.0 292.5 jit_solution(15214158843559421701)
XLA Ops:
  7.2 0.0 all-gather.2.cloned.1.call-start
  7.2 0.8 copy.8
  8.0 0.2 fusion.6
  8.3 0.1 copy.9
  8.4 1.0 fusion.5
  9.5 0.7 compare_select_fusion
  10.2 7.9 %scatter_custom_fusion.1 = bf16[2048,768]{1,0:T(8,128)(2,1)} fusion(s32[1024]{0:T(1024)S(1)} %bitcast.44, bf16[1024,768]{1,0:T(8,128)(2,1)} %param.2, bf16[]{:T(256)} %constant.26.clone.1), kind=kCustom, calls=%fused_computation.10 | custom fusion | bytes 3146240 | tf_op jit(solution)/shard_map/scatter | solution.py:31
  18.1 2.3 copy.12
  20.4 85.0 %all_to_all.20 = bf16[2,64,16,768]{3,2,0,1:T(8,128)(2,1)S(1)} all-to-all(bf16[2,64,16,768]{3,2,0,1:T(8,128)(2,1)S(1)} %copy.12), channel_id=1, replica_groups=mesh['owner'=64,'help'=4] {'owner'}, dimensions={1} | all-to-all | bytes 6291456 | tf_op jit(solution)/shard_map/all_to_all | solution.py:36
  105.4 1.9 copy.13
  107.3 0.0 copy-start
  107.3 0.0 all-gather.2.cloned.1.call-update
  107.4 7.6 %scatter_custom_fusion = bf16[2048]{0:T(1024)(128)(2,1)S(1)} fusion(s32[1024]{0:T(1024)S(1)} %bitcast.45, bf16[1024]{0:T(1024)(128)(2,1)S(1)} %broadcast.99, bf16[]{:T(256)} %constant.26.clone.1), kind=kCustom, calls=%fused_computation.45 | custom fusion | bytes 4098 | tf_op jit(solution)/shard_map/scatter | solution.py:32
  115.0 0.1 reshape.86
  115.1 0.6 copy.10
  115.7 6.8 %all-to-all-start = ((bf16[2,64,16]{2,0,1:T(2,128)(2,1)}), bf16[2,64,16]{2,0,1:T(2,128)(2,1)S(1)}, u32[]{:S(2)}, u32[]{:S(2)}) async-start(bf16[2,64,16]{2,0,1:T(2,128)(2,1)} %copy.10), calls=%async_computation | async-start | bytes 65536 | tf_op jit(solution)/shard_map/all_to_all | solution.py:37
  122.5 5.3 %iota_compare_fusion = pred[1024,4096]{1,0:T(8,128)(4,1)} fusion(s32[1024]{0:T(1024)S(1)} %iota_add_fusion), kind=kLoop, calls=%fused_computation.7 | loop fusion | flops 4194304 | bytes 4198400 | tf_op jit(solution)/shard_map/ne | solution.py:51
  127.8 4.0 %all-to-all-done = bf16[2,64,16]{2,0,1:T(2,128)(2,1)S(1)} async-done(((bf16[2,64,16]{2,0,1:T(2,128)(2,1)}), bf16[2,64,16]{2,0,1:T(2,128)(2,1)S(1)}, u32[]{:S(2)}, u32[]{:S(2)}) %all-to-all-start) | async-done | bytes 4128 | tf_op jit(solution)/shard_map/all_to_all | solution.py:37
  131.8 0.1 reshape.87
  131.9 0.1 reshape.134
  132.0 12.0 %all_gather.6 = bf16[2,4096]{1,0:T(2,128)(2,1)S(1)} all-gather(bf16[2,1024]{1,0:T(2,128)(2,1)S(1)} %reshape.87), channel_id=1, replica_groups=mesh['owner'=64,'help'=4] {'help'}, dimensions={1}, use_global_device_ids=true | all-gather | bytes 20480 | tf_op jit(solution)/shard_map/all_gather | solution.py:47
  144.0 0.2 convert_reduce_fusion
  144.2 0.0 copy-done
  144.2 0.5 fusion.17
  144.8 8.9 %all-reduce = (f32[2,768]{1,0:T(2,128)S(1)}, f32[2]{0:T(128)S(1)}) all-reduce(f32[2,768]{1,0:T(2,128)S(1)} %bitcast.41, f32[2]{0:T(128)S(1)} %convert_reduce_fusion), channel_id=1, replica_groups=mesh['owner'=64,'help'=4] {'help'}, use_global_device_ids=true, to_apply=%region_6.7 | all-reduce | flops 1538 | bytes 12304 | tf_op jit(solution)/shard_map/psum | solution.py:55
  153.7 0.8 broadcast_divide_fusion
  154.5 2.5 fusion.11
  157.0 0.7 fusion.1
  157.7 0.1 fusion.10
  157.8 0.1 reshape.91
  157.9 0.7 copy.16
  158.6 6.4 %all-to-all-start.3 = ((f32[2,64,16]{2,0,1:T(2,128)}), f32[2,64,16]{2,0,1:T(2,128)S(1)}, u32[]{:S(2)}, u32[]{:S(2)}) async-start(f32[2,64,16]{2,0,1:T(2,128)} %copy.16), calls=%async_computation.3 | async-start | bytes 131072 | tf_op jit(solution)/shard_map/all_to_all | solution.py:66
  164.9 61.5 %all-gather.2.cloned.1.call-done = bf16[2,4096,768]{2,1,0:T(8,128)(2,1)} async-done(((bf16[2,1024,768]{2,1,0:T(8,128)(2,1)}), bf16[2,4096,768]{2,1,0:T(8,128)(2,1)}) %all-gather.2.cloned.1.call-update) | async-done | bytes 12582928 | tf_op jit(solution)/shard_map/all_gather | solution.py:46
  226.4 7.1 %fusion = f32[2,4096]{1,0:T(2,128)S(1)} fusion(bf16[2,4096,768]{2,1,0:T(8,128)(2,1)} %all-gather.2.cloned.1.call-done), kind=kLoop, calls=%fused_computation.6 | loop fusion | flops 18866176 | bytes 12615680 | tf_op jit(solution)/shard_map/ksd,ksd->ks/dot_general | solution.py:13
  233.6 19.5 %select_reduce_fusion = f32[2,1024]{1,0:T(2,128)S(1)} fusion(f32[2,4096]{1,0:T(2,128)S(1)} %add_rsqrt_fusion, f32[2,1024]{1,0:T(2,128)S(1)} %get-tuple-element.6, pred[1024,4096]{1,0:T(8,128)(4,1)} %iota_compare_fusion, pred[2,4096]{1,0:T(4,128)(4,1)S(1)} %broadcast_compare_fusion, bf16[2,1024,768]{2,1,0:T(8,128)(2,1)S(1)} %bitcast.37, ...), kind=kOutput, calls=%fused_computation.4 | convolution fusion | flops 12935231488 | bytes 19980288 | tf_op jit(solution)/shard_map/ksd,kpd->ksp/dot_general | solution.py:18
  253.2 0.1 max_broadcast_in_dim.8
  253.2 0.7 copy.14
  253.9 0.0 all-to-all-done.3
  253.9 10.5 %all-to-all-start.2 = ((f32[2,64,16]{2,0,1:T(2,128)}), f32[2,64,16]{2,0,1:T(2,128)S(1)}, u32[]{:S(2)}, u32[]{:S(2)}) async-start(f32[2,64,16]{2,0,1:T(2,128)} %copy.14), calls=%async_computation.2 | async-start | bytes 131072 | tf_op jit(solution)/shard_map/all_to_all | solution.py:63
  264.4 0.1 reshape.92
  264.5 10.5 %gather_fusion.1 = f32[1024]{0:T(1024)} fusion(f32[2048]{0:T(1024)S(1)} %reshape.92, s32[1024]{0:T(1024)S(1)} %broadcast_clamp_fusion), kind=kCustom, calls=%fused_computation.1 | custom fusion | bytes 12288 | tf_op jit(solution)/shard_map/gather | solution.py:71
  275.0 0.0 all-to-all-done.2
  275.1 0.1 reshape.90
  275.1 10.5 %gather_fusion = f32[1024]{0:T(1024)} fusion(f32[2048]{0:T(1024)S(1)} %reshape.90, s32[1024]{0:T(1024)S(1)} %broadcast_clamp_fusion), kind=kCustom, calls=%fused_computation | custom fusion | bytes 12288 | tf_op jit(solution)/shard_map/gather | solution.py:70
  (15 shorter events, 0.2 us)
Async XLA Ops:
  7.2 219.3 %all-gather.2.cloned.1.call-start = ((), (), s32[]{:S(2)}) async-start(), calls=%async_computation.4 | async-start | bytes 15728640 | tf_op jit(solution)/shard_map/all_gather | solution.py:46
  107.3 36.9 %copy-start = (bf16[2,64,16,768]{3,2,1,0:T(8,128)(2,1)S(1)}, bf16[2,64,16,768]{3,2,1,0:T(8,128)(2,1)}, u32[]{:S(2)}) copy-start(bf16[2,64,16,768]{3,2,1,0:T(8,128)(2,1)} %copy.13) | copy-start | bytes 9437188
  115.7 16.1 %all-to-all-start = ((bf16[2,64,16]{2,0,1:T(2,128)(2,1)}), bf16[2,64,16]{2,0,1:T(2,128)(2,1)S(1)}, u32[]{:S(2)}, u32[]{:S(2)}) async-start(bf16[2,64,16]{2,0,1:T(2,128)(2,1)} %copy.10), calls=%async_computation | async-start | bytes 65536 | tf_op jit(solution)/shard_map/all_to_all | solution.py:37
  158.6 95.3 %all-to-all-start.3 = ((f32[2,64,16]{2,0,1:T(2,128)}), f32[2,64,16]{2,0,1:T(2,128)S(1)}, u32[]{:S(2)}, u32[]{:S(2)}) async-start(f32[2,64,16]{2,0,1:T(2,128)} %copy.16), calls=%async_computation.3 | async-start | bytes 131072 | tf_op jit(solution)/shard_map/all_to_all | solution.py:66
  253.9 21.1 %all-to-all-start.2 = ((f32[2,64,16]{2,0,1:T(2,128)}), f32[2,64,16]{2,0,1:T(2,128)S(1)}, u32[]{:S(2)}, u32[]{:S(2)}) async-start(f32[2,64,16]{2,0,1:T(2,128)} %copy.14), calls=%async_computation.2 | async-start | bytes 131072 | tf_op jit(solution)/shard_map/all_to_all | solution.py:63
Sparse Core Ops, SparseCore 0:
  107.5 118.9 all-gather.1
where the time goes:
time: 294 us; the launch traced here: 293 us
  blocking collectives  106 us (36%)
  waiting for transfers between devices  65.6 us (22%)
  local copies, waits for them, and re-layouts  44.3 us (15%)
  starting transfers between devices  23.7 us (8%)
  matrix products  22.6 us (8%)
  other arithmetic  16.3 us (6%)
  between operations  14.2 us (5%)
    all_to_all x1, blocking collectives, shards(): lax.all_to_all(send, 'owner', split_axis=1, concat_axis=1, tiled=True)  85 us
    all_gather x1, waiting for transfers between devices, shards(): other = lax.all_gather(block, 'help', axis=1, tiled=True)  61.5 us
    dot_general x1, matrix products, cosines(): jnp.einsum('ksd,kpd->ksp', mine, other, preferred_element_type=jnp.float32)  19.5 us
    all_gather x1, blocking collectives, shards(): other_live = lax.all_gather(alive, 'help', axis=1, tiled=True)  12 us
    gather x1, local copies, waits for them, and re-layouts, shards(): centre_cosine = back_centre.reshape(-1)[position]  10.5 us
    gather x1, local copies, waits for them, and re-layouts, shards(): nearest = back_best.reshape(-1)[position]  10.5 us
    all_to_all x1, starting transfers between devices, shards(): lax.all_to_all(best.reshape(CL_OWN, owners, cap), 'owner', split_axis=1,...  10.5 us
    psum x1, blocking collectives, shards(): totals, counts = lax.psum((partial_totals, partial_counts), 'help')  8.93 us
  transfers between devices with their start and end apart: 4, of which 2 were waited for; matrix products, arithmetic and copies ran while one was open for 20% of the time, Pallas kernels for 0%

commit v1 on v0

v1 whole, which is shorter than its diff:
```python
import jax
import jax.numpy as jnp
from jax import lax
from jax.experimental import pallas as pl
from jax.experimental.pallas import tpu as pltpu
from jax.sharding import Mesh, PartitionSpec as P

EPS = 1e-06
ROWS = 1024
WIDTH = 768
CAP = 16
CHIPS = 128
SLOTS = CHIPS * CAP
MARK = 64.0
LOW = -1e30
TILE = 512
NT = (((1,), (1,)), ((), ()))
TN = (((0,), (0,)), ((), ()))
F32 = jnp.float32
BF16 = jnp.bfloat16


def iota(shape, dim):
    return lax.broadcasted_iota(jnp.int32, shape, dim)


def split3(v):
    hi = v.astype(BF16)
    rest = v - hi.astype(F32)
    mid = rest.astype(BF16)
    lo = (rest - mid.astype(F32)).astype(BF16)
    return hi, mid, lo


def pack_kernel(ids_ref, x_ref, send_ref, rank_ref):
    ids = ids_ref[...]
    same = iota((CHIPS, ROWS), 0) == ids
    onehot = same.astype(F32).astype(BF16)
    before = (iota((ROWS, ROWS), 0) < iota((ROWS, ROWS), 1)).astype(F32).astype(BF16)
    earlier = jnp.dot(onehot, before, preferred_element_type=F32)
    rank = jnp.sum(jnp.where(same, earlier, 0.0), axis=0, keepdims=True).astype(jnp.int32)
    rank_ref[...] = rank
    position = ids * CAP + rank
    step = 256

    def block(b, _):
        start = pl.multiple_of(b * step, step)
        pick = (iota((step, ROWS), 0) + start == position).astype(F32)
        live = jnp.sum(pick, axis=1, keepdims=True)
        rows = jnp.dot(pick.astype(BF16), x_ref[...], preferred_element_type=F32)
        mark = jnp.where(iota((step, 128), 1) == 0, (1.0 - live) * MARK, 0.0)
        send_ref[pl.ds(start, step), 0:128] = (rows[:, 0:128] + mark).astype(BF16)
        send_ref[pl.ds(start, step), 128:] = rows[:, 128:].astype(BF16)
        return 0

    lax.fori_loop(0, SLOTS // step, block, 0)


def stats(x_ref, inv_ref, bias_ref):
    def block(b, carry):
        total, count = carry
        start = pl.multiple_of(b * 128, 128)
        x = x_ref[pl.ds(start, 128), :].astype(F32)
        live = x[:, 0:1] < MARK / 2
        x = jnp.where(live, x, 0.0)
        inv_ref[pl.ds(start, 128), :] = lax.rsqrt(
            jnp.sum(x * x, axis=1, keepdims=True) / WIDTH + EPS
        )
        bias_ref[pl.ds(start, 128), :] = jnp.where(live, 0.0, LOW)
        total = total + jnp.sum(x.reshape(16, 8, WIDTH), axis=0)
        count = count + jnp.sum(live.astype(F32).reshape(16, 8, 1), axis=0)
        return total, count

    zero = (jnp.zeros((8, WIDTH), F32), jnp.zeros((8, 1), F32))
    total, count = lax.fori_loop(0, SLOTS // 128, block, zero)
    return jnp.sum(total, axis=0, keepdims=True), jnp.sum(count, axis=0, keepdims=True)


def tile_best(other_ref, inv_ref, bias_ref, j, mine, diagonal=False):
    start = pl.multiple_of(j * TILE, TILE)
    dots = lax.dot_general(other_ref[pl.ds(start, TILE), :], mine, NT, preferred_element_type=F32)
    value = dots * inv_ref[pl.ds(start, TILE), :] + bias_ref[pl.ds(start, TILE), :]
    square = None
    if diagonal:
        eye = iota((TILE, TILE), 0) == iota((TILE, TILE), 1)
        square = jnp.sum(jnp.where(eye, dots, 0.0), axis=0, keepdims=True)
        value = jnp.where(eye, LOW, value)
    return jnp.max(value.reshape(TILE // 8, 8, TILE), axis=0), square


def own_kernel(x_ref, best_ref, inv_row_ref, total_ref, inv_ref, bias_ref):
    total, count = stats(x_ref, inv_ref, bias_ref)
    total_ref[:, :WIDTH] = total
    total_ref[:, WIDTH:] = jnp.broadcast_to(count, (1, 128))
    tiles = SLOTS // TILE
    for i in range(tiles):
        mine = x_ref[i * TILE : (i + 1) * TILE, :]
        best, square = tile_best(x_ref, inv_ref, bias_ref, i, mine, True)

        def other(k, best):
            j = lax.rem(i + 1 + k, tiles)
            return jnp.maximum(best, tile_best(x_ref, inv_ref, bias_ref, j, mine)[0])

        best = lax.fori_loop(0, tiles - 1, other, best)
        best_ref[:, i * TILE : (i + 1) * TILE] = jnp.max(best, axis=0, keepdims=True)
        inv_row_ref[:, i * TILE : (i + 1) * TILE] = lax.rsqrt(square / WIDTH + EPS)


def rest_kernel(x_ref, sib_ref, best_ref, inv_row_ref, total_ref, out_ref, inv_ref, bias_ref, near_ref):
    sib_total, _ = stats(sib_ref, inv_ref, bias_ref)
    total = total_ref[:, :WIDTH] + sib_total
    tiles = SLOTS // TILE

    def row(i, _):
        start = pl.multiple_of(i * TILE, TILE)
        mine = x_ref[pl.ds(start, TILE), :]

        def other(j, best):
            return jnp.maximum(best, tile_best(sib_ref, inv_ref, bias_ref, j, mine)[0])

        best = lax.fori_loop(0, tiles, other, jnp.full((8, TILE), LOW, F32))
        best = jnp.max(best, axis=0, keepdims=True)
        best = jnp.maximum(best, best_ref[:, pl.ds(start, TILE)])
        inv = inv_row_ref[:, pl.ds(start, TILE)]
        near_ref[:, pl.ds(start, TILE)] = jnp.maximum(-1.0, best * inv / WIDTH)
        return 0

    lax.fori_loop(0, tiles, row, 0)
    scale = lax.rsqrt(jnp.sum(total * total, axis=1, keepdims=True) / WIDTH + EPS)
    parts = jnp.concatenate(split3(total) + (jnp.zeros((13, WIDTH), BF16),), axis=0)
    toward = lax.dot_general(parts, x_ref[...], NT, preferred_element_type=F32)
    toward = toward[0:1] + toward[1:2] + toward[2:3]
    centre = toward * inv_row_ref[...] * scale / WIDTH
    lane = iota((CAP, SLOTS), 1)
    slot = lax.rem(lane, CAP) == iota((CAP, SLOTS), 0)
    near = jnp.where(slot, near_ref[...], 0.0)
    centre = jnp.where(slot, centre, 0.0)
    parts = jnp.concatenate(split3(jnp.concatenate([near, centre], axis=0)), axis=0)
    source = (iota((CHIPS, SLOTS), 1) // CAP == iota((CHIPS, SLOTS), 0)).astype(F32).astype(BF16)
    spread = lax.dot_general(source, parts, NT, preferred_element_type=F32)
    out_ref[...] = (
        spread[:, 0 : 2 * CAP] + spread[:, 2 * CAP : 4 * CAP] + spread[:, 4 * CAP : 6 * CAP]
    )


def unpack_kernel(ids_ref, rank_ref, back_ref, near_ref, centre_ref):
    same = iota((CHIPS, ROWS), 0) == ids_ref[...]
    onehot = same.astype(F32).astype(BF16)
    parts = jnp.concatenate(split3(back_ref[...]), axis=1)
    picked = lax.dot_general(parts, onehot, TN, preferred_element_type=F32)
    picked = picked[0 : 2 * CAP] + picked[2 * CAP : 4 * CAP] + picked[4 * CAP : 6 * CAP]
    slot = iota((CAP, ROWS), 0) == rank_ref[...]
    near_ref[...] = jnp.sum(jnp.where(slot, picked[0:CAP], 0.0), axis=0, keepdims=True)
    centre_ref[...] = jnp.sum(jnp.where(slot, picked[CAP:], 0.0), axis=0, keepdims=True)


def struct(shape, dtype):
    return jax.ShapeDtypeStruct(shape, dtype)


def call(kernel, outs, flops, scratch=()):
    return pl.pallas_call(
        kernel,
        out_shape=outs,
        scratch_shapes=list(scratch),
        compiler_params=pltpu.CompilerParams(vmem_limit_bytes=40 * 1024 * 1024),
        cost_estimate=pl.CostEstimate(
            flops=int(flops), bytes_accessed=6_000_000, transcendentals=0
        ),
    )


def shards(embeddings, cluster_ids):
    ids = cluster_ids.reshape(1, ROWS)
    send, rank = call(
        pack_kernel,
        (struct((SLOTS, WIDTH), BF16), struct((1, ROWS), jnp.int32)),
        2 * SLOTS * ROWS * WIDTH,
    )(ids, embeddings)
    chips = ("y", "z", "x")
    mine = lax.all_to_all(send.reshape(CHIPS, CAP, WIDTH), chips, 0, 0, tiled=True)
    mine = mine.reshape(SLOTS, WIDTH)
    swap = [(0, 1), (1, 0)]
    sib = lax.ppermute(mine, "core", swap)
    column = pltpu.VMEM((SLOTS, 1), F32)
    lanes = struct((1, SLOTS), F32)
    best, inv_row, part = call(
        own_kernel,
        (lanes, lanes, struct((1, WIDTH + 128), F32)),
        2 * SLOTS * SLOTS * WIDTH,
        (column, column),
    )(mine)
    total = part + lax.ppermute(part, "core", swap)
    mean = total[:, :WIDTH] / total[:, WIDTH : WIDTH + 1]
    x = lax.axis_index("x")
    core = lax.axis_index("core")
    means = jnp.zeros((2, WIDTH), F32)
    for k in range(4):
        came = mean if k == 0 else lax.ppermute(mean, "x", [(i, (i + k) % 4) for i in range(4)])
        place = lax.rem(x - k + 4, 4) - 2 * core
        means = jnp.where(jnp.arange(2)[:, None] == place, came, means)
    out = call(
        rest_kernel,
        struct((CHIPS, 2 * CAP), F32),
        2 * SLOTS * SLOTS * WIDTH,
        (column, column, pltpu.VMEM((1, SLOTS), F32)),
    )(mine, sib, best, inv_row, part)
    back = lax.all_to_all(out, chips, 0, 0, tiled=True)
    near, centre = call(
        unpack_kernel, (struct((1, ROWS), F32), struct((1, ROWS), F32)), 1e8
    )(ids, rank, back)
    return near.reshape(ROWS), centre.reshape(ROWS), means


def solution(mesh):
    fine = Mesh(mesh.devices.reshape(4, 8, 2, 4), ("y", "z", "core", "x"))
    owner = ("y", "z", "core")
    every = owner + ("x",)
    return jax.shard_map(
        shards,
        mesh=fine,
        in_specs=(P(every, None), P(every, None)),
        out_specs=(P(every), P(every), P(owner, None)),
        check_vma=False,
    )
```

time: 294 us -> 159 us (0.54)
  waiting for transfers between devices: 65.6 us -> 14.1 us
  local copies, waits for them, and re-layouts: 44.3 us -> 2.61 us
  Pallas kernels: 0 us -> 37.3 us
  matrix products: 22.6 us -> 0 us
  blocking collectives: 106 us -> 89.4 us
  other arithmetic: 16.3 us -> 1.39 us
  between operations: 14.2 us -> 0.71 us
  starting transfers between devices: 23.7 us -> 13.2 us
    all_gather x1 -> x0, waiting for transfers between devices: 61.5 us -> none  [shards(): other = lax.all_gather(block, 'help', axis=1, tiled=True)]
    pallas_call x0 -> x4, Pallas kernels: none -> 37.3 us  [the longest x1 17.6 us: shards(): call(rest_kernel, struct((CHIPS, 2 * CAP), F32), 2 * SLOTS * SLOTS * WIDT...]
    dot_general x3 -> x0, matrix products: 22.6 us -> none  [the longest x1 19.5 us: cosines(): jnp.einsum('ksd,kpd->ksp', mine, other, preferred_element_type=jnp.float32)]
    gather x2 -> x0, local copies, waits for them, and re-layouts: 21.1 us -> none  [the longest x1 10.5 us: shards(): centre_cosine = back_centre.reshape(-1)[position]]
    scatter x2 -> x0, local copies, waits for them, and re-layouts: 15.5 us -> none  [the longest x1 7.9 us: shards(): jnp.zeros((CL_OWN * owners * cap, width), jnp.bfloat16).at[position]]
    all_to_all x3 -> x1, starting transfers between devices: 23.6 us -> 8.31 us  [shards(): back = lax.all_to_all(out, chips, 0, 0, tiled=True)]
    all_gather x1 -> x0, blocking collectives: 12 us -> none  [shards(): other_live = lax.all_gather(alive, 'help', axis=1, tiled=True)]
    psum x1 -> x0, blocking collectives: 8.93 us -> none  [shards(): totals, counts = lax.psum((partial_totals, partial_counts), 'help')]
  transfers between devices with their start and end apart: 4 -> 6, of which waited for: 2 -> 4; matrix products, arithmetic and copies ran while one was open for 20% -> 1% of each run, Pallas kernels for 0% -> 8%
where the time goes in v1:
time: 159 us
  blocking collectives  89.4 us (56%)
  Pallas kernels  37.3 us (23%)
  waiting for transfers between devices  14.1 us (9%)
  starting transfers between devices  13.2 us (8%)
  local copies, waits for them, and re-layouts  2.61 us (2%)
    all_to_all x1, blocking collectives, shards(): lax.all_to_all(send.reshape(CHIPS, CAP, WIDTH), chips, 0, 0, tiled=True)  89.4 us
    pallas_call x1, Pallas kernels, shards(): call(rest_kernel, struct((CHIPS, 2 * CAP), F32), 2 * SLOTS * SLOTS * WIDT...  17.6 us
    pallas_call x1, Pallas kernels, shards(): call(own_kernel, (lanes, lanes, struct((1, WIDTH + 128), F32)), 2 * SLOTS...  13.2 us
    all_to_all x1, waiting for transfers between devices, shards(): back = lax.all_to_all(out, chips, 0, 0, tiled=True)  10.5 us
    all_to_all x1, starting transfers between devices, shards(): back = lax.all_to_all(out, chips, 0, 0, tiled=True)  8.31 us
    pallas_call x1, Pallas kernels, shards(): call(pack_kernel, (struct((SLOTS, WIDTH), BF16), struct((1, ROWS), jnp.in...  5.52 us
    ppermute x3, starting transfers between devices, shards(): lax.ppermute(mean, 'x', [(i, (i + k) % 4) for i in range(4)])  4.32 us
  transfers between devices with their start and end apart: 6, of which 4 were waited for; matrix products, arithmetic and copies ran while one was open for 1% of the time, Pallas kernels for 8%

profile of v1, /device:TPU:2, one launch (start us, length us, event | category | flops | bytes accessed | tf_op | source)
XLA Modules:
  0.0 158.6 jit_solution(668325315118239563)
XLA Ops:
  0.6 0.0 copy-start
  0.6 1.4 copy-done
  2.0 0.0 copy-start.1
  2.0 0.7 copy-done.1
  2.7 5.5 %shard_map.49 = (bf16[2048,768]{1,0:T(8,128)(2,1)S(1)}, s32[1,1024]{1,0:T(1,128)S(1)}) custom-call(s32[1,1024]{1,0:T(1,128)S(1)} %bitcast.15, bf16[1024,768]{1,0:T(8,128)(2,1)S(1)} %copy-done), custom_call_target="tpu_custom_call" | custom-call | flops 3221225472 | bytes 6000000 | tf_op jit(solution)/shard_map/pallas_call | solution.py:175
  8.2 89.4 %all_to_all.16 = bf16[128,16,768]{2,1,0:T(8,128)(2,1)S(1)} all-to-all(bf16[128,16,768]{2,1,0:T(8,128)(2,1)S(1)} %bitcast.13), channel_id=1, replica_groups=mesh['y'=4,'z'=8,'core'=2,'x'=4] {'y','z','x'}, dimensions={0} | all-to-all | bytes 6291456 | tf_op jit(solution)/shard_map/all_to_all | solution.py:181
  97.6 0.0 collective-permute-start
  97.6 13.2 %shard_map.50 = (f32[1,2048]{1,0:T(1,128)S(1)}, f32[1,2048]{1,0:T(1,128)S(1)}, f32[1,896]{1,0:T(1,128)S(1)}) custom-call(bf16[2048,768]{1,0:T(8,128)(2,1)S(1)} %bitcast.11), custom_call_target="tpu_custom_call" | custom-call | flops 6442450944 | bytes 6000000 | tf_op jit(solution)/shard_map/pallas_call | solution.py:187
  110.9 0.6 collective-permute-start.1
  111.5 0.8 collective-permute-done.1
  112.3 0.5 slice.9
  112.8 0.7 fusion
  113.5 0.1 collective-permute-start.4
  113.6 3.4 %collective-permute-start.3 = (f32[1,768]{1,0:T(1,128)S(1)}, f32[1,768]{1,0:T(1,128)S(1)}, u32[]{:S(2)}, u32[]{:S(2)}) collective-permute-start(f32[1,768]{1,0:T(1,128)S(1)} %get-tuple-element.18), channel_id=1, source_target_pairs={{0,2},{1,3},{2,0},{3,1},{4,6},{5,7},{6,4},{7,5},{8,10},{9,11},{10,... | collective-permute-start | bytes 9224 | tf_op jit(solution)/shard_map/ppermute | solution.py:199
  117.0 0.8 collective-permute-start.2
  117.8 0.0 collective-permute-done.4
  117.9 0.9 collective-permute-done.3
  118.8 1.8 %collective-permute-done.2 = f32[1,768]{1,0:T(1,128)S(1)} collective-permute-done((f32[1,768]{1,0:T(1,128)S(1)}, f32[1,768]{1,0:T(1,128)S(1)}, u32[]{:S(2)}, u32[]{:S(2)}) %collective-permute-start.2) | collective-permute-done | bytes 3104 | tf_op jit(solution)/shard_map/ppermute | solution.py:199
  120.6 0.0 collective-permute-done.sib_ref
  120.7 0.0 copy-start.2
  120.7 17.6 %shard_map.51 = f32[128,32]{1,0:T(8,128)} custom-call(bf16[2048,768]{1,0:T(8,128)(2,1)S(1)} %bitcast.12, bf16[2048,768]{1,0:T(8,128)(2,1)} %collective-permute-done.sib_ref, f32[1,2048]{1,0:T(1,128)S(1)} %get-tuple-element.12.best_ref, f32[1,2048]{1,0:T(1,128)S(1)} %get-tuple-element.13.inv_row_ref, f32[1,896]{1,0:T(1,128)S(1)} %get-tuple-element.14.total_ref), custom_call_target="tpu_custom_call" | custom-call | flops 6442450944 | bytes 6000000 | tf_op jit(solution)/shard_map/pallas_call | solution.py:202
  138.2 8.3 %all-to-all-start.1 = ((f32[128,1,32]{2,1,0:T(1,128)}), f32[128,1,32]{2,1,0:T(1,128)S(1)}, u32[]{:S(2)}, u32[]{:S(2)}) async-start(f32[128,1,32]{2,1,0:T(1,128)} %bitcast.4), calls=%async_computation.1 | async-start | bytes 131072 | tf_op jit(solution)/shard_map/all_to_all | solution.py:208
  146.6 0.7 select_select_fusion
  147.2 10.5 %all-to-all-done.1 = f32[128,1,32]{2,1,0:T(1,128)S(1)} async-done(((f32[128,1,32]{2,1,0:T(1,128)}), f32[128,1,32]{2,1,0:T(1,128)S(1)}, u32[]{:S(2)}, u32[]{:S(2)}) %all-to-all-start.1) | async-done | bytes 16416 | tf_op jit(solution)/shard_map/all_to_all | solution.py:208
  157.7 0.0 copy-done.2
  157.7 0.9 shard_map.52
  (6 shorter events, 0.1 us)
Async XLA Ops:
  0.6 1.4 copy-start
  2.0 0.7 copy-start.1
  97.6 23.0 %collective-permute-start = (bf16[2048,768]{1,0:T(8,128)(2,1)S(1)}, bf16[2048,768]{1,0:T(8,128)(2,1)}, u32[]{:S(2)}, u32[]{:S(2)}) collective-permute-start(bf16[2048,768]{1,0:T(8,128)(2,1)S(1)} %bitcast.10), channel_id=1, source_target_pairs={{0,4},{4,0},{1,5},{5,1},{2,6},{6,2},{3,7},{7,3},{8,12},{12,8},{9,1... | collective-permute-start | bytes 9437192 | tf_op jit(solution)/shard_map/ppermute | solution.py:184
  110.9 1.4 collective-permute-start.1
  113.5 4.3 %collective-permute-start.4 = (f32[1,768]{1,0:T(1,128)S(1)}, f32[1,768]{1,0:T(1,128)S(1)}, u32[]{:S(2)}, u32[]{:S(2)}) collective-permute-start(f32[1,768]{1,0:T(1,128)S(1)} %get-tuple-element.18), channel_id=1, source_target_pairs={{0,1},{1,2},{2,3},{3,0},{4,5},{5,6},{6,7},{7,4},{8,9},{9,10},{10,1... | collective-permute-start | bytes 9224 | tf_op jit(solution)/shard_map/ppermute | solution.py:199
  113.6 5.2 %collective-permute-start.3 = (f32[1,768]{1,0:T(1,128)S(1)}, f32[1,768]{1,0:T(1,128)S(1)}, u32[]{:S(2)}, u32[]{:S(2)}) collective-permute-start(f32[1,768]{1,0:T(1,128)S(1)} %get-tuple-element.18), channel_id=1, source_target_pairs={{0,2},{1,3},{2,0},{3,1},{4,6},{5,7},{6,4},{7,5},{8,10},{9,11},{10,... | collective-permute-start | bytes 9224 | tf_op jit(solution)/shard_map/ppermute | solution.py:199
  117.0 3.6 %collective-permute-start.2 = (f32[1,768]{1,0:T(1,128)S(1)}, f32[1,768]{1,0:T(1,128)S(1)}, u32[]{:S(2)}, u32[]{:S(2)}) collective-permute-start(f32[1,768]{1,0:T(1,128)S(1)} %get-tuple-element.18), channel_id=1, source_target_pairs={{0,3},{1,0},{2,1},{3,2},{4,7},{5,4},{6,5},{7,6},{8,11},{9,8},{10,9... | collective-permute-start | bytes 9224 | tf_op jit(solution)/shard_map/ppermute | solution.py:199
  120.7 37.1 %copy-start.2 = (s32[1024,1]{0,1:T(1,128)S(1)}, s32[1024,1]{0,1:T(1,128)}, u32[]{:S(2)}) copy-start(s32[1024,1]{0,1:T(1,128)} %param.3) | copy-start | bytes 12292
  138.2 19.5 %all-to-all-start.1 = ((f32[128,1,32]{2,1,0:T(1,128)}), f32[128,1,32]{2,1,0:T(1,128)S(1)}, u32[]{:S(2)}, u32[]{:S(2)}) async-start(f32[128,1,32]{2,1,0:T(1,128)} %bitcast.4), calls=%async_computation.1 | async-start | bytes 131072 | tf_op jit(solution)/shard_map/all_to_all | solution.py:208

commit v2 on v1

v2 whole, which is shorter than its diff:
```python
import jax
import jax.numpy as jnp
from jax import lax
from jax.experimental import pallas as pl
from jax.experimental.pallas import tpu as pltpu
from jax.sharding import Mesh, PartitionSpec as P

EPS = 1e-06
ROWS = 1024
WIDTH = 768
CAP = 16
CHIPS = 128
SLOTS = CHIPS * CAP
MARK = 64.0
LOW = -1e30
TILE = 512
TILES = SLOTS // TILE
NT = (((1,), (1,)), ((), ()))
TN = (((0,), (0,)), ((), ()))
F32 = jnp.float32
BF16 = jnp.bfloat16


def iota(shape, dim):
    return lax.broadcasted_iota(jnp.int32, shape, dim)


def split3(v):
    hi = v.astype(BF16)
    rest = v - hi.astype(F32)
    mid = rest.astype(BF16)
    lo = (rest - mid.astype(F32)).astype(BF16)
    return hi, mid, lo


def chip_of(ids):
    return ((ids >> 2) & 7) * 16 + (ids & 3) * 4 + (ids >> 5)


def eye(n):
    return iota((n, n), 0) == iota((n, n), 1)


def to_row(column):
    blocks = [
        jnp.sum(jnp.where(eye(128), column[k : k + 128], 0.0), axis=0, keepdims=True)
        for k in range(0, column.shape[0], 128)
    ]
    return jnp.concatenate(blocks, axis=1)


def to_column(row):
    blocks = [
        jnp.sum(jnp.where(eye(128), row[:, k : k + 128], 0.0), axis=1, keepdims=True)
        for k in range(0, row.shape[1], 128)
    ]
    return jnp.concatenate(blocks, axis=0)


def fold_lanes(value):
    best = value[:, 0:128]
    for k in range(128, value.shape[1], 128):
        best = jnp.maximum(best, value[:, k : k + 128])
    return best


def part(ref, i):
    return ref[i * TILE : (i + 1) * TILE, :]


def lanes(ref, row, i):
    return ref[row : row + 1, i * TILE : (i + 1) * TILE]


def pack_kernel(ids_ref, x_hbm, send_ref, rank_ref, x_ref, sem):
    copy = pltpu.make_async_copy(x_hbm, x_ref, sem)
    copy.start()
    chip = chip_of(ids_ref[...])
    same = iota((CHIPS, ROWS), 0) == chip
    onehot = same.astype(F32).astype(BF16)
    before = (iota((ROWS, ROWS), 0) < iota((ROWS, ROWS), 1)).astype(F32).astype(BF16)
    earlier = jnp.dot(onehot, before, preferred_element_type=F32)
    rank = jnp.sum(jnp.where(same, earlier, 0.0), axis=0, keepdims=True).astype(jnp.int32)
    rank_ref[...] = rank
    position = chip * CAP + rank
    step = 256
    copy.wait()
    for start in range(0, SLOTS, step):
        pick = (iota((step, ROWS), 0) + start == position).astype(F32)
        live = jnp.sum(pick, axis=1, keepdims=True)
        rows = jnp.dot(pick.astype(BF16), x_ref[...], preferred_element_type=F32)
        mark = jnp.where(iota((step, 128), 1) == 0, (1.0 - live) * MARK, 0.0)
        send_ref[start : start + step, 0:128] = (rows[:, 0:128] + mark).astype(BF16)
        send_ref[start : start + step, 128:] = rows[:, 128:].astype(BF16)


def diagonal_kernel(x_ref, info_ref, best_ref):
    first = (iota((8, WIDTH), 1) == 0).astype(F32).astype(BF16)
    marks = lax.dot_general(first, x_ref[...], NT, preferred_element_type=F32)
    live = (marks < MARK / 2).astype(F32)
    totals = jnp.dot(live.astype(BF16), x_ref[...], preferred_element_type=F32)
    info_ref[1:2, :] = jnp.where(live[0:1] > 0, 0.0, LOW)
    info_ref[2:3, 0:WIDTH] = totals[0:1]
    count = jnp.sum(live[0:1], axis=1, keepdims=True)
    info_ref[2:3, WIDTH:] = jnp.broadcast_to(count, (1, SLOTS - WIDTH))
    for i in range(TILES):
        dots = lax.dot_general(part(x_ref, i), part(x_ref, i), NT, preferred_element_type=F32)
        square = jnp.sum(jnp.where(eye(TILE), dots, 0.0), axis=0, keepdims=True)
        inv = lax.rsqrt(square / WIDTH + EPS)
        info_ref[0:1, i * TILE : (i + 1) * TILE] = inv
        value = jnp.where(eye(TILE), LOW, dots * inv + lanes(info_ref, 1, i))
        best = jnp.max(fold_lanes(value), axis=1, keepdims=True)
        best_ref[:, i * TILE : (i + 1) * TILE] = to_row(best)


def own_kernel(x_ref, info_ref, before_ref, best_ref, fold_ref):
    best_ref[...] = before_ref[...]
    for i in range(TILES - 1):
        inv = to_column(lanes(info_ref, 0, i))
        bias = to_column(lanes(info_ref, 1, i))
        for j in range(i + 1, TILES):
            dots = lax.dot_general(part(x_ref, i), part(x_ref, j), NT, preferred_element_type=F32)
            fold = fold_lanes(dots * lanes(info_ref, 0, j) + lanes(info_ref, 1, j))
            fold_ref[...] = fold if j == i + 1 else jnp.maximum(fold_ref[...], fold)
            down = jnp.max(dots * inv + bias, axis=0, keepdims=True)
            best_ref[:, j * TILE : (j + 1) * TILE] = jnp.maximum(lanes(best_ref, 0, j), down)
        best = to_row(jnp.max(fold_ref[...], axis=1, keepdims=True))
        best_ref[:, i * TILE : (i + 1) * TILE] = jnp.maximum(lanes(best_ref, 0, i), best)


def rest_kernel(x_ref, sib_ref, info_ref, sib_info_ref, best_ref, out_ref, mean_ref, near_ref, fold_ref):
    for i in range(TILES):
        for j in range(TILES):
            dots = lax.dot_general(part(x_ref, i), part(sib_ref, j), NT, preferred_element_type=F32)
            fold = fold_lanes(dots * lanes(sib_info_ref, 0, j) + lanes(sib_info_ref, 1, j))
            fold_ref[...] = fold if j == 0 else jnp.maximum(fold_ref[...], fold)
        best = to_row(jnp.max(fold_ref[...], axis=1, keepdims=True))
        best = jnp.maximum(best, lanes(best_ref, 0, i))
        near_ref[:, i * TILE : (i + 1) * TILE] = jnp.maximum(
            -1.0, best * lanes(info_ref, 0, i) / WIDTH
        )
    total = info_ref[2:3, 0:WIDTH] + sib_info_ref[2:3, 0:WIDTH]
    count = info_ref[2:3, WIDTH : WIDTH + 1] + sib_info_ref[2:3, WIDTH : WIDTH + 1]
    mean_ref[...] = total / count
    scale = lax.rsqrt(jnp.sum(total * total, axis=1, keepdims=True) / WIDTH + EPS)
    parts = jnp.concatenate(split3(total) + (jnp.zeros((13, WIDTH), BF16),), axis=0)
    toward = lax.dot_general(parts, x_ref[...], NT, preferred_element_type=F32)
    toward = toward[0:1] + toward[1:2] + toward[2:3]
    centre = toward * info_ref[0:1, :] * scale / WIDTH
    slot = lax.rem(iota((CAP, SLOTS), 1), CAP) == iota((CAP, SLOTS), 0)
    near = jnp.where(slot, near_ref[...], 0.0)
    centre = jnp.where(slot, centre, 0.0)
    parts = jnp.concatenate(split3(jnp.concatenate([near, centre], axis=0)), axis=0)
    source = (iota((CHIPS, SLOTS), 1) // CAP == iota((CHIPS, SLOTS), 0)).astype(F32).astype(BF16)
    spread = lax.dot_general(source, parts, NT, preferred_element_type=F32)
    out_ref[...] = (
        spread[:, 0 : 2 * CAP] + spread[:, 2 * CAP : 4 * CAP] + spread[:, 4 * CAP : 6 * CAP]
    )


def unpack_kernel(ids_ref, rank_ref, back_ref, near_ref, centre_ref):
    same = iota((CHIPS, ROWS), 0) == chip_of(ids_ref[...])
    onehot = same.astype(F32).astype(BF16)
    parts = jnp.concatenate(split3(back_ref[...]), axis=1)
    picked = lax.dot_general(parts, onehot, TN, preferred_element_type=F32)
    picked = picked[0 : 2 * CAP] + picked[2 * CAP : 4 * CAP] + picked[4 * CAP : 6 * CAP]
    slot = iota((CAP, ROWS), 0) == rank_ref[...]
    near_ref[...] = jnp.sum(jnp.where(slot, picked[0:CAP], 0.0), axis=0, keepdims=True)
    centre_ref[...] = jnp.sum(jnp.where(slot, picked[CAP:], 0.0), axis=0, keepdims=True)


def struct(shape, dtype):
    return jax.ShapeDtypeStruct(shape, dtype)


def call(kernel, outs, flops, scratch=(), **specs):
    return pl.pallas_call(
        kernel,
        out_shape=outs,
        scratch_shapes=list(scratch),
        compiler_params=pltpu.CompilerParams(vmem_limit_bytes=40 * 1024 * 1024),
        cost_estimate=pl.CostEstimate(
            flops=int(flops), bytes_accessed=6_000_000, transcendentals=0
        ),
        **specs,
    )


def shards(embeddings, cluster_ids):
    ids = cluster_ids.reshape(1, ROWS)
    block = 2 * SLOTS * SLOTS * WIDTH
    send, rank = call(
        pack_kernel,
        (struct((SLOTS, WIDTH), BF16), struct((1, ROWS), jnp.int32)),
        2 * SLOTS * ROWS * WIDTH,
        (pltpu.VMEM((ROWS, WIDTH), BF16), pltpu.SemaphoreType.DMA),
        in_specs=[pl.BlockSpec(memory_space=pltpu.VMEM), pl.BlockSpec(memory_space=pltpu.HBM)],
    )(ids, embeddings)
    chips = ("z", "x", "y")
    mine = lax.all_to_all(send.reshape(CHIPS, CAP, WIDTH), chips, 0, 0, tiled=True)
    mine = mine.reshape(SLOTS, WIDTH)
    swap = [(0, 1), (1, 0)]
    sib = lax.ppermute(mine, "core", swap)
    row = struct((1, SLOTS), F32)
    info, best = call(diagonal_kernel, (struct((3, SLOTS), F32), row), block / 4)(mine)
    sib_info = lax.ppermute(info, "core", swap)
    fold = pltpu.VMEM((TILE, 128), F32)
    best = call(own_kernel, row, block * 3 / 8, (fold,))(mine, info, best)
    out, mean = call(
        rest_kernel,
        (struct((CHIPS, 2 * CAP), F32), struct((1, WIDTH), F32)),
        block,
        (pltpu.VMEM((1, SLOTS), F32), fold),
    )(mine, sib, info, sib_info, best)
    back = lax.all_to_all(out, chips, 0, 0, tiled=True)
    x = lax.axis_index("x")
    core = lax.axis_index("core")
    means = jnp.zeros((2, WIDTH), F32)
    for k in range(4):
        came = mean if k == 0 else lax.ppermute(mean, "x", [(i, (i + k) % 4) for i in range(4)])
        place = lax.rem(x - k + 4, 4) - 2 * core
        means = jnp.where(jnp.arange(2)[:, None] == place, came, means)
    near, centre = call(
        unpack_kernel, (struct((1, ROWS), F32), struct((1, ROWS), F32)), 1e8
    )(ids, rank, back)
    return near.reshape(ROWS), centre.reshape(ROWS), means


def solution(mesh):
    fine = Mesh(mesh.devices.reshape(4, 8, 2, 4), ("y", "z", "core", "x"))
    owner = ("y", "z", "core")
    every = owner + ("x",)
    return jax.shard_map(
        shards,
        mesh=fine,
        in_specs=(P(every, None), P(every, None)),
        out_specs=(P(every), P(every), P(owner, None)),
        check_vma=False,
    )
```

time: 159 us -> 140 us (0.88)
  Pallas kernels: 37.3 us -> 21.9 us
  waiting for transfers between devices: 14.1 us -> 10.6 us
    pallas_call x2 -> x3, Pallas kernels: 30.8 us -> 16.9 us  [the longest x1 10.4 us: shards(): call(rest_kernel, (struct((CHIPS, 2 * CAP), F32), struct((1, WIDTH), F32)...]
    ppermute x3, waiting for transfers between devices: 2.76 us -> 0.01 us  [shards(): lax.ppermute(mean, 'x', [(i, (i + k) % 4) for i in range(4)])]
  transfers between devices with their start and end apart: 6 -> 6, of which waited for: 4 -> 1; matrix products, arithmetic and copies ran while one was open for 1% -> 1% of each run, Pallas kernels for 8% -> 5%
where the time goes in v2:
time: 140 us; the launch traced here: 139 us
  blocking collectives  89.4 us (64%)
  Pallas kernels  21.9 us (16%)
  starting transfers between devices  13.9 us (10%)
  waiting for transfers between devices  10.6 us (8%)
  local copies, waits for them, and re-layouts  2.09 us (1%)
    all_to_all x1, blocking collectives, shards(): lax.all_to_all(send.reshape(CHIPS, CAP, WIDTH), chips, 0, 0, tiled=True)  89.4 us
    all_to_all x1, waiting for transfers between devices, shards(): back = lax.all_to_all(out, chips, 0, 0, tiled=True)  10.6 us
    pallas_call x1, Pallas kernels, shards(): call(rest_kernel, (struct((CHIPS, 2 * CAP), F32), struct((1, WIDTH), F32)...  10.4 us
    all_to_all x1, starting transfers between devices, shards(): back = lax.all_to_all(out, chips, 0, 0, tiled=True)  9.65 us
    pallas_call x1, Pallas kernels, shards(): call(pack_kernel, (struct((SLOTS, WIDTH), BF16), struct((1, ROWS), jnp.in...  4.1 us
    ppermute x3, starting transfers between devices, shards(): lax.ppermute(mean, 'x', [(i, (i + k) % 4) for i in range(4)])  3.44 us
    pallas_call x1, Pallas kernels, shards(): call(diagonal_kernel, (struct((3, SLOTS), F32), row), block / 4)(mine)  3.4 us
    pallas_call x1, Pallas kernels, shards(): best = call(own_kernel, row, block * 3 / 8, (fold,))(mine, info, best)  3.1 us
  transfers between devices with their start and end apart: 6, of which 1 were waited for; matrix products, arithmetic and copies ran while one was open for 1% of the time, Pallas kernels for 5%

profile of v2, /device:TPU:2, one launch (start us, length us, event | category | flops | bytes accessed | tf_op | source)
XLA Modules:
  0.0 139.4 jit_solution(8913578881213467119)
XLA Ops:
  0.6 0.0 copy-start
  0.6 1.4 %copy-done = bf16[1024,768]{1,0:T(8,128)(2,1)S(1)} copy-done((bf16[1024,768]{1,0:T(8,128)(2,1)S(1)}, bf16[1024,768]{1,0:T(8,128)(2,1)}, u32[]{:S(2)}) %copy-start) | copy-done | bytes 1572888
  2.0 0.0 copy-start.1
  2.0 0.7 copy-done.1
  2.7 4.1 %shard_map.49 = (bf16[2048,768]{1,0:T(8,128)(2,1)S(1)}, s32[1,1024]{1,0:T(1,128)S(1)}) custom-call(s32[1,1024]{1,0:T(1,128)S(1)} %bitcast.15, bf16[1024,768]{1,0:T(8,128)(2,1)S(1)} %copy-done), custom_call_target="tpu_custom_call" | custom-call | flops 3221225472 | bytes 6000000 | tf_op jit(solution)/shard_map/pallas_call | solution.py:192
  6.8 89.4 %all_to_all.16 = bf16[128,16,768]{2,1,0:T(8,128)(2,1)S(1)} all-to-all(bf16[128,16,768]{2,1,0:T(8,128)(2,1)S(1)} %bitcast.13), channel_id=1, replica_groups=mesh['y'=4,'z'=8,'core'=2,'x'=4] {'z','x','y'}, dimensions={0} | all-to-all | bytes 6291456 | tf_op jit(solution)/shard_map/all_to_all | solution.py:200
  96.2 0.0 collective-permute-start
  96.3 3.4 %shard_map.50 = (f32[3,2048]{1,0:T(4,128)S(1)}, f32[1,2048]{1,0:T(1,128)S(1)}) custom-call(bf16[2048,768]{1,0:T(8,128)(2,1)S(1)} %bitcast.10), custom_call_target="tpu_custom_call" | custom-call | flops 1610612736 | bytes 6000000 | tf_op jit(solution)/shard_map/pallas_call | solution.py:205
  99.7 0.8 collective-permute-start.1
  100.4 3.1 %shard_map.51.best_ref = f32[1,2048]{1,0:T(1,128)S(1)} custom-call(bf16[2048,768]{1,0:T(8,128)(2,1)S(1)} %bitcast.11, f32[3,2048]{1,0:T(4,128)S(1)} %get-tuple-element.13.info_ref, f32[1,2048]{1,0:T(1,128)S(1)} %get-tuple-element.14.before_ref), custom_call_target="tpu_custom_call" | custom-call | flops 2415919104 | bytes 6000000 | tf_op jit(solution)/shard_map/pallas_call | solution.py:208
  103.5 0.0 copy-start.2
  103.6 0.0 collective-permute-done.1.sib_info_ref
  103.6 0.0 collective-permute-done.sib_ref
  103.6 10.4 %shard_map.52 = (f32[128,32]{1,0:T(8,128)}, f32[1,768]{1,0:T(1,128)S(1)}) custom-call(bf16[2048,768]{1,0:T(8,128)(2,1)S(1)} %bitcast.12, bf16[2048,768]{1,0:T(8,128)(2,1)} %collective-permute-done.sib_ref, f32[3,2048]{1,0:T(4,128)S(1)} %get-tuple-element.13.info_ref, f32[3,2048]{1,0:T(4,128)S(1)} %collective-permute-done.1.sib_info_ref, ...), custom_call_target="tpu_custom_call" | custom-call | flops 6442450944 | bytes 6000000 | tf_op jit(solution)/shard_map/pallas_call | solution.py:209
  114.0 1.1 collective-permute-start.4
  115.1 2.3 %collective-permute-start.3 = (f32[1,768]{1,0:T(1,128)S(1)}, f32[1,768]{1,0:T(1,128)S(1)}, u32[]{:S(2)}, u32[]{:S(2)}) collective-permute-start(f32[1,768]{1,0:T(1,128)S(1)} %get-tuple-element.18), channel_id=1, source_target_pairs={{0,2},{1,3},{2,0},{3,1},{4,6},{5,7},{6,4},{7,5},{8,10},{9,11},{10,... | collective-permute-start | bytes 9224 | tf_op jit(solution)/shard_map/ppermute | solution.py:220
  117.4 0.0 collective-permute-start.2
  117.4 9.6 %all-to-all-start.1 = ((f32[128,1,32]{2,1,0:T(1,128)}), f32[128,1,32]{2,1,0:T(1,128)S(1)}, u32[]{:S(2)}, u32[]{:S(2)}) async-start(f32[128,1,32]{2,1,0:T(1,128)} %bitcast.4), calls=%async_computation.1 | async-start | bytes 131072 | tf_op jit(solution)/shard_map/all_to_all | solution.py:215
  127.1 0.0 collective-permute-done.4
  127.1 0.0 collective-permute-done.3
  127.2 0.0 collective-permute-done.2
  127.2 0.7 select_select_fusion
  127.9 10.6 %all-to-all-done.1 = f32[128,1,32]{2,1,0:T(1,128)S(1)} async-done(((f32[128,1,32]{2,1,0:T(1,128)}), f32[128,1,32]{2,1,0:T(1,128)S(1)}, u32[]{:S(2)}, u32[]{:S(2)}) %all-to-all-start.1) | async-done | bytes 16416 | tf_op jit(solution)/shard_map/all_to_all | solution.py:215
  138.4 0.0 copy-done.2
  138.4 0.9 shard_map.53
  (6 shorter events, 0.1 us)
Async XLA Ops:
  0.6 1.4 %copy-start = (bf16[1024,768]{1,0:T(8,128)(2,1)S(1)}, bf16[1024,768]{1,0:T(8,128)(2,1)}, u32[]{:S(2)}) copy-start(bf16[1024,768]{1,0:T(8,128)(2,1)} %x_hbm.1) | copy-start | bytes 4718596
  2.0 0.7 copy-start.1
  96.2 7.3 %collective-permute-start = (bf16[2048,768]{1,0:T(8,128)(2,1)S(1)}, bf16[2048,768]{1,0:T(8,128)(2,1)}, u32[]{:S(2)}, u32[]{:S(2)}) collective-permute-start(bf16[2048,768]{1,0:T(8,128)(2,1)S(1)} %bitcast.9), channel_id=1, source_target_pairs={{0,4},{4,0},{1,5},{5,1},{2,6},{6,2},{3,7},{7,3},{8,12},{12,8},{9,1... | collective-permute-start | bytes 9437192 | tf_op jit(solution)/shard_map/ppermute | solution.py:203
  99.7 3.9 %collective-permute-start.1 = (f32[3,2048]{1,0:T(4,128)S(1)}, f32[3,2048]{1,0:T(4,128)S(1)}, u32[]{:S(2)}, u32[]{:S(2)}) collective-permute-start(f32[3,2048]{1,0:T(4,128)S(1)} %get-tuple-element.13.info_ref), channel_id=1, source_target_pairs={{0,4},{4,0},{1,5},{5,1},{2,6},{6,2},{3,7},{7,3},{8,12},{12,8},{9,1... | collective-permute-start | bytes 73736 | tf_op jit(solution)/shard_map/ppermute | solution.py:206
  103.5 34.9 %copy-start.2 = (s32[1024,1]{0,1:T(1,128)S(1)}, s32[1024,1]{0,1:T(1,128)}, u32[]{:S(2)}) copy-start(s32[1024,1]{0,1:T(1,128)} %param.3) | copy-start | bytes 12292
  114.0 13.1 %collective-permute-start.4 = (f32[1,768]{1,0:T(1,128)S(1)}, f32[1,768]{1,0:T(1,128)S(1)}, u32[]{:S(2)}, u32[]{:S(2)}) collective-permute-start(f32[1,768]{1,0:T(1,128)S(1)} %get-tuple-element.18), channel_id=1, source_target_pairs={{0,1},{1,2},{2,3},{3,0},{4,5},{5,6},{6,7},{7,4},{8,9},{9,10},{10,1... | collective-permute-start | bytes 9224 | tf_op jit(solution)/shard_map/ppermute | solution.py:220
  115.1 12.1 %collective-permute-start.3 = (f32[1,768]{1,0:T(1,128)S(1)}, f32[1,768]{1,0:T(1,128)S(1)}, u32[]{:S(2)}, u32[]{:S(2)}) collective-permute-start(f32[1,768]{1,0:T(1,128)S(1)} %get-tuple-element.18), channel_id=1, source_target_pairs={{0,2},{1,3},{2,0},{3,1},{4,6},{5,7},{6,4},{7,5},{8,10},{9,11},{10,... | collective-permute-start | bytes 9224 | tf_op jit(solution)/shard_map/ppermute | solution.py:220
  117.4 9.8 %collective-permute-start.2 = (f32[1,768]{1,0:T(1,128)S(1)}, f32[1,768]{1,0:T(1,128)S(1)}, u32[]{:S(2)}, u32[]{:S(2)}) collective-permute-start(f32[1,768]{1,0:T(1,128)S(1)} %get-tuple-element.18), channel_id=1, source_target_pairs={{0,3},{1,0},{2,1},{3,2},{4,7},{5,4},{6,5},{7,6},{8,11},{9,8},{10,9... | collective-permute-start | bytes 9224 | tf_op jit(solution)/shard_map/ppermute | solution.py:220
  117.4 21.0 %all-to-all-start.1 = ((f32[128,1,32]{2,1,0:T(1,128)}), f32[128,1,32]{2,1,0:T(1,128)S(1)}, u32[]{:S(2)}, u32[]{:S(2)}) async-start(f32[128,1,32]{2,1,0:T(1,128)} %bitcast.4), calls=%async_computation.1 | async-start | bytes 131072 | tf_op jit(solution)/shard_map/all_to_all | solution.py:215

commit v3 on v2

--- a/solution.py
+++ b/solution.py
@@ -72,7 +72,7 @@
     return ref[row : row + 1, i * TILE : (i + 1) * TILE]
 
 
-def pack_kernel(ids_ref, x_hbm, send_ref, rank_ref, x_ref, sem):
+def pack_kernel(ids_ref, x_hbm, send_hbm, rank_ref, x_ref, sem, send_ref, sems):
     copy = pltpu.make_async_copy(x_hbm, x_ref, sem)
     copy.start()
     chip = chip_of(ids_ref[...])
@@ -85,6 +85,7 @@
     position = chip * CAP + rank
     step = 256
     copy.wait()
+    copies = []
     for start in range(0, SLOTS, step):
         pick = (iota((step, ROWS), 0) + start == position).astype(F32)
         live = jnp.sum(pick, axis=1, keepdims=True)
@@ -92,16 +93,25 @@
         mark = jnp.where(iota((step, 128), 1) == 0, (1.0 - live) * MARK, 0.0)
         send_ref[start : start + step, 0:128] = (rows[:, 0:128] + mark).astype(BF16)
         send_ref[start : start + step, 128:] = rows[:, 128:].astype(BF16)
+        copies.append(
+            pltpu.make_async_copy(
+                send_ref.at[start : start + step, :],
+                send_hbm.at[start : start + step, :],
+                sems.at[start // step],
+            )
+        )
+        copies[-1].start()
+    for copy in copies:
+        copy.wait()
 
 
 def diagonal_kernel(x_ref, info_ref, best_ref):
-    first = (iota((8, WIDTH), 1) == 0).astype(F32).astype(BF16)
-    marks = lax.dot_general(first, x_ref[...], NT, preferred_element_type=F32)
-    live = (marks < MARK / 2).astype(F32)
-    totals = jnp.dot(live.astype(BF16), x_ref[...], preferred_element_type=F32)
-    info_ref[1:2, :] = jnp.where(live[0:1] > 0, 0.0, LOW)
+    live = to_row((x_ref[:, 0:1].astype(F32) < MARK / 2).astype(F32))
+    weights = jnp.broadcast_to(live, (8, SLOTS)).astype(BF16)
+    totals = jnp.dot(weights, x_ref[...], preferred_element_type=F32)
+    info_ref[1:2, :] = jnp.where(live > 0, 0.0, LOW)
     info_ref[2:3, 0:WIDTH] = totals[0:1]
-    count = jnp.sum(live[0:1], axis=1, keepdims=True)
+    count = jnp.sum(live, axis=1, keepdims=True)
     info_ref[2:3, WIDTH:] = jnp.broadcast_to(count, (1, SLOTS - WIDTH))
     for i in range(TILES):
         dots = lax.dot_general(part(x_ref, i), part(x_ref, i), NT, preferred_element_type=F32)
@@ -128,9 +138,19 @@
         best_ref[:, i * TILE : (i + 1) * TILE] = jnp.maximum(lanes(best_ref, 0, i), best)
 
 
-def rest_kernel(x_ref, sib_ref, info_ref, sib_info_ref, best_ref, out_ref, mean_ref, near_ref, fold_ref):
+def rest_kernel(
+    x_ref, sib_hbm, info_ref, sib_info_ref, best_ref, out_ref, mean_ref, near_ref, fold_ref, sib_ref, sems
+):
+    copies = [
+        pltpu.make_async_copy(part(sib_hbm.at, j), part(sib_ref.at, j), sems.at[j])
+        for j in range(TILES)
+    ]
+    for copy in copies:
+        copy.start()
     for i in range(TILES):
         for j in range(TILES):
+            if i == 0:
+                copies[j].wait()
             dots = lax.dot_general(part(x_ref, i), part(sib_ref, j), NT, preferred_element_type=F32)
             fold = fold_lanes(dots * lanes(sib_info_ref, 0, j) + lanes(sib_info_ref, 1, j))
             fold_ref[...] = fold if j == 0 else jnp.maximum(fold_ref[...], fold)
@@ -173,12 +193,12 @@
     return jax.ShapeDtypeStruct(shape, dtype)
 
 
-def call(kernel, outs, flops, scratch=(), **specs):
+def call(kernel, outs, flops, scratch=(), grant=20, **specs):
     return pl.pallas_call(
         kernel,
         out_shape=outs,
         scratch_shapes=list(scratch),
-        compiler_params=pltpu.CompilerParams(vmem_limit_bytes=40 * 1024 * 1024),
+        compiler_params=pltpu.CompilerParams(vmem_limit_bytes=grant * 1024 * 1024),
         cost_estimate=pl.CostEstimate(
             flops=int(flops), bytes_accessed=6_000_000, transcendentals=0
         ),
@@ -189,12 +209,20 @@
 def shards(embeddings, cluster_ids):
     ids = cluster_ids.reshape(1, ROWS)
     block = 2 * SLOTS * SLOTS * WIDTH
+    here = pl.BlockSpec(memory_space=pltpu.VMEM)
     send, rank = call(
         pack_kernel,
         (struct((SLOTS, WIDTH), BF16), struct((1, ROWS), jnp.int32)),
         2 * SLOTS * ROWS * WIDTH,
-        (pltpu.VMEM((ROWS, WIDTH), BF16), pltpu.SemaphoreType.DMA),
-        in_specs=[pl.BlockSpec(memory_space=pltpu.VMEM), pl.BlockSpec(memory_space=pltpu.HBM)],
+        (
+            pltpu.VMEM((ROWS, WIDTH), BF16),
+            pltpu.SemaphoreType.DMA,
+            pltpu.VMEM((SLOTS, WIDTH), BF16),
+            pltpu.SemaphoreType.DMA((8,)),
+        ),
+        grant=60,
+        in_specs=[here, pl.BlockSpec(memory_space=pltpu.HBM)],
+        out_specs=(pl.BlockSpec(memory_space=pltpu.HBM), here),
     )(ids, embeddings)
     chips = ("z", "x", "y")
     mine = lax.all_to_all(send.reshape(CHIPS, CAP, WIDTH), chips, 0, 0, tiled=True)
@@ -210,7 +238,13 @@
         rest_kernel,
         (struct((CHIPS, 2 * CAP), F32), struct((1, WIDTH), F32)),
         block,
-        (pltpu.VMEM((1, SLOTS), F32), fold),
+        (
+            pltpu.VMEM((1, SLOTS), F32),
+            fold,
+            pltpu.VMEM((SLOTS, WIDTH), BF16),
+            pltpu.SemaphoreType.DMA((TILES,)),
+        ),
+        in_specs=[here, pl.BlockSpec(memory_space=pltpu.HBM), here, here, here],
     )(mine, sib, info, sib_info, best)
     back = lax.all_to_all(out, chips, 0, 0, tiled=True)
     x = lax.axis_index("x")

time: 140 us -> 140 us (level)
  Pallas kernels: 21.9 us -> 24.2 us
  local copies, waits for them, and re-layouts: 2.09 us -> 0.01 us
    pallas_call x1, Pallas kernels: 4.1 us -> 7.07 us  [shards(): call(pack_kernel, (struct((SLOTS, WIDTH), BF16), struct((1, ROWS), jnp.in...]
    unnamed x6 -> x4, local copies, waits for them, and re-layouts: 2.09 us -> 0.01 us
  transfers between devices with their start and end apart: 6 -> 6, of which waited for: 1 -> 1; matrix products, arithmetic and copies ran while one was open for 1% -> 1% of each run, Pallas kernels for 5% -> 4%
where the time goes in v3:
time: 140 us
  blocking collectives  89.6 us (64%)
  Pallas kernels  24.2 us (17%)
  starting transfers between devices  13.9 us (10%)
  waiting for transfers between devices  10.6 us (8%)
    all_to_all x1, blocking collectives, shards(): lax.all_to_all(send.reshape(CHIPS, CAP, WIDTH), chips, 0, 0, tiled=True)  89.6 us
    all_to_all x1, waiting for transfers between devices, shards(): back = lax.all_to_all(out, chips, 0, 0, tiled=True)  10.5 us
    pallas_call x1, Pallas kernels, shards(): call(rest_kernel, (struct((CHIPS, 2 * CAP), F32), struct((1, WIDTH), F32)...  10.4 us
    all_to_all x1, starting transfers between devices, shards(): back = lax.all_to_all(out, chips, 0, 0, tiled=True)  9.64 us
    pallas_call x1, Pallas kernels, shards(): call(pack_kernel, (struct((SLOTS, WIDTH), BF16), struct((1, ROWS), jnp.in...  7.07 us
    ppermute x3, starting transfers between devices, shards(): lax.ppermute(mean, 'x', [(i, (i + k) % 4) for i in range(4)])  3.51 us
    pallas_call x1, Pallas kernels, shards(): best = call(own_kernel, row, block * 3 / 8, (fold,))(mine, info, best)  3.1 us
  transfers between devices with their start and end apart: 6, of which 1 were waited for; matrix products, arithmetic and copies ran while one was open for 1% of the time, Pallas kernels for 4%

profile of v3, /device:TPU:2, one launch (start us, length us, event | category | flops | bytes accessed | tf_op | source)
XLA Modules:
  0.0 139.8 jit_solution(13280118705320572589)
XLA Ops:
  0.6 7.1 %shard_map.49 = (bf16[2048,768]{1,0:T(8,128)(2,1)}, s32[1,1024]{1,0:T(1,128)}) custom-call(s32[1,1024]{1,0:T(1,128)} %bitcast.14, bf16[1024,768]{1,0:T(8,128)(2,1)} %x_hbm.1), custom_call_target="tpu_custom_call" | custom-call | flops 3221225472 | bytes 6000000 | tf_op jit(solution)/shard_map/pallas_call | solution.py:213
  7.7 89.6 %all_to_all.16 = bf16[128,16,768]{2,1,0:T(8,128)(2,1)S(1)} all-to-all(bf16[128,16,768]{2,1,0:T(8,128)(2,1)} %bitcast.16), channel_id=1, replica_groups=mesh['y'=4,'z'=8,'core'=2,'x'=4] {'z','x','y'}, dimensions={0} | all-to-all | bytes 6291456 | tf_op jit(solution)/shard_map/all_to_all | solution.py:228
  97.3 0.0 collective-permute-start
  97.3 2.7 %shard_map.50 = (f32[3,2048]{1,0:T(4,128)S(1)}, f32[1,2048]{1,0:T(1,128)S(1)}) custom-call(bf16[2048,768]{1,0:T(8,128)(2,1)S(1)} %bitcast.10), custom_call_target="tpu_custom_call" | custom-call | flops 1610612736 | bytes 6000000 | tf_op jit(solution)/shard_map/pallas_call | solution.py:233
  100.0 0.8 collective-permute-start.1
  100.8 3.1 %shard_map.51.best_ref = f32[1,2048]{1,0:T(1,128)S(1)} custom-call(bf16[2048,768]{1,0:T(8,128)(2,1)S(1)} %bitcast.11, f32[3,2048]{1,0:T(4,128)S(1)} %get-tuple-element.13.info_ref, f32[1,2048]{1,0:T(1,128)S(1)} %get-tuple-element.14.before_ref), custom_call_target="tpu_custom_call" | custom-call | flops 2415919104 | bytes 6000000 | tf_op jit(solution)/shard_map/pallas_call | solution.py:236
  103.9 0.0 copy-start
  103.9 0.0 copy-start.1
  104.0 0.0 collective-permute-done.1.sib_info_ref
  104.0 0.0 collective-permute-done.sib_hbm
  104.0 10.4 %shard_map.52 = (f32[128,32]{1,0:T(8,128)}, f32[1,768]{1,0:T(1,128)S(1)}) custom-call(bf16[2048,768]{1,0:T(8,128)(2,1)S(1)} %bitcast.12, bf16[2048,768]{1,0:T(8,128)(2,1)} %collective-permute-done.sib_hbm, f32[3,2048]{1,0:T(4,128)S(1)} %get-tuple-element.13.info_ref, f32[3,2048]{1,0:T(4,128)S(1)} %collective-permute-done.1.sib_info_ref, ...), custom_call_target="tpu_custom_call" | custom-call | flops 6442450944 | bytes 6000000 | tf_op jit(solution)/shard_map/pallas_call | solution.py:237
  114.4 1.2 collective-permute-start.4
  115.5 2.3 %collective-permute-start.3 = (f32[1,768]{1,0:T(1,128)S(1)}, f32[1,768]{1,0:T(1,128)S(1)}, u32[]{:S(2)}, u32[]{:S(2)}) collective-permute-start(f32[1,768]{1,0:T(1,128)S(1)} %get-tuple-element.18), channel_id=1, source_target_pairs={{0,2},{1,3},{2,0},{3,1},{4,6},{5,7},{6,4},{7,5},{8,10},{9,11},{10,... | collective-permute-start | bytes 9224 | tf_op jit(solution)/shard_map/ppermute | solution.py:254
  117.8 0.0 collective-permute-start.2
  117.9 9.6 %all-to-all-start.1 = ((f32[128,1,32]{2,1,0:T(1,128)}), f32[128,1,32]{2,1,0:T(1,128)S(1)}, u32[]{:S(2)}, u32[]{:S(2)}) async-start(f32[128,1,32]{2,1,0:T(1,128)} %bitcast.4), calls=%async_computation.1 | async-start | bytes 131072 | tf_op jit(solution)/shard_map/all_to_all | solution.py:249
  127.5 0.0 collective-permute-done.4
  127.6 0.0 collective-permute-done.3
  127.6 0.0 collective-permute-done.2
  127.6 0.7 select_select_fusion
  128.3 10.5 %all-to-all-done.1 = f32[128,1,32]{2,1,0:T(1,128)S(1)} async-done(((f32[128,1,32]{2,1,0:T(1,128)}), f32[128,1,32]{2,1,0:T(1,128)S(1)}, u32[]{:S(2)}, u32[]{:S(2)}) %all-to-all-start.1) | async-done | bytes 16416 | tf_op jit(solution)/shard_map/all_to_all | solution.py:249
  138.9 0.0 copy-done
  138.9 0.0 copy-done.1
  138.9 0.9 shard_map.53
  (6 shorter events, 0.1 us)
Async XLA Ops:
  97.3 6.6 %collective-permute-start = (bf16[2048,768]{1,0:T(8,128)(2,1)S(1)}, bf16[2048,768]{1,0:T(8,128)(2,1)}, u32[]{:S(2)}, u32[]{:S(2)}) collective-permute-start(bf16[2048,768]{1,0:T(8,128)(2,1)S(1)} %bitcast.9), channel_id=1, source_target_pairs={{0,4},{4,0},{1,5},{5,1},{2,6},{6,2},{3,7},{7,3},{8,12},{12,8},{9,1... | collective-permute-start | bytes 9437192 | tf_op jit(solution)/shard_map/ppermute | solution.py:231
  100.0 3.9 %collective-permute-start.1 = (f32[3,2048]{1,0:T(4,128)S(1)}, f32[3,2048]{1,0:T(4,128)S(1)}, u32[]{:S(2)}, u32[]{:S(2)}) collective-permute-start(f32[3,2048]{1,0:T(4,128)S(1)} %get-tuple-element.13.info_ref), channel_id=1, source_target_pairs={{0,4},{4,0},{1,5},{5,1},{2,6},{6,2},{3,7},{7,3},{8,12},{12,8},{9,1... | collective-permute-start | bytes 73736 | tf_op jit(solution)/shard_map/ppermute | solution.py:234
  103.9 34.9 %copy-start = (s32[1024,1]{0,1:T(1,128)S(1)}, s32[1024,1]{0,1:T(1,128)}, u32[]{:S(2)}) copy-start(s32[1024,1]{0,1:T(1,128)} %param.3) | copy-start | bytes 12292
  103.9 34.9 %copy-start.1 = (s32[1,1024]{1,0:T(1,128)S(1)}, s32[1,1024]{1,0:T(1,128)}, u32[]{:S(2)}) copy-start(s32[1,1024]{1,0:T(1,128)} %get-tuple-element.11.rank_ref) | copy-start | bytes 12292
  114.4 13.2 %collective-permute-start.4 = (f32[1,768]{1,0:T(1,128)S(1)}, f32[1,768]{1,0:T(1,128)S(1)}, u32[]{:S(2)}, u32[]{:S(2)}) collective-permute-start(f32[1,768]{1,0:T(1,128)S(1)} %get-tuple-element.18), channel_id=1, source_target_pairs={{0,1},{1,2},{2,3},{3,0},{4,5},{5,6},{6,7},{7,4},{8,9},{9,10},{10,1... | collective-permute-start | bytes 9224 | tf_op jit(solution)/shard_map/ppermute | solution.py:254
  115.5 12.0 %collective-permute-start.3 = (f32[1,768]{1,0:T(1,128)S(1)}, f32[1,768]{1,0:T(1,128)S(1)}, u32[]{:S(2)}, u32[]{:S(2)}) collective-permute-start(f32[1,768]{1,0:T(1,128)S(1)} %get-tuple-element.18), channel_id=1, source_target_pairs={{0,2},{1,3},{2,0},{3,1},{4,6},{5,7},{6,4},{7,5},{8,10},{9,11},{10,... | collective-permute-start | bytes 9224 | tf_op jit(solution)/shard_map/ppermute | solution.py:254
  117.8 9.8 %collective-permute-start.2 = (f32[1,768]{1,0:T(1,128)S(1)}, f32[1,768]{1,0:T(1,128)S(1)}, u32[]{:S(2)}, u32[]{:S(2)}) collective-permute-start(f32[1,768]{1,0:T(1,128)S(1)} %get-tuple-element.18), channel_id=1, source_target_pairs={{0,3},{1,0},{2,1},{3,2},{4,7},{5,4},{6,5},{7,6},{8,11},{9,8},{10,9... | collective-permute-start | bytes 9224 | tf_op jit(solution)/shard_map/ppermute | solution.py:254
  117.9 21.0 %all-to-all-start.1 = ((f32[128,1,32]{2,1,0:T(1,128)}), f32[128,1,32]{2,1,0:T(1,128)S(1)}, u32[]{:S(2)}, u32[]{:S(2)}) async-start(f32[128,1,32]{2,1,0:T(1,128)} %bitcast.4), calls=%async_computation.1 | async-start | bytes 131072 | tf_op jit(solution)/shard_map/all_to_all | solution.py:249

commit v4 on v3

--- a/solution.py
+++ b/solution.py
@@ -72,9 +72,7 @@
     return ref[row : row + 1, i * TILE : (i + 1) * TILE]
 
 
-def pack_kernel(ids_ref, x_hbm, send_hbm, rank_ref, x_ref, sem, send_ref, sems):
-    copy = pltpu.make_async_copy(x_hbm, x_ref, sem)
-    copy.start()
+def pack_kernel(ids_ref, x_ref, send_ref, rank_ref):
     chip = chip_of(ids_ref[...])
     same = iota((CHIPS, ROWS), 0) == chip
     onehot = same.astype(F32).astype(BF16)
@@ -84,8 +82,6 @@
     rank_ref[...] = rank
     position = chip * CAP + rank
     step = 256
-    copy.wait()
-    copies = []
     for start in range(0, SLOTS, step):
         pick = (iota((step, ROWS), 0) + start == position).astype(F32)
         live = jnp.sum(pick, axis=1, keepdims=True)
@@ -93,16 +89,6 @@
         mark = jnp.where(iota((step, 128), 1) == 0, (1.0 - live) * MARK, 0.0)
         send_ref[start : start + step, 0:128] = (rows[:, 0:128] + mark).astype(BF16)
         send_ref[start : start + step, 128:] = rows[:, 128:].astype(BF16)
-        copies.append(
-            pltpu.make_async_copy(
-                send_ref.at[start : start + step, :],
-                send_hbm.at[start : start + step, :],
-                sems.at[start // step],
-            )
-        )
-        copies[-1].start()
-    for copy in copies:
-        copy.wait()
 
 
 def diagonal_kernel(x_ref, info_ref, best_ref):
@@ -147,18 +133,22 @@
     ]
     for copy in copies:
         copy.start()
-    for i in range(TILES):
+    for copy in copies:
+        copy.wait()
+
+    def row(i, _):
+        rows = pl.ds(pl.multiple_of(i * TILE, TILE), TILE)
+        fold = None
         for j in range(TILES):
-            if i == 0:
-                copies[j].wait()
-            dots = lax.dot_general(part(x_ref, i), part(sib_ref, j), NT, preferred_element_type=F32)
-            fold = fold_lanes(dots * lanes(sib_info_ref, 0, j) + lanes(sib_info_ref, 1, j))
-            fold_ref[...] = fold if j == 0 else jnp.maximum(fold_ref[...], fold)
-        best = to_row(jnp.max(fold_ref[...], axis=1, keepdims=True))
-        best = jnp.maximum(best, lanes(best_ref, 0, i))
-        near_ref[:, i * TILE : (i + 1) * TILE] = jnp.maximum(
-            -1.0, best * lanes(info_ref, 0, i) / WIDTH
-        )
+            dots = lax.dot_general(x_ref[rows, :], part(sib_ref, j), NT, preferred_element_type=F32)
+            value = fold_lanes(dots * lanes(sib_info_ref, 0, j) + lanes(sib_info_ref, 1, j))
+            fold = value if j == 0 else jnp.maximum(fold, value)
+        best = to_row(jnp.max(fold, axis=1, keepdims=True))
+        best = jnp.maximum(best, best_ref[:, rows])
+        near_ref[:, rows] = jnp.maximum(-1.0, best * info_ref[0:1, rows] / WIDTH)
+        return 0
+
+    lax.fori_loop(0, TILES, row, 0)
     total = info_ref[2:3, 0:WIDTH] + sib_info_ref[2:3, 0:WIDTH]
     count = info_ref[2:3, WIDTH : WIDTH + 1] + sib_info_ref[2:3, WIDTH : WIDTH + 1]
     mean_ref[...] = total / count
@@ -214,15 +204,6 @@
         pack_kernel,
         (struct((SLOTS, WIDTH), BF16), struct((1, ROWS), jnp.int32)),
         2 * SLOTS * ROWS * WIDTH,
-        (
-            pltpu.VMEM((ROWS, WIDTH), BF16),
-            pltpu.SemaphoreType.DMA,
-            pltpu.VMEM((SLOTS, WIDTH), BF16),
-            pltpu.SemaphoreType.DMA((8,)),
-        ),
-        grant=60,
-        in_specs=[here, pl.BlockSpec(memory_space=pltpu.HBM)],
-        out_specs=(pl.BlockSpec(memory_space=pltpu.HBM), here),
     )(ids, embeddings)
     chips = ("z", "x", "y")
     mine = lax.all_to_all(send.reshape(CHIPS, CAP, WIDTH), chips, 0, 0, tiled=True)

time: 140 us -> 141 us (level)
  local copies, waits for them, and re-layouts: 0.01 us -> 2.09 us
    pallas_call x1, Pallas kernels: 7.07 us -> 4.69 us  [shards(): call(pack_kernel, (struct((SLOTS, WIDTH), BF16), struct((1, ROWS), jnp.in...]
    unnamed x4 -> x6, local copies, waits for them, and re-layouts: 0.01 us -> 2.09 us
where the time goes in v4:
time: 141 us; the launch traced here: 140 us
  blocking collectives  89.4 us (63%)
  Pallas kernels  22.9 us (16%)
  starting transfers between devices  13.9 us (10%)
  waiting for transfers between devices  10.6 us (8%)
  local copies, waits for them, and re-layouts  2.09 us (1%)
    all_to_all x1, blocking collectives, shards(): lax.all_to_all(send.reshape(CHIPS, CAP, WIDTH), chips, 0, 0, tiled=True)  89.4 us
    pallas_call x1, Pallas kernels, shards(): call(rest_kernel, (struct((CHIPS, 2 * CAP), F32), struct((1, WIDTH), F32)...  11.5 us
    all_to_all x1, waiting for transfers between devices, shards(): back = lax.all_to_all(out, chips, 0, 0, tiled=True)  10.6 us
    all_to_all x1, starting transfers between devices, shards(): back = lax.all_to_all(out, chips, 0, 0, tiled=True)  9.64 us
    pallas_call x1, Pallas kernels, shards(): call(pack_kernel, (struct((SLOTS, WIDTH), BF16), struct((1, ROWS), jnp.in...  4.69 us
    ppermute x3, starting transfers between devices, shards(): lax.ppermute(mean, 'x', [(i, (i + k) % 4) for i in range(4)])  3.52 us
    pallas_call x1, Pallas kernels, shards(): best = call(own_kernel, row, block * 3 / 8, (fold,))(mine, info, best)  3.11 us
  transfers between devices with their start and end apart: 6, of which 1 were waited for; matrix products, arithmetic and copies ran while one was open for 1% of the time, Pallas kernels for 4%

profile of v4, /device:TPU:2, one launch (start us, length us, event | category | flops | bytes accessed | tf_op | source)
XLA Modules:
  0.0 140.4 jit_solution(8602297326593762635)
XLA Ops:
  0.6 0.0 copy-start
  0.6 1.4 copy-done
  2.0 0.0 copy-start.1
  2.0 0.7 copy-done.1
  2.7 4.7 %shard_map.49 = (bf16[2048,768]{1,0:T(8,128)(2,1)S(1)}, s32[1,1024]{1,0:T(1,128)S(1)}) custom-call(s32[1,1024]{1,0:T(1,128)S(1)} %bitcast.15, bf16[1024,768]{1,0:T(8,128)(2,1)S(1)} %copy-done), custom_call_target="tpu_custom_call" | custom-call | flops 3221225472 | bytes 6000000 | tf_op jit(solution)/shard_map/pallas_call | solution.py:203
  7.4 89.4 %all_to_all.16 = bf16[128,16,768]{2,1,0:T(8,128)(2,1)S(1)} all-to-all(bf16[128,16,768]{2,1,0:T(8,128)(2,1)S(1)} %bitcast.13), channel_id=1, replica_groups=mesh['y'=4,'z'=8,'core'=2,'x'=4] {'z','x','y'}, dimensions={0} | all-to-all | bytes 6291456 | tf_op jit(solution)/shard_map/all_to_all | solution.py:209
  96.8 0.0 collective-permute-start
  96.8 2.7 %shard_map.50 = (f32[3,2048]{1,0:T(4,128)S(1)}, f32[1,2048]{1,0:T(1,128)S(1)}) custom-call(bf16[2048,768]{1,0:T(8,128)(2,1)S(1)} %bitcast.10), custom_call_target="tpu_custom_call" | custom-call | flops 1610612736 | bytes 6000000 | tf_op jit(solution)/shard_map/pallas_call | solution.py:214
  99.6 0.8 collective-permute-start.1
  100.3 3.1 %shard_map.51.best_ref = f32[1,2048]{1,0:T(1,128)S(1)} custom-call(bf16[2048,768]{1,0:T(8,128)(2,1)S(1)} %bitcast.11, f32[3,2048]{1,0:T(4,128)S(1)} %get-tuple-element.13.info_ref, f32[1,2048]{1,0:T(1,128)S(1)} %get-tuple-element.14.before_ref), custom_call_target="tpu_custom_call" | custom-call | flops 2415919104 | bytes 6000000 | tf_op jit(solution)/shard_map/pallas_call | solution.py:217
  103.4 0.0 copy-start.2
  103.4 0.0 collective-permute-done.1.sib_info_ref
  103.5 0.0 collective-permute-done.sib_hbm
  103.5 11.5 %shard_map.52 = (f32[128,32]{1,0:T(8,128)}, f32[1,768]{1,0:T(1,128)S(1)}) custom-call(bf16[2048,768]{1,0:T(8,128)(2,1)S(1)} %bitcast.12, bf16[2048,768]{1,0:T(8,128)(2,1)} %collective-permute-done.sib_hbm, f32[3,2048]{1,0:T(4,128)S(1)} %get-tuple-element.13.info_ref, f32[3,2048]{1,0:T(4,128)S(1)} %collective-permute-done.1.sib_info_ref, ...), custom_call_target="tpu_custom_call" | custom-call | flops 6442450944 | bytes 6000000 | tf_op jit(solution)/shard_map/pallas_call | solution.py:218
  115.0 1.2 collective-permute-start.4
  116.2 2.3 %collective-permute-start.3 = (f32[1,768]{1,0:T(1,128)S(1)}, f32[1,768]{1,0:T(1,128)S(1)}, u32[]{:S(2)}, u32[]{:S(2)}) collective-permute-start(f32[1,768]{1,0:T(1,128)S(1)} %get-tuple-element.18), channel_id=1, source_target_pairs={{0,2},{1,3},{2,0},{3,1},{4,6},{5,7},{6,4},{7,5},{8,10},{9,11},{10,... | collective-permute-start | bytes 9224 | tf_op jit(solution)/shard_map/ppermute | solution.py:235
  118.5 0.0 collective-permute-start.2
  118.5 9.6 %all-to-all-start.1 = ((f32[128,1,32]{2,1,0:T(1,128)}), f32[128,1,32]{2,1,0:T(1,128)S(1)}, u32[]{:S(2)}, u32[]{:S(2)}) async-start(f32[128,1,32]{2,1,0:T(1,128)} %bitcast.4), calls=%async_computation.1 | async-start | bytes 131072 | tf_op jit(solution)/shard_map/all_to_all | solution.py:230
  128.2 0.0 collective-permute-done.4
  128.2 0.0 collective-permute-done.3
  128.2 0.0 collective-permute-done.2
  128.3 0.7 select_select_fusion
  129.0 10.6 %all-to-all-done.1 = f32[128,1,32]{2,1,0:T(1,128)S(1)} async-done(((f32[128,1,32]{2,1,0:T(1,128)}), f32[128,1,32]{2,1,0:T(1,128)S(1)}, u32[]{:S(2)}, u32[]{:S(2)}) %all-to-all-start.1) | async-done | bytes 16416 | tf_op jit(solution)/shard_map/all_to_all | solution.py:230
  139.5 0.0 copy-done.2
  139.5 0.9 shard_map.53
  (6 shorter events, 0.1 us)
Async XLA Ops:
  0.6 1.4 %copy-start = (bf16[1024,768]{1,0:T(8,128)(2,1)S(1)}, bf16[1024,768]{1,0:T(8,128)(2,1)}, u32[]{:S(2)}) copy-start(bf16[1024,768]{1,0:T(8,128)(2,1)} %x_ref.1) | copy-start | bytes 4718596
  2.0 0.7 copy-start.1
  96.8 6.6 %collective-permute-start = (bf16[2048,768]{1,0:T(8,128)(2,1)S(1)}, bf16[2048,768]{1,0:T(8,128)(2,1)}, u32[]{:S(2)}, u32[]{:S(2)}) collective-permute-start(bf16[2048,768]{1,0:T(8,128)(2,1)S(1)} %bitcast.9), channel_id=1, source_target_pairs={{0,4},{4,0},{1,5},{5,1},{2,6},{6,2},{3,7},{7,3},{8,12},{12,8},{9,1... | collective-permute-start | bytes 9437192 | tf_op jit(solution)/shard_map/ppermute | solution.py:212
  99.6 3.9 %collective-permute-start.1 = (f32[3,2048]{1,0:T(4,128)S(1)}, f32[3,2048]{1,0:T(4,128)S(1)}, u32[]{:S(2)}, u32[]{:S(2)}) collective-permute-start(f32[3,2048]{1,0:T(4,128)S(1)} %get-tuple-element.13.info_ref), channel_id=1, source_target_pairs={{0,4},{4,0},{1,5},{5,1},{2,6},{6,2},{3,7},{7,3},{8,12},{12,8},{9,1... | collective-permute-start | bytes 73736 | tf_op jit(solution)/shard_map/ppermute | solution.py:215
  103.4 36.1 %copy-start.2 = (s32[1024,1]{0,1:T(1,128)S(1)}, s32[1024,1]{0,1:T(1,128)}, u32[]{:S(2)}) copy-start(s32[1024,1]{0,1:T(1,128)} %param.3) | copy-start | bytes 12292
  115.0 13.2 %collective-permute-start.4 = (f32[1,768]{1,0:T(1,128)S(1)}, f32[1,768]{1,0:T(1,128)S(1)}, u32[]{:S(2)}, u32[]{:S(2)}) collective-permute-start(f32[1,768]{1,0:T(1,128)S(1)} %get-tuple-element.18), channel_id=1, source_target_pairs={{0,1},{1,2},{2,3},{3,0},{4,5},{5,6},{6,7},{7,4},{8,9},{9,10},{10,1... | collective-permute-start | bytes 9224 | tf_op jit(solution)/shard_map/ppermute | solution.py:235
  116.2 12.1 %collective-permute-start.3 = (f32[1,768]{1,0:T(1,128)S(1)}, f32[1,768]{1,0:T(1,128)S(1)}, u32[]{:S(2)}, u32[]{:S(2)}) collective-permute-start(f32[1,768]{1,0:T(1,128)S(1)} %get-tuple-element.18), channel_id=1, source_target_pairs={{0,2},{1,3},{2,0},{3,1},{4,6},{5,7},{6,4},{7,5},{8,10},{9,11},{10,... | collective-permute-start | bytes 9224 | tf_op jit(solution)/shard_map/ppermute | solution.py:235
  118.5 9.8 %collective-permute-start.2 = (f32[1,768]{1,0:T(1,128)S(1)}, f32[1,768]{1,0:T(1,128)S(1)}, u32[]{:S(2)}, u32[]{:S(2)}) collective-permute-start(f32[1,768]{1,0:T(1,128)S(1)} %get-tuple-element.18), channel_id=1, source_target_pairs={{0,3},{1,0},{2,1},{3,2},{4,7},{5,4},{6,5},{7,6},{8,11},{9,8},{10,9... | collective-permute-start | bytes 9224 | tf_op jit(solution)/shard_map/ppermute | solution.py:235
  118.5 21.0 %all-to-all-start.1 = ((f32[128,1,32]{2,1,0:T(1,128)}), f32[128,1,32]{2,1,0:T(1,128)S(1)}, u32[]{:S(2)}, u32[]{:S(2)}) async-start(f32[128,1,32]{2,1,0:T(1,128)} %bitcast.4), calls=%async_computation.1 | async-start | bytes 131072 | tf_op jit(solution)/shard_map/all_to_all | solution.py:230

commit v5 on v4

--- a/solution.py
+++ b/solution.py
@@ -72,7 +72,9 @@
     return ref[row : row + 1, i * TILE : (i + 1) * TILE]
 
 
-def pack_kernel(ids_ref, x_ref, send_ref, rank_ref):
+def pack_kernel(ids_ref, x_hbm, send_ref, rank_ref, x_ref, sem):
+    copy = pltpu.make_async_copy(x_hbm, x_ref, sem)
+    copy.start()
     chip = chip_of(ids_ref[...])
     same = iota((CHIPS, ROWS), 0) == chip
     onehot = same.astype(F32).astype(BF16)
@@ -82,6 +84,7 @@
     rank_ref[...] = rank
     position = chip * CAP + rank
     step = 256
+    copy.wait()
     for start in range(0, SLOTS, step):
         pick = (iota((step, ROWS), 0) + start == position).astype(F32)
         live = jnp.sum(pick, axis=1, keepdims=True)
@@ -127,28 +130,11 @@
 def rest_kernel(
     x_ref, sib_hbm, info_ref, sib_info_ref, best_ref, out_ref, mean_ref, near_ref, fold_ref, sib_ref, sems
 ):
-    copies = [
-        pltpu.make_async_copy(part(sib_hbm.at, j), part(sib_ref.at, j), sems.at[j])
-        for j in range(TILES)
-    ]
-    for copy in copies:
-        copy.start()
-    for copy in copies:
-        copy.wait()
-
-    def row(i, _):
-        rows = pl.ds(pl.multiple_of(i * TILE, TILE), TILE)
-        fold = None
-        for j in range(TILES):
-            dots = lax.dot_general(x_ref[rows, :], part(sib_ref, j), NT, preferred_element_type=F32)
-            value = fold_lanes(dots * lanes(sib_info_ref, 0, j) + lanes(sib_info_ref, 1, j))
-            fold = value if j == 0 else jnp.maximum(fold, value)
-        best = to_row(jnp.max(fold, axis=1, keepdims=True))
-        best = jnp.maximum(best, best_ref[:, rows])
-        near_ref[:, rows] = jnp.maximum(-1.0, best * info_ref[0:1, rows] / WIDTH)
-        return 0
-
-    lax.fori_loop(0, TILES, row, 0)
+    def copy(j):
+        rows = slice(j * TILE, (j + 1) * TILE)
+        return pltpu.make_async_copy(sib_hbm.at[rows, :], sib_ref.at[rows, :], sems.at[j])
+
+    copy(0).start()
     total = info_ref[2:3, 0:WIDTH] + sib_info_ref[2:3, 0:WIDTH]
     count = info_ref[2:3, WIDTH : WIDTH + 1] + sib_info_ref[2:3, WIDTH : WIDTH + 1]
     mean_ref[...] = total / count
@@ -157,6 +143,22 @@
     toward = lax.dot_general(parts, x_ref[...], NT, preferred_element_type=F32)
     toward = toward[0:1] + toward[1:2] + toward[2:3]
     centre = toward * info_ref[0:1, :] * scale / WIDTH
+    for j in range(TILES):
+        copy(j).wait()
+        if j + 1 < TILES:
+            copy(j + 1).start()
+        for i in range(TILES):
+            dots = lax.dot_general(part(x_ref, i), part(sib_ref, j), NT, preferred_element_type=F32)
+            fold = fold_lanes(dots * lanes(sib_info_ref, 0, j) + lanes(sib_info_ref, 1, j))
+            fold = fold if j == 0 else jnp.maximum(part(fold_ref, i), fold)
+            if j + 1 < TILES:
+                fold_ref[i * TILE : (i + 1) * TILE, :] = fold
+            else:
+                best = to_row(jnp.max(fold, axis=1, keepdims=True))
+                best = jnp.maximum(best, lanes(best_ref, 0, i))
+                near_ref[:, i * TILE : (i + 1) * TILE] = jnp.maximum(
+                    -1.0, best * lanes(info_ref, 0, i) / WIDTH
+                )
     slot = lax.rem(iota((CAP, SLOTS), 1), CAP) == iota((CAP, SLOTS), 0)
     near = jnp.where(slot, near_ref[...], 0.0)
     centre = jnp.where(slot, centre, 0.0)
@@ -183,7 +185,7 @@
     return jax.ShapeDtypeStruct(shape, dtype)
 
 
-def call(kernel, outs, flops, scratch=(), grant=20, **specs):
+def call(kernel, outs, flops, scratch=(), grant=40, **specs):
     return pl.pallas_call(
         kernel,
         out_shape=outs,
@@ -196,6 +198,19 @@
     )
 
 
+def share_means(mean):
+    x, core = lax.axis_index("x"), lax.axis_index("core")
+    first = [(0, 2), (4, 1), (1, 3), (5, 0), (6, 4), (2, 7), (7, 5), (3, 6)]
+    second = [(0, 3), (1, 2), (6, 5), (7, 4)]
+    one = lax.ppermute(mean, ("core", "x"), first)
+    two = lax.ppermute(mean, ("core", "x"), second)
+    near = x // 2 == core
+    other = jnp.where(near, mean, two)
+    low = lax.rem(x, 2) == 0
+    own_low = jnp.where(near, low, ~low)
+    return jnp.where(own_low == (jnp.arange(2)[:, None] == 0), other, one)
+
+
 def shards(embeddings, cluster_ids):
     ids = cluster_ids.reshape(1, ROWS)
     block = 2 * SLOTS * SLOTS * WIDTH
@@ -204,6 +219,8 @@
         pack_kernel,
         (struct((SLOTS, WIDTH), BF16), struct((1, ROWS), jnp.int32)),
         2 * SLOTS * ROWS * WIDTH,
+        (pltpu.VMEM((ROWS, WIDTH), BF16), pltpu.SemaphoreType.DMA),
+        in_specs=[here, pl.BlockSpec(memory_space=pltpu.HBM)],
     )(ids, embeddings)
     chips = ("z", "x", "y")
     mine = lax.all_to_all(send.reshape(CHIPS, CAP, WIDTH), chips, 0, 0, tiled=True)
@@ -221,20 +238,14 @@
         block,
         (
             pltpu.VMEM((1, SLOTS), F32),
-            fold,
+            pltpu.VMEM((SLOTS, 128), F32),
             pltpu.VMEM((SLOTS, WIDTH), BF16),
             pltpu.SemaphoreType.DMA((TILES,)),
         ),
         in_specs=[here, pl.BlockSpec(memory_space=pltpu.HBM), here, here, here],
     )(mine, sib, info, sib_info, best)
     back = lax.all_to_all(out, chips, 0, 0, tiled=True)
-    x = lax.axis_index("x")
-    core = lax.axis_index("core")
-    means = jnp.zeros((2, WIDTH), F32)
-    for k in range(4):
-        came = mean if k == 0 else lax.ppermute(mean, "x", [(i, (i + k) % 4) for i in range(4)])
-        place = lax.rem(x - k + 4, 4) - 2 * core
-        means = jnp.where(jnp.arange(2)[:, None] == place, came, means)
+    means = share_means(mean)
     near, centre = call(
         unpack_kernel, (struct((1, ROWS), F32), struct((1, ROWS), F32)), 1e8
     )(ids, rank, back)

time: 141 us -> 138 us (0.979)
  Pallas kernels: 22.9 us -> 20.7 us
    pallas_call x1, Pallas kernels: 11.5 us -> 9.88 us  [shards(): call(rest_kernel, (struct((CHIPS, 2 * CAP), F32), struct((1, WIDTH), F32)...]
    ppermute x3 -> x2, starting transfers between devices: 3.52 us -> 3.11 us  [the longest x1 3.01 us: share_means(): two = lax.ppermute(mean, ('core', 'x'), second)]
  transfers between devices with their start and end apart: 6 -> 5, of which waited for: 1 -> 1; matrix products, arithmetic and copies ran while one was open for 1% -> 1% of each run, Pallas kernels for 4% -> 4%
where the time goes in v5:
time: 138 us
  blocking collectives  89.4 us (65%)
  Pallas kernels  20.7 us (15%)
  starting transfers between devices  13.7 us (10%)
  waiting for transfers between devices  10.6 us (8%)
  local copies, waits for them, and re-layouts  2.09 us (2%)
    all_to_all x1, blocking collectives, shards(): lax.all_to_all(send.reshape(CHIPS, CAP, WIDTH), chips, 0, 0, tiled=True)  89.4 us
    all_to_all x1, waiting for transfers between devices, shards(): back = lax.all_to_all(out, chips, 0, 0, tiled=True)  10.6 us
    pallas_call x1, Pallas kernels, shards(): call(rest_kernel, (struct((CHIPS, 2 * CAP), F32), struct((1, WIDTH), F32)...  9.88 us
    all_to_all x1, starting transfers between devices, shards(): back = lax.all_to_all(out, chips, 0, 0, tiled=True)  9.84 us
    pallas_call x1, Pallas kernels, shards(): call(pack_kernel, (struct((SLOTS, WIDTH), BF16), struct((1, ROWS), jnp.in...  4.1 us
    pallas_call x1, Pallas kernels, shards(): best = call(own_kernel, row, block * 3 / 8, (fold,))(mine, info, best)  3.11 us
    ppermute x1, starting transfers between devices, share_means(): two = lax.ppermute(mean, ('core', 'x'), second)  3.01 us
  transfers between devices with their start and end apart: 5, of which 1 were waited for; matrix products, arithmetic and copies ran while one was open for 1% of the time, Pallas kernels for 4%

profile of v5, /device:TPU:2, one launch (start us, length us, event | category | flops | bytes accessed | tf_op | source)
XLA Modules:
  0.0 138.0 jit_solution(2957078529862610331)
XLA Ops:
  0.6 0.0 copy-start
  0.6 1.4 %copy-done = bf16[1024,768]{1,0:T(8,128)(2,1)S(1)} copy-done((bf16[1024,768]{1,0:T(8,128)(2,1)S(1)}, bf16[1024,768]{1,0:T(8,128)(2,1)}, u32[]{:S(2)}) %copy-start) | copy-done | bytes 1572888
  2.0 0.0 copy-start.1
  2.0 0.7 copy-done.1
  2.7 4.1 %shard_map.49 = (bf16[2048,768]{1,0:T(8,128)(2,1)S(1)}, s32[1,1024]{1,0:T(1,128)S(1)}) custom-call(s32[1,1024]{1,0:T(1,128)S(1)} %bitcast.15, bf16[1024,768]{1,0:T(8,128)(2,1)S(1)} %copy-done), custom_call_target="tpu_custom_call" | custom-call | flops 3221225472 | bytes 6000000 | tf_op jit(solution)/shard_map/pallas_call | solution.py:218
  6.8 89.4 %all_to_all.16 = bf16[128,16,768]{2,1,0:T(8,128)(2,1)S(1)} all-to-all(bf16[128,16,768]{2,1,0:T(8,128)(2,1)S(1)} %bitcast.13), channel_id=1, replica_groups=mesh['y'=4,'z'=8,'core'=2,'x'=4] {'z','x','y'}, dimensions={0} | all-to-all | bytes 6291456 | tf_op jit(solution)/shard_map/all_to_all | solution.py:226
  96.2 0.0 collective-permute-start
  96.2 2.7 %shard_map.50 = (f32[3,2048]{1,0:T(4,128)S(1)}, f32[1,2048]{1,0:T(1,128)S(1)}) custom-call(bf16[2048,768]{1,0:T(8,128)(2,1)S(1)} %bitcast.10), custom_call_target="tpu_custom_call" | custom-call | flops 1610612736 | bytes 6000000 | tf_op jit(solution)/shard_map/pallas_call | solution.py:231
  98.9 0.8 collective-permute-start.1
  99.7 3.1 %shard_map.51.best_ref = f32[1,2048]{1,0:T(1,128)S(1)} custom-call(bf16[2048,768]{1,0:T(8,128)(2,1)S(1)} %bitcast.11, f32[3,2048]{1,0:T(4,128)S(1)} %get-tuple-element.13.info_ref, f32[1,2048]{1,0:T(1,128)S(1)} %get-tuple-element.14.before_ref), custom_call_target="tpu_custom_call" | custom-call | flops 2415919104 | bytes 6000000 | tf_op jit(solution)/shard_map/pallas_call | solution.py:234
  102.8 0.0 copy-start.2
  102.8 0.0 collective-permute-done.1.sib_info_ref
  102.9 0.0 collective-permute-done.sib_hbm
  102.9 9.9 %shard_map.52 = (f32[128,32]{1,0:T(8,128)}, f32[1,768]{1,0:T(1,128)S(1)}) custom-call(bf16[2048,768]{1,0:T(8,128)(2,1)S(1)} %bitcast.12, bf16[2048,768]{1,0:T(8,128)(2,1)} %collective-permute-done.sib_hbm, f32[3,2048]{1,0:T(4,128)S(1)} %get-tuple-element.13.info_ref, f32[3,2048]{1,0:T(4,128)S(1)} %collective-permute-done.1.sib_info_ref, ...), custom_call_target="tpu_custom_call" | custom-call | flops 6442450944 | bytes 6000000 | tf_op jit(solution)/shard_map/pallas_call | solution.py:235
  112.8 3.0 %collective-permute-start.2 = (f32[1,768]{1,0:T(1,128)S(1)}, f32[1,768]{1,0:T(1,128)S(1)}, u32[]{:S(2)}, u32[]{:S(2)}) collective-permute-start(f32[1,768]{1,0:T(1,128)S(1)} %get-tuple-element.18), channel_id=1, source_target_pairs={{0,3},{1,2},{6,5},{7,4},{8,11},{9,10},{14,13},{15,12},{16,19},{17,... | collective-permute-start | bytes 9224 | tf_op jit(solution)/shard_map/ppermute | solution.py:206
  115.8 0.1 collective-permute-start.3
  115.9 9.8 %all-to-all-start.1 = ((f32[128,1,32]{2,1,0:T(1,128)}), f32[128,1,32]{2,1,0:T(1,128)S(1)}, u32[]{:S(2)}, u32[]{:S(2)}) async-start(f32[128,1,32]{2,1,0:T(1,128)} %bitcast.4), calls=%async_computation.1 | async-start | bytes 131072 | tf_op jit(solution)/shard_map/all_to_all | solution.py:247
  125.7 0.0 collective-permute-done.2
  125.8 0.0 collective-permute-done.3
  125.8 0.7 broadcast_select_fusion
  126.5 10.6 %all-to-all-done.1 = f32[128,1,32]{2,1,0:T(1,128)S(1)} async-done(((f32[128,1,32]{2,1,0:T(1,128)}), f32[128,1,32]{2,1,0:T(1,128)S(1)}, u32[]{:S(2)}, u32[]{:S(2)}) %all-to-all-start.1) | async-done | bytes 16416 | tf_op jit(solution)/shard_map/all_to_all | solution.py:247
  137.1 0.0 copy-done.2
  137.1 0.9 shard_map.53
  (3 shorter events, 0.0 us)
Async XLA Ops:
  0.6 1.4 %copy-start = (bf16[1024,768]{1,0:T(8,128)(2,1)S(1)}, bf16[1024,768]{1,0:T(8,128)(2,1)}, u32[]{:S(2)}) copy-start(bf16[1024,768]{1,0:T(8,128)(2,1)} %x_hbm.1) | copy-start | bytes 4718596
  2.0 0.7 copy-start.1
  96.2 6.6 %collective-permute-start = (bf16[2048,768]{1,0:T(8,128)(2,1)S(1)}, bf16[2048,768]{1,0:T(8,128)(2,1)}, u32[]{:S(2)}, u32[]{:S(2)}) collective-permute-start(bf16[2048,768]{1,0:T(8,128)(2,1)S(1)} %bitcast.9), channel_id=1, source_target_pairs={{0,4},{4,0},{1,5},{5,1},{2,6},{6,2},{3,7},{7,3},{8,12},{12,8},{9,1... | collective-permute-start | bytes 9437192 | tf_op jit(solution)/shard_map/ppermute | solution.py:229
  98.9 3.9 %collective-permute-start.1 = (f32[3,2048]{1,0:T(4,128)S(1)}, f32[3,2048]{1,0:T(4,128)S(1)}, u32[]{:S(2)}, u32[]{:S(2)}) collective-permute-start(f32[3,2048]{1,0:T(4,128)S(1)} %get-tuple-element.13.info_ref), channel_id=1, source_target_pairs={{0,4},{4,0},{1,5},{5,1},{2,6},{6,2},{3,7},{7,3},{8,12},{12,8},{9,1... | collective-permute-start | bytes 73736 | tf_op jit(solution)/shard_map/ppermute | solution.py:232
  102.8 34.2 %copy-start.2 = (s32[1024,1]{0,1:T(1,128)S(1)}, s32[1024,1]{0,1:T(1,128)}, u32[]{:S(2)}) copy-start(s32[1024,1]{0,1:T(1,128)} %param.3) | copy-start | bytes 12292
  112.8 13.0 %collective-permute-start.2 = (f32[1,768]{1,0:T(1,128)S(1)}, f32[1,768]{1,0:T(1,128)S(1)}, u32[]{:S(2)}, u32[]{:S(2)}) collective-permute-start(f32[1,768]{1,0:T(1,128)S(1)} %get-tuple-element.18), channel_id=1, source_target_pairs={{0,3},{1,2},{6,5},{7,4},{8,11},{9,10},{14,13},{15,12},{16,19},{17,... | collective-permute-start | bytes 9224 | tf_op jit(solution)/shard_map/ppermute | solution.py:206
  115.8 10.0 %collective-permute-start.3 = (f32[1,768]{1,0:T(1,128)S(1)}, f32[1,768]{1,0:T(1,128)S(1)}, u32[]{:S(2)}, u32[]{:S(2)}) collective-permute-start(f32[1,768]{1,0:T(1,128)S(1)} %get-tuple-element.18), channel_id=1, source_target_pairs={{0,2},{4,1},{1,3},{5,0},{6,4},{2,7},{7,5},{3,6},{8,10},{12,9},{9,1... | collective-permute-start | bytes 9224 | tf_op jit(solution)/shard_map/ppermute | solution.py:205
  115.9 21.2 %all-to-all-start.1 = ((f32[128,1,32]{2,1,0:T(1,128)}), f32[128,1,32]{2,1,0:T(1,128)S(1)}, u32[]{:S(2)}, u32[]{:S(2)}) async-start(f32[128,1,32]{2,1,0:T(1,128)} %bitcast.4), calls=%async_computation.1 | async-start | bytes 131072 | tf_op jit(solution)/shard_map/all_to_all | solution.py:247

commit v6 on v5

--- a/solution.py
+++ b/solution.py
@@ -127,14 +127,44 @@
         best_ref[:, i * TILE : (i + 1) * TILE] = jnp.maximum(lanes(best_ref, 0, i), best)
 
 
-def rest_kernel(
-    x_ref, sib_hbm, info_ref, sib_info_ref, best_ref, out_ref, mean_ref, near_ref, fold_ref, sib_ref, sems
+def across_kernel(
+    core_ref, x_ref, sib_hbm, info_ref, sib_info_ref, before_ref, best_ref, give_ref, fold_ref, sib_ref, sems
 ):
-    def copy(j):
-        rows = slice(j * TILE, (j + 1) * TILE)
-        return pltpu.make_async_copy(sib_hbm.at[rows, :], sib_ref.at[rows, :], sems.at[j])
+    core = core_ref[0, 0]
+
+    def rows(k):
+        return pl.ds(pl.multiple_of(((core + k) & 3) * TILE, TILE), TILE)
+
+    def copy(k):
+        return pltpu.make_async_copy(
+            sib_hbm.at[rows(k), :], sib_ref.at[rows(k), :], sems.at[k]
+        )
 
     copy(0).start()
+    copy(2).start()
+    give_ref[...] = jnp.full((1, SLOTS), LOW, F32)
+    for i in range(TILES):
+        inv = to_column(lanes(info_ref, 0, i))
+        bias = to_column(lanes(info_ref, 1, i))
+        fold = None
+        for k in (i, i + 2):
+            if i < 2:
+                copy(k).wait()
+                if i == 0:
+                    copy(k + 1).start()
+            other = rows(k)
+            dots = lax.dot_general(
+                part(x_ref, i), sib_ref[other, :], NT, preferred_element_type=F32
+            )
+            value = fold_lanes(dots * sib_info_ref[0:1, other] + sib_info_ref[1:2, other])
+            fold = value if fold is None else jnp.maximum(fold, value)
+            down = jnp.max(dots * inv + bias, axis=0, keepdims=True)
+            give_ref[:, other] = jnp.maximum(give_ref[:, other], down)
+        best = to_row(jnp.max(fold, axis=1, keepdims=True))
+        best_ref[:, i * TILE : (i + 1) * TILE] = jnp.maximum(lanes(before_ref, 0, i), best)
+
+
+def centre_kernel(after_ref, x_ref, info_ref, sib_info_ref, centre_ref, mean_ref):
     total = info_ref[2:3, 0:WIDTH] + sib_info_ref[2:3, 0:WIDTH]
     count = info_ref[2:3, WIDTH : WIDTH + 1] + sib_info_ref[2:3, WIDTH : WIDTH + 1]
     mean_ref[...] = total / count
@@ -142,26 +172,15 @@
     parts = jnp.concatenate(split3(total) + (jnp.zeros((13, WIDTH), BF16),), axis=0)
     toward = lax.dot_general(parts, x_ref[...], NT, preferred_element_type=F32)
     toward = toward[0:1] + toward[1:2] + toward[2:3]
-    centre = toward * info_ref[0:1, :] * scale / WIDTH
-    for j in range(TILES):
-        copy(j).wait()
-        if j + 1 < TILES:
-            copy(j + 1).start()
-        for i in range(TILES):
-            dots = lax.dot_general(part(x_ref, i), part(sib_ref, j), NT, preferred_element_type=F32)
-            fold = fold_lanes(dots * lanes(sib_info_ref, 0, j) + lanes(sib_info_ref, 1, j))
-            fold = fold if j == 0 else jnp.maximum(part(fold_ref, i), fold)
-            if j + 1 < TILES:
-                fold_ref[i * TILE : (i + 1) * TILE, :] = fold
-            else:
-                best = to_row(jnp.max(fold, axis=1, keepdims=True))
-                best = jnp.maximum(best, lanes(best_ref, 0, i))
-                near_ref[:, i * TILE : (i + 1) * TILE] = jnp.maximum(
-                    -1.0, best * lanes(info_ref, 0, i) / WIDTH
-                )
+    centre_ref[...] = toward * info_ref[0:1, :] * scale / WIDTH
+
+
+def spread_kernel(best_ref, taken_ref, centre_ref, info_ref, out_ref):
+    best = jnp.maximum(best_ref[...], taken_ref[...])
+    near = jnp.maximum(-1.0, best * info_ref[0:1, :] / WIDTH)
     slot = lax.rem(iota((CAP, SLOTS), 1), CAP) == iota((CAP, SLOTS), 0)
-    near = jnp.where(slot, near_ref[...], 0.0)
-    centre = jnp.where(slot, centre, 0.0)
+    near = jnp.where(slot, near, 0.0)
+    centre = jnp.where(slot, centre_ref[...], 0.0)
     parts = jnp.concatenate(split3(jnp.concatenate([near, centre], axis=0)), axis=0)
     source = (iota((CHIPS, SLOTS), 1) // CAP == iota((CHIPS, SLOTS), 0)).astype(F32).astype(BF16)
     spread = lax.dot_general(source, parts, NT, preferred_element_type=F32)
@@ -232,18 +251,26 @@
     sib_info = lax.ppermute(info, "core", swap)
     fold = pltpu.VMEM((TILE, 128), F32)
     best = call(own_kernel, row, block * 3 / 8, (fold,))(mine, info, best)
-    out, mean = call(
-        rest_kernel,
-        (struct((CHIPS, 2 * CAP), F32), struct((1, WIDTH), F32)),
-        block,
+    core = lax.axis_index("core").astype(jnp.int32).reshape(1, 1)
+    best, give = call(
+        across_kernel,
+        (row, row),
+        block / 2,
         (
-            pltpu.VMEM((1, SLOTS), F32),
-            pltpu.VMEM((SLOTS, 128), F32),
+            fold,
             pltpu.VMEM((SLOTS, WIDTH), BF16),
             pltpu.SemaphoreType.DMA((TILES,)),
         ),
-        in_specs=[here, pl.BlockSpec(memory_space=pltpu.HBM), here, here, here],
-    )(mine, sib, info, sib_info, best)
+        in_specs=[
+            pl.BlockSpec(memory_space=pltpu.SMEM), here, pl.BlockSpec(memory_space=pltpu.HBM),
+            here, here, here,
+        ],
+    )(core, mine, sib, info, sib_info, best)
+    taken = lax.ppermute(give, "core", swap)
+    centre, mean = call(
+        centre_kernel, (row, struct((1, WIDTH), F32)), block / 8
+    )(give, mine, info, sib_info)
+    out = call(spread_kernel, struct((CHIPS, 2 * CAP), F32), 1e8)(best, taken, centre, info)
     back = lax.all_to_all(out, chips, 0, 0, tiled=True)
     means = share_means(mean)
     near, centre = call(

time: 138 us -> 140 us (1.014)
  starting transfers between devices: 13.7 us -> 16.4 us
  Pallas kernels: 20.7 us -> 18.6 us
  waiting for transfers between devices: 10.6 us -> 12 us
    pallas_call x1 -> x3, Pallas kernels: 9.88 us -> 7.82 us  [the longest x1 5.87 us: shards(): call(across_kernel, (row, row), block / 2, (fold, pltpu.VMEM((SLOTS, WIDT...]
    ppermute x1, starting transfers between devices: 0.09 us -> 2.03 us  [share_means(): one = lax.ppermute(mean, ('core', 'x'), first)]
  transfers between devices with their start and end apart: 5 -> 6, of which waited for: 1 -> 2; matrix products, arithmetic and copies ran while one was open for 1% -> 1% of each run, Pallas kernels for 4% -> 4%
where the time goes in v6:
time: 140 us
  blocking collectives  89.4 us (64%)
  Pallas kernels  18.6 us (13%)
  starting transfers between devices  16.4 us (12%)
  waiting for transfers between devices  12 us (9%)
  local copies, waits for them, and re-layouts  2.09 us (1%)
    all_to_all x1, blocking collectives, shards(): lax.all_to_all(send.reshape(CHIPS, CAP, WIDTH), chips, 0, 0, tiled=True)  89.4 us
    all_to_all x1, waiting for transfers between devices, shards(): back = lax.all_to_all(out, chips, 0, 0, tiled=True)  10.7 us
    all_to_all x1, starting transfers between devices, shards(): back = lax.all_to_all(out, chips, 0, 0, tiled=True)  10.5 us
    pallas_call x1, Pallas kernels, shards(): call(across_kernel, (row, row), block / 2, (fold, pltpu.VMEM((SLOTS, WIDT...  5.87 us
    pallas_call x1, Pallas kernels, shards(): call(pack_kernel, (struct((SLOTS, WIDTH), BF16), struct((1, ROWS), jnp.in...  4.1 us
    pallas_call x1, Pallas kernels, shards(): best = call(own_kernel, row, block * 3 / 8, (fold,))(mine, info, best)  3.11 us
    ppermute x1, starting transfers between devices, share_means(): two = lax.ppermute(mean, ('core', 'x'), second)  3.01 us
  transfers between devices with their start and end apart: 6, of which 2 were waited for; matrix products, arithmetic and copies ran while one was open for 1% of the time, Pallas kernels for 4%

profile of v6, /device:TPU:2, one launch (start us, length us, event | category | flops | bytes accessed | tf_op | source)
XLA Modules:
  0.0 140.0 jit_solution(13665191523526187486)
XLA Ops:
  0.6 0.0 copy-start
  0.6 1.4 copy-done
  2.0 0.0 copy-start.1
  2.0 0.7 copy-done.1
  2.7 4.1 %shard_map.49 = (bf16[2048,768]{1,0:T(8,128)(2,1)S(1)}, s32[1,1024]{1,0:T(1,128)S(1)}) custom-call(s32[1,1024]{1,0:T(1,128)S(1)} %bitcast.17, bf16[1024,768]{1,0:T(8,128)(2,1)S(1)} %copy-done), custom_call_target="tpu_custom_call" | custom-call | flops 3221225472 | bytes 6000000 | tf_op jit(solution)/shard_map/pallas_call | solution.py:237
  6.8 89.4 %all_to_all.16 = bf16[128,16,768]{2,1,0:T(8,128)(2,1)S(1)} all-to-all(bf16[128,16,768]{2,1,0:T(8,128)(2,1)S(1)} %bitcast.15), channel_id=1, replica_groups=mesh['y'=4,'z'=8,'core'=2,'x'=4] {'z','x','y'}, dimensions={0} | all-to-all | bytes 6291456 | tf_op jit(solution)/shard_map/all_to_all | solution.py:245
  96.2 0.0 collective-permute-start
  96.2 2.7 %shard_map.50 = (f32[3,2048]{1,0:T(4,128)S(1)}, f32[1,2048]{1,0:T(1,128)S(1)}) custom-call(bf16[2048,768]{1,0:T(8,128)(2,1)S(1)} %bitcast.11), custom_call_target="tpu_custom_call" | custom-call | flops 1610612736 | bytes 6000000 | tf_op jit(solution)/shard_map/pallas_call | solution.py:250
  98.9 0.8 collective-permute-start.1
  99.7 3.1 %shard_map.51.before_ref = f32[1,2048]{1,0:T(1,128)S(1)} custom-call(bf16[2048,768]{1,0:T(8,128)(2,1)S(1)} %bitcast.12, f32[3,2048]{1,0:T(4,128)S(1)} %get-tuple-element.15.info_ref, f32[1,2048]{1,0:T(1,128)S(1)} %get-tuple-element.16.before_ref), custom_call_target="tpu_custom_call" | custom-call | flops 2415919104 | bytes 6000000 | tf_op jit(solution)/shard_map/pallas_call | solution.py:253
  102.8 0.0 collective-permute-done.1.sib_info_ref
  102.8 0.0 collective-permute-done.sib_hbm
  102.9 5.9 %shard_map.52 = (f32[1,2048]{1,0:T(1,128)S(1)}, f32[1,2048]{1,0:T(1,128)S(1)}) custom-call(s32[1,1]{1,0:T(1,128)} %bitcast.1.core_ref, bf16[2048,768]{1,0:T(8,128)(2,1)S(1)} %bitcast.13, bf16[2048,768]{1,0:T(8,128)(2,1)} %collective-permute-done.sib_hbm, f32[3,2048]{1,0:T(4,128)S(1)} %get-tuple-element.15.info_ref, ...), custom_call_target="tpu_custom_call" | custom-call | flops 3221225472 | bytes 6000000 | tf_op jit(solution)/shard_map/pallas_call | solution.py:255
  108.7 0.0 copy-start.2
  108.7 0.9 shard_map.53
  109.7 3.0 %collective-permute-start.3 = (f32[1,768]{1,0:T(1,128)S(1)}, f32[1,768]{1,0:T(1,128)S(1)}, u32[]{:S(2)}, u32[]{:S(2)}) collective-permute-start(f32[1,768]{1,0:T(1,128)S(1)} %get-tuple-element.22), channel_id=1, source_target_pairs={{0,3},{1,2},{6,5},{7,4},{8,11},{9,10},{14,13},{15,12},{16,19},{17,... | collective-permute-start | bytes 9224 | tf_op jit(solution)/shard_map/ppermute | solution.py:225
  112.7 0.1 collective-permute-start.2
  112.8 2.0 %collective-permute-start.4 = (f32[1,768]{1,0:T(1,128)S(1)}, f32[1,768]{1,0:T(1,128)S(1)}, u32[]{:S(2)}, u32[]{:S(2)}) collective-permute-start(f32[1,768]{1,0:T(1,128)S(1)} %get-tuple-element.22), channel_id=1, source_target_pairs={{0,2},{4,1},{1,3},{5,0},{6,4},{2,7},{7,5},{3,6},{8,10},{12,9},{9,1... | collective-permute-start | bytes 9224 | tf_op jit(solution)/shard_map/ppermute | solution.py:224
  114.9 0.0 collective-permute-done.3
  114.9 1.3 collective-permute-done.4
  116.2 0.0 collective-permute-done.2.taken_ref
  116.2 1.0 shard_map.54
  117.2 10.5 %all-to-all-start.1 = ((f32[128,1,32]{2,1,0:T(1,128)}), f32[128,1,32]{2,1,0:T(1,128)S(1)}, u32[]{:S(2)}, u32[]{:S(2)}) async-start(f32[128,1,32]{2,1,0:T(1,128)} %bitcast.5), calls=%async_computation.1 | async-start | bytes 131072 | tf_op jit(solution)/shard_map/all_to_all | solution.py:274
  127.7 0.7 broadcast_select_fusion
  128.4 10.7 %all-to-all-done.1 = f32[128,1,32]{2,1,0:T(1,128)S(1)} async-done(((f32[128,1,32]{2,1,0:T(1,128)}), f32[128,1,32]{2,1,0:T(1,128)S(1)}, u32[]{:S(2)}, u32[]{:S(2)}) %all-to-all-start.1) | async-done | bytes 16416 | tf_op jit(solution)/shard_map/all_to_all | solution.py:274
  139.1 0.0 copy-done.2
  139.1 0.9 shard_map.55
  (3 shorter events, 0.0 us)
Async XLA Ops:
  0.6 1.4 %copy-start = (bf16[1024,768]{1,0:T(8,128)(2,1)S(1)}, bf16[1024,768]{1,0:T(8,128)(2,1)}, u32[]{:S(2)}) copy-start(bf16[1024,768]{1,0:T(8,128)(2,1)} %x_hbm.1) | copy-start | bytes 4718596
  2.0 0.7 copy-start.1
  96.2 6.6 %collective-permute-start = (bf16[2048,768]{1,0:T(8,128)(2,1)S(1)}, bf16[2048,768]{1,0:T(8,128)(2,1)}, u32[]{:S(2)}, u32[]{:S(2)}) collective-permute-start(bf16[2048,768]{1,0:T(8,128)(2,1)S(1)} %bitcast.10), channel_id=1, source_target_pairs={{0,4},{4,0},{1,5},{5,1},{2,6},{6,2},{3,7},{7,3},{8,12},{12,8},{9,1... | collective-permute-start | bytes 9437192 | tf_op jit(solution)/shard_map/ppermute | solution.py:248
  98.9 3.9 %collective-permute-start.1 = (f32[3,2048]{1,0:T(4,128)S(1)}, f32[3,2048]{1,0:T(4,128)S(1)}, u32[]{:S(2)}, u32[]{:S(2)}) collective-permute-start(f32[3,2048]{1,0:T(4,128)S(1)} %get-tuple-element.15.info_ref), channel_id=1, source_target_pairs={{0,4},{4,0},{1,5},{5,1},{2,6},{6,2},{3,7},{7,3},{8,12},{12,8},{9,1... | collective-permute-start | bytes 73736 | tf_op jit(solution)/shard_map/ppermute | solution.py:251
  108.7 30.4 %copy-start.2 = (s32[1024,1]{0,1:T(1,128)S(1)}, s32[1024,1]{0,1:T(1,128)}, u32[]{:S(2)}) copy-start(s32[1024,1]{0,1:T(1,128)} %param.3) | copy-start | bytes 12292
  109.7 5.2 %collective-permute-start.3 = (f32[1,768]{1,0:T(1,128)S(1)}, f32[1,768]{1,0:T(1,128)S(1)}, u32[]{:S(2)}, u32[]{:S(2)}) collective-permute-start(f32[1,768]{1,0:T(1,128)S(1)} %get-tuple-element.22), channel_id=1, source_target_pairs={{0,3},{1,2},{6,5},{7,4},{8,11},{9,10},{14,13},{15,12},{16,19},{17,... | collective-permute-start | bytes 9224 | tf_op jit(solution)/shard_map/ppermute | solution.py:225
  112.7 3.5 %collective-permute-start.2 = (f32[1,2048]{1,0:T(1,128)S(1)}, f32[1,2048]{1,0:T(1,128)S(1)}, u32[]{:S(2)}, u32[]{:S(2)}) collective-permute-start(f32[1,2048]{1,0:T(1,128)S(1)} %get-tuple-element.18.after_ref), channel_id=1, source_target_pairs={{0,4},{4,0},{1,5},{5,1},{2,6},{6,2},{3,7},{7,3},{8,12},{12,8},{9,1... | collective-permute-start | bytes 24584 | tf_op jit(solution)/shard_map/ppermute | solution.py:269
  112.8 3.3 %collective-permute-start.4 = (f32[1,768]{1,0:T(1,128)S(1)}, f32[1,768]{1,0:T(1,128)S(1)}, u32[]{:S(2)}, u32[]{:S(2)}) collective-permute-start(f32[1,768]{1,0:T(1,128)S(1)} %get-tuple-element.22), channel_id=1, source_target_pairs={{0,2},{4,1},{1,3},{5,0},{6,4},{2,7},{7,5},{3,6},{8,10},{12,9},{9,1... | collective-permute-start | bytes 9224 | tf_op jit(solution)/shard_map/ppermute | solution.py:224
  117.2 21.9 %all-to-all-start.1 = ((f32[128,1,32]{2,1,0:T(1,128)}), f32[128,1,32]{2,1,0:T(1,128)S(1)}, u32[]{:S(2)}, u32[]{:S(2)}) async-start(f32[128,1,32]{2,1,0:T(1,128)} %bitcast.5), calls=%async_computation.1 | async-start | bytes 131072 | tf_op jit(solution)/shard_map/all_to_all | solution.py:274

commit v7 on v5

--- a/solution.py
+++ b/solution.py
@@ -10,6 +10,8 @@
 WIDTH = 768
 CAP = 16
 CHIPS = 128
+XS = 4
+PAIR = 2 * CAP
 SLOTS = CHIPS * CAP
 MARK = 64.0
 LOW = -1e30
@@ -128,8 +130,10 @@
 
 
 def rest_kernel(
-    x_ref, sib_hbm, info_ref, sib_info_ref, best_ref, out_ref, mean_ref, near_ref, fold_ref, sib_ref, sems
+    place_ref, x_ref, sib_hbm, info_ref, sib_info_ref, best_ref, *refs
 ):
+    out_refs, (near_ref, fold_ref, sib_ref, sems) = refs[:XS], refs[XS:]
+
     def copy(j):
         rows = slice(j * TILE, (j + 1) * TILE)
         return pltpu.make_async_copy(sib_hbm.at[rows, :], sib_ref.at[rows, :], sems.at[j])
@@ -137,7 +141,7 @@
     copy(0).start()
     total = info_ref[2:3, 0:WIDTH] + sib_info_ref[2:3, 0:WIDTH]
     count = info_ref[2:3, WIDTH : WIDTH + 1] + sib_info_ref[2:3, WIDTH : WIDTH + 1]
-    mean_ref[...] = total / count
+    mean = total / count
     scale = lax.rsqrt(jnp.sum(total * total, axis=1, keepdims=True) / WIDTH + EPS)
     parts = jnp.concatenate(split3(total) + (jnp.zeros((13, WIDTH), BF16),), axis=0)
     toward = lax.dot_general(parts, x_ref[...], NT, preferred_element_type=F32)
@@ -163,22 +167,44 @@
     near = jnp.where(slot, near_ref[...], 0.0)
     centre = jnp.where(slot, centre, 0.0)
     parts = jnp.concatenate(split3(jnp.concatenate([near, centre], axis=0)), axis=0)
-    source = (iota((CHIPS, SLOTS), 1) // CAP == iota((CHIPS, SLOTS), 0)).astype(F32).astype(BF16)
+    here = place_ref[0, 0]
+    chip = iota((1, SLOTS), 1) // CAP
+    row = (((chip >> 2) - here) & 3) * 32 + (chip >> 4) * 4 + (chip & 3)
+    source = (row == iota((CHIPS, SLOTS), 0)).astype(F32).astype(BF16)
     spread = lax.dot_general(source, parts, NT, preferred_element_type=F32)
-    out_ref[...] = (
-        spread[:, 0 : 2 * CAP] + spread[:, 2 * CAP : 4 * CAP] + spread[:, 4 * CAP : 6 * CAP]
-    )
+    spread = spread[:, 0:PAIR] + spread[:, PAIR : 2 * PAIR] + spread[:, 2 * PAIR : 3 * PAIR]
+    spread = jnp.concatenate([spread] * XS, axis=1)
+    spread = jnp.where(iota((CHIPS, XS * PAIR), 1) // PAIR == here, spread, 0.0)
+    folded = [mean[:, k : k + 128] for k in range(0, WIDTH, 128)]
+    folded = jnp.concatenate(folded + [jnp.zeros((2, 128), F32)], axis=0)
+    for k in range(XS):
+        out_refs[k][0:32, :] = spread[32 * k : 32 * (k + 1)]
+        out_refs[k][32:40, :] = folded
+
+
+def merge_kernel(place_ref, *refs):
+    came, (out_ref, mean_ref) = refs[:XS], refs[XS:]
+    out_ref[...] = sum(ref[0:32, :] for ref in came)
+    for k in range(2):
+        offset = (place_ref[0, 0] - 2 * place_ref[0, 1] - k) & 3
+        folded = sum(jnp.where(offset == i, ref[32:40, :], 0.0) for i, ref in enumerate(came))
+        for j in range(WIDTH // 128):
+            mean_ref[k : k + 1, j * 128 : (j + 1) * 128] = folded[j : j + 1]
 
 
 def unpack_kernel(ids_ref, rank_ref, back_ref, near_ref, centre_ref):
-    same = iota((CHIPS, ROWS), 0) == chip_of(ids_ref[...])
+    ids = ids_ref[...]
+    same = iota((32, ROWS), 0) == ((ids >> 2) & 7) * 4 + (ids >> 5)
     onehot = same.astype(F32).astype(BF16)
     parts = jnp.concatenate(split3(back_ref[...]), axis=1)
     picked = lax.dot_general(parts, onehot, TN, preferred_element_type=F32)
-    picked = picked[0 : 2 * CAP] + picked[2 * CAP : 4 * CAP] + picked[4 * CAP : 6 * CAP]
-    slot = iota((CAP, ROWS), 0) == rank_ref[...]
-    near_ref[...] = jnp.sum(jnp.where(slot, picked[0:CAP], 0.0), axis=0, keepdims=True)
-    centre_ref[...] = jnp.sum(jnp.where(slot, picked[CAP:], 0.0), axis=0, keepdims=True)
+    picked = picked[0:128] + picked[128:256] + picked[256:384]
+    place = (ids & 3) * PAIR + rank_ref[...]
+    line = iota((128, ROWS), 0)
+    near_ref[...] = jnp.sum(jnp.where(line == place, picked, 0.0), axis=0, keepdims=True)
+    centre_ref[...] = jnp.sum(
+        jnp.where(line == place + CAP, picked, 0.0), axis=0, keepdims=True
+    )
 
 
 def struct(shape, dtype):
@@ -196,19 +222,6 @@
         ),
         **specs,
     )
-
-
-def share_means(mean):
-    x, core = lax.axis_index("x"), lax.axis_index("core")
-    first = [(0, 2), (4, 1), (1, 3), (5, 0), (6, 4), (2, 7), (7, 5), (3, 6)]
-    second = [(0, 3), (1, 2), (6, 5), (7, 4)]
-    one = lax.ppermute(mean, ("core", "x"), first)
-    two = lax.ppermute(mean, ("core", "x"), second)
-    near = x // 2 == core
-    other = jnp.where(near, mean, two)
-    low = lax.rem(x, 2) == 0
-    own_low = jnp.where(near, low, ~low)
-    return jnp.where(own_low == (jnp.arange(2)[:, None] == 0), other, one)
 
 
 def shards(embeddings, cluster_ids):
@@ -232,9 +245,13 @@
     sib_info = lax.ppermute(info, "core", swap)
     fold = pltpu.VMEM((TILE, 128), F32)
     best = call(own_kernel, row, block * 3 / 8, (fold,))(mine, info, best)
-    out, mean = call(
+    axes = [lax.axis_index("x"), lax.axis_index("core")]
+    place = jnp.stack(axes).astype(jnp.int32).reshape(1, 2)
+    scalars = pl.BlockSpec(memory_space=pltpu.SMEM)
+    line = struct((40, 128), F32)
+    outs = call(
         rest_kernel,
-        (struct((CHIPS, 2 * CAP), F32), struct((1, WIDTH), F32)),
+        (line,) * XS,
         block,
         (
             pltpu.VMEM((1, SLOTS), F32),
@@ -242,10 +259,18 @@
             pltpu.VMEM((SLOTS, WIDTH), BF16),
             pltpu.SemaphoreType.DMA((TILES,)),
         ),
-        in_specs=[here, pl.BlockSpec(memory_space=pltpu.HBM), here, here, here],
-    )(mine, sib, info, sib_info, best)
-    back = lax.all_to_all(out, chips, 0, 0, tiled=True)
-    means = share_means(mean)
+        in_specs=[scalars, here, pl.BlockSpec(memory_space=pltpu.HBM), here, here, here],
+    )(place, mine, sib, info, sib_info, best)
+    came = [outs[0]]
+    for k in range(1, XS):
+        came.append(lax.ppermute(outs[k], "x", [(i, (i + k) % XS) for i in range(XS)]))
+    out, means = call(
+        merge_kernel,
+        (struct((32, 128), F32), struct((2, WIDTH), F32)),
+        1e6,
+        in_specs=[scalars] + [here] * XS,
+    )(place, *came)
+    back = lax.all_to_all(out, ("z", "y"), 0, 0, tiled=True)
     near, centre = call(
         unpack_kernel, (struct((1, ROWS), F32), struct((1, ROWS), F32)), 1e8
     )(ids, rank, back)

time: 138 us -> 137 us (level)
  blocking collectives: 89.4 us -> 104 us
  starting transfers between devices: 13.7 us -> 4.29 us
  waiting for transfers between devices: 10.6 us -> 3.77 us
    all_to_all x0 -> x1, blocking collectives: none -> 14.7 us  [shards(): back = lax.all_to_all(out, ('z', 'y'), 0, 0, tiled=True)]
    all_to_all x1 -> x0, waiting for transfers between devices: 10.6 us -> none  [shards(): back = lax.all_to_all(out, chips, 0, 0, tiled=True)]
    all_to_all x1 -> x0, starting transfers between devices: 9.84 us -> none  [shards(): back = lax.all_to_all(out, chips, 0, 0, tiled=True)]
    ppermute x2 -> x3, waiting for transfers between devices: 0.01 us -> 3.77 us  [shards(): lax.ppermute(outs[k], 'x', [(i, (i + k) % XS) for i in range(XS)])]
    pallas_call x1 -> x2, Pallas kernels: 9.88 us -> 10.9 us  [the longest x1 9.75 us: shards(): call(rest_kernel, (line,) * XS, block, (pltpu.VMEM((1, SLOTS), F32), pltp...]
    ppermute x2 -> x3, starting transfers between devices: 3.11 us -> 3.51 us  [shards(): lax.ppermute(outs[k], 'x', [(i, (i + k) % XS) for i in range(XS)])]
  transfers between devices with their start and end apart: 5 -> 5, of which waited for: 1 -> 3; matrix products, arithmetic and copies ran while one was open for 1% -> 0% of each run, Pallas kernels for 4% -> 4%
where the time goes in v7:
time: 137 us
  blocking collectives  104 us (76%)
  Pallas kernels  21.9 us (16%)
  starting transfers between devices  4.29 us (3%)
  waiting for transfers between devices  3.77 us (3%)
  local copies, waits for them, and re-layouts  2.09 us (2%)
    all_to_all x1, blocking collectives, shards(): lax.all_to_all(send.reshape(CHIPS, CAP, WIDTH), chips, 0, 0, tiled=True)  89.4 us
    all_to_all x1, blocking collectives, shards(): back = lax.all_to_all(out, ('z', 'y'), 0, 0, tiled=True)  14.7 us
    pallas_call x1, Pallas kernels, shards(): call(rest_kernel, (line,) * XS, block, (pltpu.VMEM((1, SLOTS), F32), pltp...  9.75 us
    pallas_call x1, Pallas kernels, shards(): call(pack_kernel, (struct((SLOTS, WIDTH), BF16), struct((1, ROWS), jnp.in...  4.1 us
    ppermute x3, waiting for transfers between devices, shards(): lax.ppermute(outs[k], 'x', [(i, (i + k) % XS) for i in range(XS)])  3.77 us
    ppermute x3, starting transfers between devices, shards(): lax.ppermute(outs[k], 'x', [(i, (i + k) % XS) for i in range(XS)])  3.51 us
    pallas_call x1, Pallas kernels, shards(): best = call(own_kernel, row, block * 3 / 8, (fold,))(mine, info, best)  3.12 us
  transfers between devices with their start and end apart: 5, of which 3 were waited for; matrix products, arithmetic and copies ran while one was open for 0% of the time, Pallas kernels for 4%

profile of v7, /device:TPU:2, one launch (start us, length us, event | category | flops | bytes accessed | tf_op | source)
XLA Modules:
  0.0 136.9 jit_solution(1136748129945955291)
XLA Ops:
  0.6 0.0 copy-start
  0.6 1.4 %copy-done = bf16[1024,768]{1,0:T(8,128)(2,1)S(1)} copy-done((bf16[1024,768]{1,0:T(8,128)(2,1)S(1)}, bf16[1024,768]{1,0:T(8,128)(2,1)}, u32[]{:S(2)}) %copy-start) | copy-done | bytes 1572888
  2.0 0.0 copy-start.1
  2.0 0.7 copy-done.1
  2.7 4.1 %shard_map.49 = (bf16[2048,768]{1,0:T(8,128)(2,1)S(1)}, s32[1,1024]{1,0:T(1,128)S(1)}) custom-call(s32[1,1024]{1,0:T(1,128)S(1)} %bitcast.20, bf16[1024,768]{1,0:T(8,128)(2,1)S(1)} %copy-done), custom_call_target="tpu_custom_call" | custom-call | flops 3221225472 | bytes 6000000 | tf_op jit(solution)/shard_map/pallas_call | solution.py:231
  6.8 89.4 %all_to_all.16 = bf16[128,16,768]{2,1,0:T(8,128)(2,1)S(1)} all-to-all(bf16[128,16,768]{2,1,0:T(8,128)(2,1)S(1)} %bitcast.17), channel_id=1, replica_groups=mesh['y'=4,'z'=8,'core'=2,'x'=4] {'z','x','y'}, dimensions={0} | all-to-all | bytes 6291456 | tf_op jit(solution)/shard_map/all_to_all | solution.py:239
  96.2 0.0 collective-permute-start
  96.2 0.1 add_bitcast_fusion.place_ref
  96.3 2.7 %shard_map.50 = (f32[3,2048]{1,0:T(4,128)S(1)}, f32[1,2048]{1,0:T(1,128)S(1)}) custom-call(bf16[2048,768]{1,0:T(8,128)(2,1)S(1)} %bitcast.14), custom_call_target="tpu_custom_call" | custom-call | flops 1610612736 | bytes 6000000 | tf_op jit(solution)/shard_map/pallas_call | solution.py:244
  99.0 0.8 collective-permute-start.1
  99.8 3.1 %shard_map.51.best_ref = f32[1,2048]{1,0:T(1,128)S(1)} custom-call(bf16[2048,768]{1,0:T(8,128)(2,1)S(1)} %bitcast.15, f32[3,2048]{1,0:T(4,128)S(1)} %get-tuple-element.17.info_ref, f32[1,2048]{1,0:T(1,128)S(1)} %get-tuple-element.18.before_ref), custom_call_target="tpu_custom_call" | custom-call | flops 2415919104 | bytes 6000000 | tf_op jit(solution)/shard_map/pallas_call | solution.py:247
  102.9 0.0 copy-start.2
  102.9 0.0 collective-permute-done.1.sib_info_ref
  103.0 0.0 collective-permute-done.sib_hbm
  103.0 9.7 %shard_map.52 = (f32[40,128]{1,0:T(8,128)S(1)}, f32[40,128]{1,0:T(8,128)S(1)}, f32[40,128]{1,0:T(8,128)S(1)}, f32[40,128]{1,0:T(8,128)S(1)}) custom-call(s32[1,2]{1,0:T(1,128)S(1)} %add_bitcast_fusion.place_ref, bf16[2048,768]{1,0:T(8,128)(2,1)S(1)} %bitcast.16, bf16[2048,768]{1,0:T(8,128)(2,1)} %collective-permute-done.sib_hbm, ...), custom_call_target="tpu_custom_call" | custom-call | flops 6442450944 | bytes 6000000 | tf_op jit(solution)/shard_map/pallas_call | solution.py:252
  112.7 1.2 collective-permute-start.2
  113.9 2.3 %collective-permute-start.3 = (f32[40,128]{1,0:T(8,128)S(1)}, f32[40,128]{1,0:T(8,128)S(1)}, u32[]{:S(2)}, u32[]{:S(2)}) collective-permute-start(f32[40,128]{1,0:T(8,128)S(1)} %get-tuple-element.21), channel_id=1, source_target_pairs={{0,2},{1,3},{2,0},{3,1},{4,6},{5,7},{6,4},{7,5},{8,10},{9,11},{10,... | collective-permute-start | bytes 61448 | tf_op jit(solution)/shard_map/ppermute | solution.py:266
  116.2 0.0 collective-permute-start.4
  116.2 0.3 collective-permute-done.2.refs_1_
  116.6 2.6 %collective-permute-done.3.refs_2_ = f32[40,128]{1,0:T(8,128)S(1)} collective-permute-done((f32[40,128]{1,0:T(8,128)S(1)}, f32[40,128]{1,0:T(8,128)S(1)}, u32[]{:S(2)}, u32[]{:S(2)}) %collective-permute-start.3) | collective-permute-done | bytes 20512 | tf_op jit(solution)/shard_map/ppermute | solution.py:266
  119.2 0.8 collective-permute-done.4.refs_3_
  120.0 1.2 shard_map.53
  121.2 14.7 %all_to_all.17 = f32[32,1,128]{2,1,0:T(1,128)S(1)} all-to-all(f32[32,1,128]{2,1,0:T(1,128)S(1)} %bitcast.18), channel_id=1, replica_groups=mesh['y'=4,'z'=8,'core'=2,'x'=4] {'z','y'}, dimensions={0} | all-to-all | bytes 32768 | tf_op jit(solution)/shard_map/all_to_all | solution.py:273
  135.9 0.0 copy-done.2
  135.9 1.0 shard_map.54
Async XLA Ops:
  0.6 1.4 %copy-start = (bf16[1024,768]{1,0:T(8,128)(2,1)S(1)}, bf16[1024,768]{1,0:T(8,128)(2,1)}, u32[]{:S(2)}) copy-start(bf16[1024,768]{1,0:T(8,128)(2,1)} %x_hbm.1) | copy-start | bytes 4718596
  2.0 0.7 copy-start.1
  96.2 6.7 %collective-permute-start = (bf16[2048,768]{1,0:T(8,128)(2,1)S(1)}, bf16[2048,768]{1,0:T(8,128)(2,1)}, u32[]{:S(2)}, u32[]{:S(2)}) collective-permute-start(bf16[2048,768]{1,0:T(8,128)(2,1)S(1)} %bitcast.13), channel_id=1, source_target_pairs={{0,4},{4,0},{1,5},{5,1},{2,6},{6,2},{3,7},{7,3},{8,12},{12,8},{9,1... | collective-permute-start | bytes 9437192 | tf_op jit(solution)/shard_map/ppermute | solution.py:242
  99.0 3.9 %collective-permute-start.1 = (f32[3,2048]{1,0:T(4,128)S(1)}, f32[3,2048]{1,0:T(4,128)S(1)}, u32[]{:S(2)}, u32[]{:S(2)}) collective-permute-start(f32[3,2048]{1,0:T(4,128)S(1)} %get-tuple-element.17.info_ref), channel_id=1, source_target_pairs={{0,4},{4,0},{1,5},{5,1},{2,6},{6,2},{3,7},{7,3},{8,12},{12,8},{9,1... | collective-permute-start | bytes 73736 | tf_op jit(solution)/shard_map/ppermute | solution.py:245
  102.9 32.9 %copy-start.2 = (s32[1024,1]{0,1:T(1,128)S(1)}, s32[1024,1]{0,1:T(1,128)}, u32[]{:S(2)}) copy-start(s32[1024,1]{0,1:T(1,128)} %param.3) | copy-start | bytes 12292
  112.7 3.9 %collective-permute-start.2 = (f32[40,128]{1,0:T(8,128)S(1)}, f32[40,128]{1,0:T(8,128)S(1)}, u32[]{:S(2)}, u32[]{:S(2)}) collective-permute-start(f32[40,128]{1,0:T(8,128)S(1)} %get-tuple-element.20), channel_id=1, source_target_pairs={{0,1},{1,2},{2,3},{3,0},{4,5},{5,6},{6,7},{7,4},{8,9},{9,10},{10,1... | collective-permute-start | bytes 61448 | tf_op jit(solution)/shard_map/ppermute | solution.py:266
  113.9 5.3 %collective-permute-start.3 = (f32[40,128]{1,0:T(8,128)S(1)}, f32[40,128]{1,0:T(8,128)S(1)}, u32[]{:S(2)}, u32[]{:S(2)}) collective-permute-start(f32[40,128]{1,0:T(8,128)S(1)} %get-tuple-element.21), channel_id=1, source_target_pairs={{0,2},{1,3},{2,0},{3,1},{4,6},{5,7},{6,4},{7,5},{8,10},{9,11},{10,... | collective-permute-start | bytes 61448 | tf_op jit(solution)/shard_map/ppermute | solution.py:266
  116.2 3.8 %collective-permute-start.4 = (f32[40,128]{1,0:T(8,128)S(1)}, f32[40,128]{1,0:T(8,128)S(1)}, u32[]{:S(2)}, u32[]{:S(2)}) collective-permute-start(f32[40,128]{1,0:T(8,128)S(1)} %get-tuple-element.22), channel_id=1, source_target_pairs={{0,3},{1,0},{2,1},{3,2},{4,7},{5,4},{6,5},{7,6},{8,11},{9,8},{10,9... | collective-permute-start | bytes 61448 | tf_op jit(solution)/shard_map/ppermute | solution.py:266

commit v8 on v7

--- a/solution.py
+++ b/solution.py
@@ -116,7 +116,7 @@
 
 def own_kernel(x_ref, info_ref, before_ref, best_ref, fold_ref):
     best_ref[...] = before_ref[...]
-    for i in range(TILES - 1):
+    for i in range(TILES - 2):
         inv = to_column(lanes(info_ref, 0, i))
         bias = to_column(lanes(info_ref, 1, i))
         for j in range(i + 1, TILES):
@@ -129,43 +129,75 @@
         best_ref[:, i * TILE : (i + 1) * TILE] = jnp.maximum(lanes(best_ref, 0, i), best)
 
 
-def rest_kernel(
-    place_ref, x_ref, sib_hbm, info_ref, sib_info_ref, best_ref, *refs
+def across_kernel(
+    place_ref, x_ref, sib_hbm, info_ref, sib_info_ref, before_ref,
+    best_ref, give_ref, centre_ref, mean_ref, sib_ref, turned_ref, sems,
 ):
-    out_refs, (near_ref, fold_ref, sib_ref, sems) = refs[:XS], refs[XS:]
-
-    def copy(j):
-        rows = slice(j * TILE, (j + 1) * TILE)
-        return pltpu.make_async_copy(sib_hbm.at[rows, :], sib_ref.at[rows, :], sems.at[j])
+    core = place_ref[0, 1]
+
+    def rows(k):
+        return pl.ds(pl.multiple_of(((core + k) & 3) * TILE, TILE), TILE)
+
+    def copy(k):
+        return pltpu.make_async_copy(
+            sib_hbm.at[rows(k), :], sib_ref.at[k * TILE : (k + 1) * TILE, :], sems.at[k]
+        )
 
     copy(0).start()
+    copy(2).start()
+    for k in range(TILES):
+        turned_ref[:, k * TILE : (k + 1) * TILE] = sib_info_ref[0:2, rows(k)]
     total = info_ref[2:3, 0:WIDTH] + sib_info_ref[2:3, 0:WIDTH]
     count = info_ref[2:3, WIDTH : WIDTH + 1] + sib_info_ref[2:3, WIDTH : WIDTH + 1]
-    mean = total / count
+    mean_ref[...] = total / count
     scale = lax.rsqrt(jnp.sum(total * total, axis=1, keepdims=True) / WIDTH + EPS)
     parts = jnp.concatenate(split3(total) + (jnp.zeros((13, WIDTH), BF16),), axis=0)
     toward = lax.dot_general(parts, x_ref[...], NT, preferred_element_type=F32)
     toward = toward[0:1] + toward[1:2] + toward[2:3]
-    centre = toward * info_ref[0:1, :] * scale / WIDTH
-    for j in range(TILES):
-        copy(j).wait()
-        if j + 1 < TILES:
-            copy(j + 1).start()
-        for i in range(TILES):
-            dots = lax.dot_general(part(x_ref, i), part(sib_ref, j), NT, preferred_element_type=F32)
-            fold = fold_lanes(dots * lanes(sib_info_ref, 0, j) + lanes(sib_info_ref, 1, j))
-            fold = fold if j == 0 else jnp.maximum(part(fold_ref, i), fold)
-            if j + 1 < TILES:
-                fold_ref[i * TILE : (i + 1) * TILE, :] = fold
-            else:
-                best = to_row(jnp.max(fold, axis=1, keepdims=True))
-                best = jnp.maximum(best, lanes(best_ref, 0, i))
-                near_ref[:, i * TILE : (i + 1) * TILE] = jnp.maximum(
-                    -1.0, best * lanes(info_ref, 0, i) / WIDTH
-                )
+    centre_ref[...] = toward * info_ref[0:1, :] * scale / WIDTH
+    columns = [
+        (to_column(lanes(info_ref, 0, i)), to_column(lanes(info_ref, 1, i))) for i in range(TILES)
+    ]
+
+    def both(i, other, row, bias):
+        dots = lax.dot_general(part(x_ref, i), other, NT, preferred_element_type=F32)
+        down = jnp.max(dots * columns[i][0] + columns[i][1], axis=0, keepdims=True)
+        return fold_lanes(dots * row + bias), down
+
+    i, j = TILES - 2, TILES - 1
+    last, own = both(i, part(x_ref, j), lanes(info_ref, 0, j), lanes(info_ref, 1, j))
+    give = {}
+    for i in range(TILES):
+        if i == 0:
+            copy(0).wait()
+            copy(2).wait()
+            copy(1).start()
+            copy(3).start()
+        if i == 1:
+            copy(1).wait()
+            copy(3).wait()
+        fold = last if i == TILES - 2 else None
+        for k in (i, (i + 2) % TILES):
+            value, down = both(i, part(sib_ref, k), lanes(turned_ref, 0, k), lanes(turned_ref, 1, k))
+            fold = value if fold is None else jnp.maximum(fold, value)
+            give[k] = jnp.maximum(give[k], down) if k in give else down
+        best = jnp.maximum(
+            lanes(before_ref, 0, i), to_row(jnp.max(fold, axis=1, keepdims=True))
+        )
+        if i == TILES - 1:
+            best = jnp.maximum(best, own)
+        best_ref[:, i * TILE : (i + 1) * TILE] = best
+    for k in range(TILES):
+        give_ref[:, rows(k)] = give[k]
+
+
+def spread_kernel(place_ref, best_ref, taken_ref, info_ref, centre_ref, mean_ref, *out_refs):
+    best = jnp.maximum(best_ref[...], taken_ref[...])
+    near = jnp.maximum(-1.0, best * info_ref[0:1, :] / WIDTH)
+    mean = mean_ref[...]
     slot = lax.rem(iota((CAP, SLOTS), 1), CAP) == iota((CAP, SLOTS), 0)
-    near = jnp.where(slot, near_ref[...], 0.0)
-    centre = jnp.where(slot, centre, 0.0)
+    near = jnp.where(slot, near, 0.0)
+    centre = jnp.where(slot, centre_ref[...], 0.0)
     parts = jnp.concatenate(split3(jnp.concatenate([near, centre], axis=0)), axis=0)
     here = place_ref[0, 0]
     chip = iota((1, SLOTS), 1) // CAP
@@ -182,17 +214,17 @@
         out_refs[k][32:40, :] = folded
 
 
-def merge_kernel(place_ref, *refs):
-    came, (out_ref, mean_ref) = refs[:XS], refs[XS:]
-    out_ref[...] = sum(ref[0:32, :] for ref in came)
+def merge_kernel(*refs):
+    refs[XS][...] = sum(ref[0:32, :] for ref in refs[:XS])
+
+
+def unpack_kernel(place_ref, ids_ref, rank_ref, back_ref, *refs):
+    came, (near_ref, centre_ref, mean_ref) = refs[:XS], refs[XS:]
     for k in range(2):
         offset = (place_ref[0, 0] - 2 * place_ref[0, 1] - k) & 3
         folded = sum(jnp.where(offset == i, ref[32:40, :], 0.0) for i, ref in enumerate(came))
         for j in range(WIDTH // 128):
             mean_ref[k : k + 1, j * 128 : (j + 1) * 128] = folded[j : j + 1]
-
-
-def unpack_kernel(ids_ref, rank_ref, back_ref, near_ref, centre_ref):
     ids = ids_ref[...]
     same = iota((32, ROWS), 0) == ((ids >> 2) & 7) * 4 + (ids >> 5)
     onehot = same.astype(F32).astype(BF16)
@@ -249,31 +281,32 @@
     place = jnp.stack(axes).astype(jnp.int32).reshape(1, 2)
     scalars = pl.BlockSpec(memory_space=pltpu.SMEM)
     line = struct((40, 128), F32)
-    outs = call(
-        rest_kernel,
-        (line,) * XS,
-        block,
+    best, give, centre, mean = call(
+        across_kernel,
+        (row, row, row, struct((1, WIDTH), F32)),
+        block / 2,
         (
-            pltpu.VMEM((1, SLOTS), F32),
-            pltpu.VMEM((SLOTS, 128), F32),
             pltpu.VMEM((SLOTS, WIDTH), BF16),
+            pltpu.VMEM((2, SLOTS), F32),
             pltpu.SemaphoreType.DMA((TILES,)),
         ),
         in_specs=[scalars, here, pl.BlockSpec(memory_space=pltpu.HBM), here, here, here],
     )(place, mine, sib, info, sib_info, best)
+    taken = lax.ppermute(give, "core", swap)
+    outs = call(
+        spread_kernel, (line,) * XS, 1e8, in_specs=[scalars] + [here] * 5
+    )(place, best, taken, info, centre, mean)
     came = [outs[0]]
     for k in range(1, XS):
         came.append(lax.ppermute(outs[k], "x", [(i, (i + k) % XS) for i in range(XS)]))
-    out, means = call(
-        merge_kernel,
-        (struct((32, 128), F32), struct((2, WIDTH), F32)),
-        1e6,
-        in_specs=[scalars] + [here] * XS,
-    )(place, *came)
+    out = call(merge_kernel, struct((32, 128), F32), 1e6)(*came)
     back = lax.all_to_all(out, ("z", "y"), 0, 0, tiled=True)
-    near, centre = call(
-        unpack_kernel, (struct((1, ROWS), F32), struct((1, ROWS), F32)), 1e8
-    )(ids, rank, back)
+    near, centre, means = call(
+        unpack_kernel,
+        (struct((1, ROWS), F32), struct((1, ROWS), F32), struct((2, WIDTH), F32)),
+        1e8,
+        in_specs=[scalars] + [here] * (3 + XS),
+    )(place, ids, rank, back, *came)
     return near.reshape(ROWS), centre.reshape(ROWS), means
 
 

time: 137 us -> 136 us (level)
  Pallas kernels: 21.9 us -> 19.2 us
    pallas_call x3 -> x4, Pallas kernels: 11.9 us -> 9.76 us  [the longest x1 7.15 us: shards(): call(across_kernel, (row, row, row, struct((1, WIDTH), F32)), block / 2,...]
  transfers between devices with their start and end apart: 5 -> 6, of which waited for: 3 -> 4; matrix products, arithmetic and copies ran while one was open for 0% -> 0% of each run, Pallas kernels for 4% -> 4%
where the time goes in v8:
time: 136 us
  blocking collectives  104 us (76%)
  Pallas kernels  19.2 us (14%)
  waiting for transfers between devices  4.92 us (4%)
  starting transfers between devices  4.4 us (3%)
  local copies, waits for them, and re-layouts  2.09 us (2%)
    all_to_all x1, blocking collectives, shards(): lax.all_to_all(send.reshape(CHIPS, CAP, WIDTH), chips, 0, 0, tiled=True)  89.4 us
    all_to_all x1, blocking collectives, shards(): back = lax.all_to_all(out, ('z', 'y'), 0, 0, tiled=True)  14.7 us
    pallas_call x1, Pallas kernels, shards(): call(across_kernel, (row, row, row, struct((1, WIDTH), F32)), block / 2,...  7.15 us
    pallas_call x1, Pallas kernels, shards(): call(pack_kernel, (struct((SLOTS, WIDTH), BF16), struct((1, ROWS), jnp.in...  4.1 us
    ppermute x3, waiting for transfers between devices, shards(): lax.ppermute(outs[k], 'x', [(i, (i + k) % XS) for i in range(XS)])  3.76 us
    ppermute x3, starting transfers between devices, shards(): lax.ppermute(outs[k], 'x', [(i, (i + k) % XS) for i in range(XS)])  3.52 us
  transfers between devices with their start and end apart: 6, of which 4 were waited for; matrix products, arithmetic and copies ran while one was open for 0% of the time, Pallas kernels for 4%

profile of v8, /device:TPU:2, one launch (start us, length us, event | category | flops | bytes accessed | tf_op | source)
XLA Modules:
  0.0 135.5 jit_solution(10809532088374264249)
XLA Ops:
  0.6 0.0 copy-start
  0.6 1.4 %copy-done = bf16[1024,768]{1,0:T(8,128)(2,1)S(1)} copy-done((bf16[1024,768]{1,0:T(8,128)(2,1)S(1)}, bf16[1024,768]{1,0:T(8,128)(2,1)}, u32[]{:S(2)}) %copy-start) | copy-done | bytes 1572888
  2.0 0.0 copy-start.1
  2.0 0.7 copy-done.1
  2.7 4.1 %shard_map.49 = (bf16[2048,768]{1,0:T(8,128)(2,1)S(1)}, s32[1,1024]{1,0:T(1,128)S(1)}) custom-call(s32[1,1024]{1,0:T(1,128)S(1)} %bitcast.20, bf16[1024,768]{1,0:T(8,128)(2,1)S(1)} %copy-done), custom_call_target="tpu_custom_call" | custom-call | flops 3221225472 | bytes 6000000 | tf_op jit(solution)/shard_map/pallas_call | solution.py:263
  6.8 89.4 %all_to_all.16 = bf16[128,16,768]{2,1,0:T(8,128)(2,1)S(1)} all-to-all(bf16[128,16,768]{2,1,0:T(8,128)(2,1)S(1)} %bitcast.17), channel_id=1, replica_groups=mesh['y'=4,'z'=8,'core'=2,'x'=4] {'z','x','y'}, dimensions={0} | all-to-all | bytes 6291456 | tf_op jit(solution)/shard_map/all_to_all | solution.py:271
  96.2 0.0 collective-permute-start
  96.2 0.1 add_bitcast_fusion.place_ref
  96.3 2.7 %shard_map.50 = (f32[3,2048]{1,0:T(4,128)S(1)}, f32[1,2048]{1,0:T(1,128)S(1)}) custom-call(bf16[2048,768]{1,0:T(8,128)(2,1)S(1)} %bitcast.14), custom_call_target="tpu_custom_call" | custom-call | flops 1610612736 | bytes 6000000 | tf_op jit(solution)/shard_map/pallas_call | solution.py:276
  99.0 0.8 collective-permute-start.1
  99.8 2.6 %shard_map.51.before_ref = f32[1,2048]{1,0:T(1,128)S(1)} custom-call(bf16[2048,768]{1,0:T(8,128)(2,1)S(1)} %bitcast.15, f32[3,2048]{1,0:T(4,128)S(1)} %get-tuple-element.20.info_ref, f32[1,2048]{1,0:T(1,128)S(1)} %get-tuple-element.21.before_ref), custom_call_target="tpu_custom_call" | custom-call | flops 2415919104 | bytes 6000000 | tf_op jit(solution)/shard_map/pallas_call | solution.py:279
  102.4 0.0 copy-start.2
  102.4 0.0 collective-permute-done.1.sib_info_ref
  102.5 0.0 collective-permute-done.sib_hbm
  102.5 7.2 %shard_map.52 = (f32[1,2048]{1,0:T(1,128)S(1)}, f32[1,2048]{1,0:T(1,128)S(1)}, f32[1,2048]{1,0:T(1,128)S(1)}, f32[1,768]{1,0:T(1,128)S(1)}) custom-call(s32[1,2]{1,0:T(1,128)S(1)} %add_bitcast_fusion.place_ref, bf16[2048,768]{1,0:T(8,128)(2,1)S(1)} %bitcast.16, bf16[2048,768]{1,0:T(8,128)(2,1)} %collective-permute-done.sib_hbm, ...), custom_call_target="tpu_custom_call" | custom-call | flops 3221225472 | bytes 6000000 | tf_op jit(solution)/shard_map/pallas_call | solution.py:284
  109.6 0.1 collective-permute-start.2
  109.7 1.2 collective-permute-done.2.taken_ref
  110.9 1.0 shard_map.53
  111.9 1.2 collective-permute-start.3
  113.1 2.3 %collective-permute-start.4 = (f32[40,128]{1,0:T(8,128)S(1)}, f32[40,128]{1,0:T(8,128)S(1)}, u32[]{:S(2)}, u32[]{:S(2)}) collective-permute-start(f32[40,128]{1,0:T(8,128)S(1)} %get-tuple-element.28), channel_id=1, source_target_pairs={{0,2},{1,3},{2,0},{3,1},{4,6},{5,7},{6,4},{7,5},{8,10},{9,11},{10,... | collective-permute-start | bytes 61448 | tf_op jit(solution)/shard_map/ppermute | solution.py:301
  115.4 0.0 collective-permute-start.5
  115.4 0.3 collective-permute-done.3.refs_1_
  115.8 2.6 %collective-permute-done.4.refs_2_ = f32[40,128]{1,0:T(8,128)S(1)} collective-permute-done((f32[40,128]{1,0:T(8,128)S(1)}, f32[40,128]{1,0:T(8,128)S(1)}, u32[]{:S(2)}, u32[]{:S(2)}) %collective-permute-start.4) | collective-permute-done | bytes 20512 | tf_op jit(solution)/shard_map/ppermute | solution.py:301
  118.4 0.8 collective-permute-done.5.refs_3_
  119.2 14.7 %all_to_all.17 = f32[32,1,128]{2,1,0:T(1,128)S(1)} all-to-all(f32[32,1,128]{2,1,0:T(1,128)S(1)} %bitcast.18), channel_id=1, replica_groups=mesh['y'=4,'z'=8,'core'=2,'x'=4] {'z','y'}, dimensions={0} | all-to-all | bytes 32768 | tf_op jit(solution)/shard_map/all_to_all | solution.py:303
  133.9 0.0 copy-done.2
  133.9 1.6 %shard_map.55 = (f32[1,1024]{1,0:T(1,128)}, f32[1,1024]{1,0:T(1,128)}, f32[2,768]{1,0:T(2,128)}) custom-call(s32[1,2]{1,0:T(1,128)S(1)} %add_bitcast_fusion.place_ref, s32[1,1024]{1,0:T(1,128)S(1)} %bitcast.21, s32[1,1024]{1,0:T(1,128)S(1)} %get-tuple-element.18.rank_ref, f32[32,128]{1,0:T(8,128)S(1)} %bitcast.19, f32[40,128]{1,0:T(8,128)S(1)} %get-tuple-element.26.refs_0_, ...), custom_call_target="tpu_custom_call" | custom-call | flops 100000000 | bytes 6000000 | tf_op jit(solution)/shard_map/pallas_call | solution.py:304
  (1 shorter events, 0.0 us)
Async XLA Ops:
  0.6 1.4 %copy-start = (bf16[1024,768]{1,0:T(8,128)(2,1)S(1)}, bf16[1024,768]{1,0:T(8,128)(2,1)}, u32[]{:S(2)}) copy-start(bf16[1024,768]{1,0:T(8,128)(2,1)} %x_hbm.1) | copy-start | bytes 4718596
  2.0 0.7 copy-start.1
  96.2 6.2 %collective-permute-start = (bf16[2048,768]{1,0:T(8,128)(2,1)S(1)}, bf16[2048,768]{1,0:T(8,128)(2,1)}, u32[]{:S(2)}, u32[]{:S(2)}) collective-permute-start(bf16[2048,768]{1,0:T(8,128)(2,1)S(1)} %bitcast.13), channel_id=1, source_target_pairs={{0,4},{4,0},{1,5},{5,1},{2,6},{6,2},{3,7},{7,3},{8,12},{12,8},{9,1... | collective-permute-start | bytes 9437192 | tf_op jit(solution)/shard_map/ppermute | solution.py:274
  99.0 3.4 %collective-permute-start.1 = (f32[3,2048]{1,0:T(4,128)S(1)}, f32[3,2048]{1,0:T(4,128)S(1)}, u32[]{:S(2)}, u32[]{:S(2)}) collective-permute-start(f32[3,2048]{1,0:T(4,128)S(1)} %get-tuple-element.20.info_ref), channel_id=1, source_target_pairs={{0,4},{4,0},{1,5},{5,1},{2,6},{6,2},{3,7},{7,3},{8,12},{12,8},{9,1... | collective-permute-start | bytes 73736 | tf_op jit(solution)/shard_map/ppermute | solution.py:277
  102.4 31.5 %copy-start.2 = (s32[1024,1]{0,1:T(1,128)S(1)}, s32[1024,1]{0,1:T(1,128)}, u32[]{:S(2)}) copy-start(s32[1024,1]{0,1:T(1,128)} %param.3) | copy-start | bytes 12292
  109.6 1.3 collective-permute-start.2
  111.9 3.9 %collective-permute-start.3 = (f32[40,128]{1,0:T(8,128)S(1)}, f32[40,128]{1,0:T(8,128)S(1)}, u32[]{:S(2)}, u32[]{:S(2)}) collective-permute-start(f32[40,128]{1,0:T(8,128)S(1)} %get-tuple-element.27), channel_id=1, source_target_pairs={{0,1},{1,2},{2,3},{3,0},{4,5},{5,6},{6,7},{7,4},{8,9},{9,10},{10,1... | collective-permute-start | bytes 61448 | tf_op jit(solution)/shard_map/ppermute | solution.py:301
  113.1 5.3 %collective-permute-start.4 = (f32[40,128]{1,0:T(8,128)S(1)}, f32[40,128]{1,0:T(8,128)S(1)}, u32[]{:S(2)}, u32[]{:S(2)}) collective-permute-start(f32[40,128]{1,0:T(8,128)S(1)} %get-tuple-element.28), channel_id=1, source_target_pairs={{0,2},{1,3},{2,0},{3,1},{4,6},{5,7},{6,4},{7,5},{8,10},{9,11},{10,... | collective-permute-start | bytes 61448 | tf_op jit(solution)/shard_map/ppermute | solution.py:301
  115.4 3.8 %collective-permute-start.5 = (f32[40,128]{1,0:T(8,128)S(1)}, f32[40,128]{1,0:T(8,128)S(1)}, u32[]{:S(2)}, u32[]{:S(2)}) collective-permute-start(f32[40,128]{1,0:T(8,128)S(1)} %get-tuple-element.29), channel_id=1, source_target_pairs={{0,3},{1,0},{2,1},{3,2},{4,7},{5,4},{6,5},{7,6},{8,11},{9,8},{10,9... | collective-permute-start | bytes 61448 | tf_op jit(solution)/shard_map/ppermute | solution.py:301

commit v9 on v8

--- a/solution.py
+++ b/solution.py
@@ -119,7 +119,7 @@
     for i in range(TILES - 2):
         inv = to_column(lanes(info_ref, 0, i))
         bias = to_column(lanes(info_ref, 1, i))
-        for j in range(i + 1, TILES):
+        for j in range(i + 1, TILES - i):
             dots = lax.dot_general(part(x_ref, i), part(x_ref, j), NT, preferred_element_type=F32)
             fold = fold_lanes(dots * lanes(info_ref, 0, j) + lanes(info_ref, 1, j))
             fold_ref[...] = fold if j == i + 1 else jnp.maximum(fold_ref[...], fold)
@@ -131,7 +131,7 @@
 
 def across_kernel(
     place_ref, x_ref, sib_hbm, info_ref, sib_info_ref, before_ref,
-    best_ref, give_ref, centre_ref, mean_ref, sib_ref, turned_ref, sems,
+    best_ref, give_ref, sib_ref, turned_ref, sems,
 ):
     core = place_ref[0, 1]
 
@@ -147,14 +147,6 @@
     copy(2).start()
     for k in range(TILES):
         turned_ref[:, k * TILE : (k + 1) * TILE] = sib_info_ref[0:2, rows(k)]
-    total = info_ref[2:3, 0:WIDTH] + sib_info_ref[2:3, 0:WIDTH]
-    count = info_ref[2:3, WIDTH : WIDTH + 1] + sib_info_ref[2:3, WIDTH : WIDTH + 1]
-    mean_ref[...] = total / count
-    scale = lax.rsqrt(jnp.sum(total * total, axis=1, keepdims=True) / WIDTH + EPS)
-    parts = jnp.concatenate(split3(total) + (jnp.zeros((13, WIDTH), BF16),), axis=0)
-    toward = lax.dot_general(parts, x_ref[...], NT, preferred_element_type=F32)
-    toward = toward[0:1] + toward[1:2] + toward[2:3]
-    centre_ref[...] = toward * info_ref[0:1, :] * scale / WIDTH
     columns = [
         (to_column(lanes(info_ref, 0, i)), to_column(lanes(info_ref, 1, i))) for i in range(TILES)
     ]
@@ -164,8 +156,12 @@
         down = jnp.max(dots * columns[i][0] + columns[i][1], axis=0, keepdims=True)
         return fold_lanes(dots * row + bias), down
 
-    i, j = TILES - 2, TILES - 1
-    last, own = both(i, part(x_ref, j), lanes(info_ref, 0, j), lanes(info_ref, 1, j))
+    def own(i):
+        j = TILES - 1
+        return both(i, part(x_ref, j), lanes(info_ref, 0, j), lanes(info_ref, 1, j))
+
+    folds, downs = {}, {}
+    folds[2], downs[2] = own(2)
     give = {}
     for i in range(TILES):
         if i == 0:
@@ -173,10 +169,11 @@
             copy(2).wait()
             copy(1).start()
             copy(3).start()
+            folds[1], downs[1] = own(1)
         if i == 1:
             copy(1).wait()
             copy(3).wait()
-        fold = last if i == TILES - 2 else None
+        fold = folds.get(i)
         for k in (i, (i + 2) % TILES):
             value, down = both(i, part(sib_ref, k), lanes(turned_ref, 0, k), lanes(turned_ref, 1, k))
             fold = value if fold is None else jnp.maximum(fold, value)
@@ -185,33 +182,49 @@
             lanes(before_ref, 0, i), to_row(jnp.max(fold, axis=1, keepdims=True))
         )
         if i == TILES - 1:
-            best = jnp.maximum(best, own)
+            best = jnp.maximum(best, jnp.maximum(downs[1], downs[2]))
         best_ref[:, i * TILE : (i + 1) * TILE] = best
     for k in range(TILES):
         give_ref[:, rows(k)] = give[k]
 
 
-def spread_kernel(place_ref, best_ref, taken_ref, info_ref, centre_ref, mean_ref, *out_refs):
+def spread(source, row):
+    slot = lax.rem(iota((CAP, SLOTS), 1), CAP) == iota((CAP, SLOTS), 0)
+    parts = jnp.concatenate(split3(jnp.where(slot, row, 0.0)), axis=0)
+    lines = lax.dot_general(source, parts, NT, preferred_element_type=F32)
+    return lines[:, 0:CAP] + lines[:, CAP : 2 * CAP] + lines[:, 2 * CAP : 3 * CAP]
+
+
+def centre_kernel(
+    place_ref, after_ref, x_ref, info_ref, sib_info_ref, source_ref, centre_ref, mean_ref
+):
+    total = info_ref[2:3, 0:WIDTH] + sib_info_ref[2:3, 0:WIDTH]
+    count = info_ref[2:3, WIDTH : WIDTH + 1] + sib_info_ref[2:3, WIDTH : WIDTH + 1]
+    mean = total / count
+    folded = [mean[:, k : k + 128] for k in range(0, WIDTH, 128)]
+    mean_ref[...] = jnp.concatenate(folded + [jnp.zeros((2, 128), F32)], axis=0)
+    scale = lax.rsqrt(jnp.sum(total * total, axis=1, keepdims=True) / WIDTH + EPS)
+    parts = jnp.concatenate(split3(total) + (jnp.zeros((13, WIDTH), BF16),), axis=0)
+    toward = lax.dot_general(parts, x_ref[...], NT, preferred_element_type=F32)
+    toward = toward[0:1] + toward[1:2] + toward[2:3]
+    centre = toward * info_ref[0:1, :] * scale / WIDTH
+    chip = iota((1, SLOTS), 1) // CAP
+    line = (((chip >> 2) - place_ref[0, 0]) & 3) * 32 + (chip >> 4) * 4 + (chip & 3)
+    source = (line == iota((CHIPS, SLOTS), 0)).astype(F32).astype(BF16)
+    source_ref[...] = source
+    centre_ref[...] = spread(source, centre)
+
+
+def spread_kernel(
+    place_ref, best_ref, taken_ref, info_ref, source_ref, centre_ref, mean_ref, *out_refs
+):
     best = jnp.maximum(best_ref[...], taken_ref[...])
     near = jnp.maximum(-1.0, best * info_ref[0:1, :] / WIDTH)
-    mean = mean_ref[...]
-    slot = lax.rem(iota((CAP, SLOTS), 1), CAP) == iota((CAP, SLOTS), 0)
-    near = jnp.where(slot, near, 0.0)
-    centre = jnp.where(slot, centre_ref[...], 0.0)
-    parts = jnp.concatenate(split3(jnp.concatenate([near, centre], axis=0)), axis=0)
-    here = place_ref[0, 0]
-    chip = iota((1, SLOTS), 1) // CAP
-    row = (((chip >> 2) - here) & 3) * 32 + (chip >> 4) * 4 + (chip & 3)
-    source = (row == iota((CHIPS, SLOTS), 0)).astype(F32).astype(BF16)
-    spread = lax.dot_general(source, parts, NT, preferred_element_type=F32)
-    spread = spread[:, 0:PAIR] + spread[:, PAIR : 2 * PAIR] + spread[:, 2 * PAIR : 3 * PAIR]
-    spread = jnp.concatenate([spread] * XS, axis=1)
-    spread = jnp.where(iota((CHIPS, XS * PAIR), 1) // PAIR == here, spread, 0.0)
-    folded = [mean[:, k : k + 128] for k in range(0, WIDTH, 128)]
-    folded = jnp.concatenate(folded + [jnp.zeros((2, 128), F32)], axis=0)
+    lines = jnp.concatenate([spread(source_ref[...], near), centre_ref[...]] * XS, axis=1)
+    lines = jnp.where(iota((CHIPS, XS * PAIR), 1) // PAIR == place_ref[0, 0], lines, 0.0)
     for k in range(XS):
-        out_refs[k][0:32, :] = spread[32 * k : 32 * (k + 1)]
-        out_refs[k][32:40, :] = folded
+        out_refs[k][0:32, :] = lines[32 * k : 32 * (k + 1)]
+        out_refs[k][32:40, :] = mean_ref[...]
 
 
 def merge_kernel(*refs):
@@ -281,9 +294,9 @@
     place = jnp.stack(axes).astype(jnp.int32).reshape(1, 2)
     scalars = pl.BlockSpec(memory_space=pltpu.SMEM)
     line = struct((40, 128), F32)
-    best, give, centre, mean = call(
+    best, give = call(
         across_kernel,
-        (row, row, row, struct((1, WIDTH), F32)),
+        (row, row),
         block / 2,
         (
             pltpu.VMEM((SLOTS, WIDTH), BF16),
@@ -293,9 +306,15 @@
         in_specs=[scalars, here, pl.BlockSpec(memory_space=pltpu.HBM), here, here, here],
     )(place, mine, sib, info, sib_info, best)
     taken = lax.ppermute(give, "core", swap)
+    source, centre, mean = call(
+        centre_kernel,
+        (struct((CHIPS, SLOTS), BF16), struct((CHIPS, CAP), F32), struct((8, 128), F32)),
+        block / 8,
+        in_specs=[scalars] + [here] * 4,
+    )(place, give, mine, info, sib_info)
     outs = call(
-        spread_kernel, (line,) * XS, 1e8, in_specs=[scalars] + [here] * 5
-    )(place, best, taken, info, centre, mean)
+        spread_kernel, (line,) * XS, 1e8, in_specs=[scalars] + [here] * 6
+    )(place, best, taken, info, source, centre, mean)
     came = [outs[0]]
     for k in range(1, XS):
         came.append(lax.ppermute(outs[k], "x", [(i, (i + k) % XS) for i in range(XS)]))

time: 136 us -> 136 us (level)
    pallas_call x1 -> x2, Pallas kernels: 7.15 us -> 8.53 us  [the longest x1 6.68 us: shards(): call(across_kernel, (row, row), block / 2, (pltpu.VMEM((SLOTS, WIDTH), BF...]
  transfers between devices with their start and end apart: 6 -> 6, of which waited for: 4 -> 3; matrix products, arithmetic and copies ran while one was open for 0% -> 0% of each run, Pallas kernels for 4% -> 5%
where the time goes in v9:
time: 136 us; the launch traced here: 135 us
  blocking collectives  104 us (76%)
  Pallas kernels  20.1 us (15%)
  starting transfers between devices  4.54 us (3%)
  waiting for transfers between devices  3.78 us (3%)
  local copies, waits for them, and re-layouts  2.09 us (2%)
    all_to_all x1, blocking collectives, shards(): lax.all_to_all(send.reshape(CHIPS, CAP, WIDTH), chips, 0, 0, tiled=True)  89.4 us
    all_to_all x1, blocking collectives, shards(): back = lax.all_to_all(out, ('z', 'y'), 0, 0, tiled=True)  14.7 us
    pallas_call x1, Pallas kernels, shards(): call(across_kernel, (row, row), block / 2, (pltpu.VMEM((SLOTS, WIDTH), BF...  6.68 us
    pallas_call x1, Pallas kernels, shards(): call(pack_kernel, (struct((SLOTS, WIDTH), BF16), struct((1, ROWS), jnp.in...  4.1 us
    ppermute x3, waiting for transfers between devices, shards(): lax.ppermute(outs[k], 'x', [(i, (i + k) % XS) for i in range(XS)])  3.76 us
    ppermute x3, starting transfers between devices, shards(): lax.ppermute(outs[k], 'x', [(i, (i + k) % XS) for i in range(XS)])  3.54 us
  transfers between devices with their start and end apart: 6, of which 3 were waited for; matrix products, arithmetic and copies ran while one was open for 0% of the time, Pallas kernels for 5%

profile of v9, /device:TPU:2, one launch (start us, length us, event | category | flops | bytes accessed | tf_op | source)
XLA Modules:
  0.0 135.5 jit_solution(4173115863406393734)
XLA Ops:
  0.6 0.0 copy-start
  0.6 1.4 %copy-done = bf16[1024,768]{1,0:T(8,128)(2,1)S(1)} copy-done((bf16[1024,768]{1,0:T(8,128)(2,1)S(1)}, bf16[1024,768]{1,0:T(8,128)(2,1)}, u32[]{:S(2)}) %copy-start) | copy-done | bytes 1572888
  2.0 0.0 copy-start.1
  2.0 0.7 copy-done.1
  2.7 4.1 %shard_map.49 = (bf16[2048,768]{1,0:T(8,128)(2,1)S(1)}, s32[1,1024]{1,0:T(1,128)S(1)}) custom-call(s32[1,1024]{1,0:T(1,128)S(1)} %bitcast.21, bf16[1024,768]{1,0:T(8,128)(2,1)S(1)} %copy-done), custom_call_target="tpu_custom_call" | custom-call | flops 3221225472 | bytes 6000000 | tf_op jit(solution)/shard_map/pallas_call | solution.py:276
  6.8 89.4 %all_to_all.16 = bf16[128,16,768]{2,1,0:T(8,128)(2,1)S(1)} all-to-all(bf16[128,16,768]{2,1,0:T(8,128)(2,1)S(1)} %bitcast.18), channel_id=1, replica_groups=mesh['y'=4,'z'=8,'core'=2,'x'=4] {'z','x','y'}, dimensions={0} | all-to-all | bytes 6291456 | tf_op jit(solution)/shard_map/all_to_all | solution.py:284
  96.2 0.0 collective-permute-start
  96.2 0.1 add_bitcast_fusion.place_ref
  96.3 2.7 %shard_map.50 = (f32[3,2048]{1,0:T(4,128)S(1)}, f32[1,2048]{1,0:T(1,128)S(1)}) custom-call(bf16[2048,768]{1,0:T(8,128)(2,1)S(1)} %bitcast.14), custom_call_target="tpu_custom_call" | custom-call | flops 1610612736 | bytes 6000000 | tf_op jit(solution)/shard_map/pallas_call | solution.py:289
  99.0 0.8 collective-permute-start.1
  99.8 2.2 %shard_map.51.before_ref = f32[1,2048]{1,0:T(1,128)S(1)} custom-call(bf16[2048,768]{1,0:T(8,128)(2,1)S(1)} %bitcast.15, f32[3,2048]{1,0:T(4,128)S(1)} %get-tuple-element.21.info_ref, f32[1,2048]{1,0:T(1,128)S(1)} %get-tuple-element.22.before_ref), custom_call_target="tpu_custom_call" | custom-call | flops 2415919104 | bytes 6000000 | tf_op jit(solution)/shard_map/pallas_call | solution.py:292
  102.0 0.0 collective-permute-done.1.sib_info_ref
  102.0 0.0 collective-permute-done.sib_hbm
  102.0 6.7 %shard_map.52 = (f32[1,2048]{1,0:T(1,128)S(1)}, f32[1,2048]{1,0:T(1,128)S(1)}) custom-call(s32[1,2]{1,0:T(1,128)S(1)} %add_bitcast_fusion.place_ref, bf16[2048,768]{1,0:T(8,128)(2,1)S(1)} %bitcast.16, bf16[2048,768]{1,0:T(8,128)(2,1)} %collective-permute-done.sib_hbm, f32[3,2048]{1,0:T(4,128)S(1)} %get-tuple-element.21.info_ref, ...), custom_call_target="tpu_custom_call" | custom-call | flops 3221225472 | bytes 6000000 | tf_op jit(solution)/shard_map/pallas_call | solution.py:297
  108.7 0.0 copy-start.2
  108.7 0.2 collective-permute-start.2
  109.0 1.9 %shard_map.53 = (bf16[128,2048]{1,0:T(8,128)(2,1)S(1)}, f32[128,16]{1,0:T(8,128)S(1)}, f32[8,128]{1,0:T(8,128)S(1)}) custom-call(s32[1,2]{1,0:T(1,128)S(1)} %add_bitcast_fusion.place_ref, f32[1,2048]{1,0:T(1,128)S(1)} %get-tuple-element.24.after_ref, bf16[2048,768]{1,0:T(8,128)(2,1)S(1)} %bitcast.17, f32[3,2048]{1,0:T(4,128)S(1)} %get-tuple-element.21.info_ref, ...), custom_call_target="tpu_custom_call" | custom-call | flops 805306368 | bytes 6000000 | tf_op jit(solution)/shard_map/pallas_call | solution.py:309
  110.8 0.0 collective-permute-done.2.taken_ref
  110.8 1.0 shard_map.54
  111.8 1.2 collective-permute-start.3
  113.0 2.3 %collective-permute-start.4 = (f32[40,128]{1,0:T(8,128)S(1)}, f32[40,128]{1,0:T(8,128)S(1)}, u32[]{:S(2)}, u32[]{:S(2)}) collective-permute-start(f32[40,128]{1,0:T(8,128)S(1)} %get-tuple-element.30), channel_id=1, source_target_pairs={{0,2},{1,3},{2,0},{3,1},{4,6},{5,7},{6,4},{7,5},{8,10},{9,11},{10,... | collective-permute-start | bytes 61448 | tf_op jit(solution)/shard_map/ppermute | solution.py:320
  115.3 0.0 collective-permute-start.5
  115.4 0.3 collective-permute-done.3.refs_1_
  115.7 2.6 %collective-permute-done.4.refs_2_ = f32[40,128]{1,0:T(8,128)S(1)} collective-permute-done((f32[40,128]{1,0:T(8,128)S(1)}, f32[40,128]{1,0:T(8,128)S(1)}, u32[]{:S(2)}, u32[]{:S(2)}) %collective-permute-start.4) | collective-permute-done | bytes 20512 | tf_op jit(solution)/shard_map/ppermute | solution.py:320
  118.3 0.8 collective-permute-done.5.refs_3_
  119.1 14.7 %all_to_all.17 = f32[32,1,128]{2,1,0:T(1,128)S(1)} all-to-all(f32[32,1,128]{2,1,0:T(1,128)S(1)} %bitcast.19), channel_id=1, replica_groups=mesh['y'=4,'z'=8,'core'=2,'x'=4] {'z','y'}, dimensions={0} | all-to-all | bytes 32768 | tf_op jit(solution)/shard_map/all_to_all | solution.py:322
  133.9 0.0 copy-done.2
  133.9 1.6 %shard_map.56 = (f32[1,1024]{1,0:T(1,128)}, f32[1,1024]{1,0:T(1,128)}, f32[2,768]{1,0:T(2,128)}) custom-call(s32[1,2]{1,0:T(1,128)S(1)} %add_bitcast_fusion.place_ref, s32[1,1024]{1,0:T(1,128)S(1)} %bitcast.22, s32[1,1024]{1,0:T(1,128)S(1)} %get-tuple-element.19.rank_ref, f32[32,128]{1,0:T(8,128)S(1)} %bitcast.20, f32[40,128]{1,0:T(8,128)S(1)} %get-tuple-element.28.refs_0_, ...), custom_call_target="tpu_custom_call" | custom-call | flops 100000000 | bytes 6000000 | tf_op jit(solution)/shard_map/pallas_call | solution.py:323
  (1 shorter events, 0.0 us)
Async XLA Ops:
  0.6 1.4 %copy-start = (bf16[1024,768]{1,0:T(8,128)(2,1)S(1)}, bf16[1024,768]{1,0:T(8,128)(2,1)}, u32[]{:S(2)}) copy-start(bf16[1024,768]{1,0:T(8,128)(2,1)} %x_hbm.1) | copy-start | bytes 4718596
  2.0 0.7 copy-start.1
  96.2 5.8 %collective-permute-start = (bf16[2048,768]{1,0:T(8,128)(2,1)S(1)}, bf16[2048,768]{1,0:T(8,128)(2,1)}, u32[]{:S(2)}, u32[]{:S(2)}) collective-permute-start(bf16[2048,768]{1,0:T(8,128)(2,1)S(1)} %bitcast.13), channel_id=1, source_target_pairs={{0,4},{4,0},{1,5},{5,1},{2,6},{6,2},{3,7},{7,3},{8,12},{12,8},{9,1... | collective-permute-start | bytes 9437192 | tf_op jit(solution)/shard_map/ppermute | solution.py:287
  99.0 3.0 %collective-permute-start.1 = (f32[3,2048]{1,0:T(4,128)S(1)}, f32[3,2048]{1,0:T(4,128)S(1)}, u32[]{:S(2)}, u32[]{:S(2)}) collective-permute-start(f32[3,2048]{1,0:T(4,128)S(1)} %get-tuple-element.21.info_ref), channel_id=1, source_target_pairs={{0,4},{4,0},{1,5},{5,1},{2,6},{6,2},{3,7},{7,3},{8,12},{12,8},{9,1... | collective-permute-start | bytes 73736 | tf_op jit(solution)/shard_map/ppermute | solution.py:290
  108.7 25.1 %copy-start.2 = (s32[1024,1]{0,1:T(1,128)S(1)}, s32[1024,1]{0,1:T(1,128)}, u32[]{:S(2)}) copy-start(s32[1024,1]{0,1:T(1,128)} %param.3) | copy-start | bytes 12292
  108.7 2.1 %collective-permute-start.2 = (f32[1,2048]{1,0:T(1,128)S(1)}, f32[1,2048]{1,0:T(1,128)S(1)}, u32[]{:S(2)}, u32[]{:S(2)}) collective-permute-start(f32[1,2048]{1,0:T(1,128)S(1)} %get-tuple-element.24.after_ref), channel_id=1, source_target_pairs={{0,4},{4,0},{1,5},{5,1},{2,6},{6,2},{3,7},{7,3},{8,12},{12,8},{9,1... | collective-permute-start | bytes 24584 | tf_op jit(solution)/shard_map/ppermute | solution.py:308
  111.8 3.9 %collective-permute-start.3 = (f32[40,128]{1,0:T(8,128)S(1)}, f32[40,128]{1,0:T(8,128)S(1)}, u32[]{:S(2)}, u32[]{:S(2)}) collective-permute-start(f32[40,128]{1,0:T(8,128)S(1)} %get-tuple-element.29), channel_id=1, source_target_pairs={{0,1},{1,2},{2,3},{3,0},{4,5},{5,6},{6,7},{7,4},{8,9},{9,10},{10,1... | collective-permute-start | bytes 61448 | tf_op jit(solution)/shard_map/ppermute | solution.py:320
  113.0 5.3 %collective-permute-start.4 = (f32[40,128]{1,0:T(8,128)S(1)}, f32[40,128]{1,0:T(8,128)S(1)}, u32[]{:S(2)}, u32[]{:S(2)}) collective-permute-start(f32[40,128]{1,0:T(8,128)S(1)} %get-tuple-element.30), channel_id=1, source_target_pairs={{0,2},{1,3},{2,0},{3,1},{4,6},{5,7},{6,4},{7,5},{8,10},{9,11},{10,... | collective-permute-start | bytes 61448 | tf_op jit(solution)/shard_map/ppermute | solution.py:320
  115.3 3.8 %collective-permute-start.5 = (f32[40,128]{1,0:T(8,128)S(1)}, f32[40,128]{1,0:T(8,128)S(1)}, u32[]{:S(2)}, u32[]{:S(2)}) collective-permute-start(f32[40,128]{1,0:T(8,128)S(1)} %get-tuple-element.31), channel_id=1, source_target_pairs={{0,3},{1,0},{2,1},{3,2},{4,7},{5,4},{6,5},{7,6},{8,11},{9,8},{10,9... | collective-permute-start | bytes 61448 | tf_op jit(solution)/shard_map/ppermute | solution.py:320

commit v10 on v9

--- a/solution.py
+++ b/solution.py
@@ -12,6 +12,7 @@
 CHIPS = 128
 XS = 4
 PAIR = 2 * CAP
+OFFSETS = (2, 1, 3, 0)
 SLOTS = CHIPS * CAP
 MARK = 64.0
 LOW = -1e30
@@ -131,7 +132,7 @@
 
 def across_kernel(
     place_ref, x_ref, sib_hbm, info_ref, sib_info_ref, before_ref,
-    best_ref, give_ref, sib_ref, turned_ref, sems,
+    best_ref, give_ref, centre_ref, mean_ref, sib_ref, turned_ref, sems,
 ):
     core = place_ref[0, 1]
 
@@ -147,6 +148,16 @@
     copy(2).start()
     for k in range(TILES):
         turned_ref[:, k * TILE : (k + 1) * TILE] = sib_info_ref[0:2, rows(k)]
+    total = info_ref[2:3, 0:WIDTH] + sib_info_ref[2:3, 0:WIDTH]
+    count = info_ref[2:3, WIDTH : WIDTH + 1] + sib_info_ref[2:3, WIDTH : WIDTH + 1]
+    mean = total / count
+    folded = [mean[:, k : k + 128] for k in range(0, WIDTH, 128)]
+    mean_ref[...] = jnp.concatenate(folded + [jnp.zeros((2, 128), F32)], axis=0)
+    scale = lax.rsqrt(jnp.sum(total * total, axis=1, keepdims=True) / WIDTH + EPS)
+    parts = jnp.concatenate(split3(total) + (jnp.zeros((13, WIDTH), BF16),), axis=0)
+    toward = lax.dot_general(parts, x_ref[...], NT, preferred_element_type=F32)
+    toward = toward[0:1] + toward[1:2] + toward[2:3]
+    centre_ref[...] = toward * info_ref[0:1, :] * scale / WIDTH
     columns = [
         (to_column(lanes(info_ref, 0, i)), to_column(lanes(info_ref, 1, i))) for i in range(TILES)
     ]
@@ -195,24 +206,12 @@
     return lines[:, 0:CAP] + lines[:, CAP : 2 * CAP] + lines[:, 2 * CAP : 3 * CAP]
 
 
-def centre_kernel(
-    place_ref, after_ref, x_ref, info_ref, sib_info_ref, source_ref, centre_ref, mean_ref
-):
-    total = info_ref[2:3, 0:WIDTH] + sib_info_ref[2:3, 0:WIDTH]
-    count = info_ref[2:3, WIDTH : WIDTH + 1] + sib_info_ref[2:3, WIDTH : WIDTH + 1]
-    mean = total / count
-    folded = [mean[:, k : k + 128] for k in range(0, WIDTH, 128)]
-    mean_ref[...] = jnp.concatenate(folded + [jnp.zeros((2, 128), F32)], axis=0)
-    scale = lax.rsqrt(jnp.sum(total * total, axis=1, keepdims=True) / WIDTH + EPS)
-    parts = jnp.concatenate(split3(total) + (jnp.zeros((13, WIDTH), BF16),), axis=0)
-    toward = lax.dot_general(parts, x_ref[...], NT, preferred_element_type=F32)
-    toward = toward[0:1] + toward[1:2] + toward[2:3]
-    centre = toward * info_ref[0:1, :] * scale / WIDTH
+def centre_kernel(place_ref, after_ref, centre_ref, source_ref, out_ref):
     chip = iota((1, SLOTS), 1) // CAP
     line = (((chip >> 2) - place_ref[0, 0]) & 3) * 32 + (chip >> 4) * 4 + (chip & 3)
     source = (line == iota((CHIPS, SLOTS), 0)).astype(F32).astype(BF16)
     source_ref[...] = source
-    centre_ref[...] = spread(source, centre)
+    out_ref[...] = spread(source, centre_ref[...])
 
 
 def spread_kernel(
@@ -235,7 +234,7 @@
     came, (near_ref, centre_ref, mean_ref) = refs[:XS], refs[XS:]
     for k in range(2):
         offset = (place_ref[0, 0] - 2 * place_ref[0, 1] - k) & 3
-        folded = sum(jnp.where(offset == i, ref[32:40, :], 0.0) for i, ref in enumerate(came))
+        folded = sum(jnp.where(offset == i, ref[32:40, :], 0.0) for i, ref in zip(OFFSETS, came))
         for j in range(WIDTH // 128):
             mean_ref[k : k + 1, j * 128 : (j + 1) * 128] = folded[j : j + 1]
     ids = ids_ref[...]
@@ -294,9 +293,9 @@
     place = jnp.stack(axes).astype(jnp.int32).reshape(1, 2)
     scalars = pl.BlockSpec(memory_space=pltpu.SMEM)
     line = struct((40, 128), F32)
-    best, give = call(
+    best, give, centre, mean = call(
         across_kernel,
-        (row, row),
+        (row, row, row, struct((8, 128), F32)),
         block / 2,
         (
             pltpu.VMEM((SLOTS, WIDTH), BF16),
@@ -306,18 +305,19 @@
         in_specs=[scalars, here, pl.BlockSpec(memory_space=pltpu.HBM), here, here, here],
     )(place, mine, sib, info, sib_info, best)
     taken = lax.ppermute(give, "core", swap)
-    source, centre, mean = call(
+    source, centre = call(
         centre_kernel,
-        (struct((CHIPS, SLOTS), BF16), struct((CHIPS, CAP), F32), struct((8, 128), F32)),
+        (struct((CHIPS, SLOTS), BF16), struct((CHIPS, CAP), F32)),
         block / 8,
-        in_specs=[scalars] + [here] * 4,
-    )(place, give, mine, info, sib_info)
+        in_specs=[scalars, here, here],
+    )(place, give, centre)
     outs = call(
         spread_kernel, (line,) * XS, 1e8, in_specs=[scalars] + [here] * 6
     )(place, best, taken, info, source, centre, mean)
-    came = [outs[0]]
-    for k in range(1, XS):
-        came.append(lax.ppermute(outs[k], "x", [(i, (i + k) % XS) for i in range(XS)]))
+    came = [
+        lax.ppermute(outs[k], "x", [(i, (i + k) % XS) for i in range(XS)]) if k else outs[k]
+        for k in OFFSETS
+    ]
     out = call(merge_kernel, struct((32, 128), F32), 1e6)(*came)
     back = lax.all_to_all(out, ("z", "y"), 0, 0, tiled=True)
     near, centre, means = call(

time: 136 us -> 135 us (level)
  transfers between devices with their start and end apart: 6 -> 6, of which waited for: 3 -> 4; matrix products, arithmetic and copies ran while one was open for 0% -> 0% of each run, Pallas kernels for 5% -> 4%
where the time goes in v10:
time: 135 us
  blocking collectives  104 us (77%)
  Pallas kernels  20.2 us (15%)
  starting transfers between devices  4.27 us (3%)
  waiting for transfers between devices  3.58 us (3%)
  local copies, waits for them, and re-layouts  2.09 us (2%)
    all_to_all x1, blocking collectives, shards(): lax.all_to_all(send.reshape(CHIPS, CAP, WIDTH), chips, 0, 0, tiled=True)  89.4 us
    all_to_all x1, blocking collectives, shards(): back = lax.all_to_all(out, ('z', 'y'), 0, 0, tiled=True)  14.7 us
    pallas_call x1, Pallas kernels, shards(): call(across_kernel, (row, row, row, struct((8, 128), F32)), block / 2, (p...  7.73 us
    pallas_call x1, Pallas kernels, shards(): call(pack_kernel, (struct((SLOTS, WIDTH), BF16), struct((1, ROWS), jnp.in...  4.1 us
    ppermute x3, waiting for transfers between devices, shards(): lax.ppermute(outs[k], 'x', [(i, (i + k) % XS) for i in range(XS)])  3.42 us
    ppermute x3, starting transfers between devices, shards(): lax.ppermute(outs[k], 'x', [(i, (i + k) % XS) for i in range(XS)])  3.26 us
  transfers between devices with their start and end apart: 6, of which 4 were waited for; matrix products, arithmetic and copies ran while one was open for 0% of the time, Pallas kernels for 4%

profile of v10, /device:TPU:2, one launch (start us, length us, event | category | flops | bytes accessed | tf_op | source)
XLA Modules:
  0.0 135.0 jit_solution(1192599394744648703)
XLA Ops:
  0.6 0.0 copy-start
  0.6 1.4 %copy-done = bf16[1024,768]{1,0:T(8,128)(2,1)S(1)} copy-done((bf16[1024,768]{1,0:T(8,128)(2,1)S(1)}, bf16[1024,768]{1,0:T(8,128)(2,1)}, u32[]{:S(2)}) %copy-start) | copy-done | bytes 1572888
  2.0 0.0 copy-start.1
  2.0 0.7 copy-done.1
  2.7 4.1 %shard_map.49 = (bf16[2048,768]{1,0:T(8,128)(2,1)S(1)}, s32[1,1024]{1,0:T(1,128)S(1)}) custom-call(s32[1,1024]{1,0:T(1,128)S(1)} %bitcast.20, bf16[1024,768]{1,0:T(8,128)(2,1)S(1)} %copy-done), custom_call_target="tpu_custom_call" | custom-call | flops 3221225472 | bytes 6000000 | tf_op jit(solution)/shard_map/pallas_call | solution.py:275
  6.8 89.4 %all_to_all.16 = bf16[128,16,768]{2,1,0:T(8,128)(2,1)S(1)} all-to-all(bf16[128,16,768]{2,1,0:T(8,128)(2,1)S(1)} %bitcast.17), channel_id=1, replica_groups=mesh['y'=4,'z'=8,'core'=2,'x'=4] {'z','x','y'}, dimensions={0} | all-to-all | bytes 6291456 | tf_op jit(solution)/shard_map/all_to_all | solution.py:283
  96.2 0.0 collective-permute-start
  96.2 0.1 add_bitcast_fusion.place_ref
  96.3 2.7 %shard_map.50 = (f32[3,2048]{1,0:T(4,128)S(1)}, f32[1,2048]{1,0:T(1,128)S(1)}) custom-call(bf16[2048,768]{1,0:T(8,128)(2,1)S(1)} %bitcast.14), custom_call_target="tpu_custom_call" | custom-call | flops 1610612736 | bytes 6000000 | tf_op jit(solution)/shard_map/pallas_call | solution.py:288
  99.0 0.8 collective-permute-start.1
  99.8 2.2 %shard_map.51.before_ref = f32[1,2048]{1,0:T(1,128)S(1)} custom-call(bf16[2048,768]{1,0:T(8,128)(2,1)S(1)} %bitcast.15, f32[3,2048]{1,0:T(4,128)S(1)} %get-tuple-element.22.info_ref, f32[1,2048]{1,0:T(1,128)S(1)} %get-tuple-element.23.before_ref), custom_call_target="tpu_custom_call" | custom-call | flops 2415919104 | bytes 6000000 | tf_op jit(solution)/shard_map/pallas_call | solution.py:291
  102.0 0.0 collective-permute-done.1.sib_info_ref
  102.0 0.1 collective-permute-done.sib_hbm
  102.0 7.7 %shard_map.52 = (f32[1,2048]{1,0:T(1,128)S(1)}, f32[1,2048]{1,0:T(1,128)S(1)}, f32[1,2048]{1,0:T(1,128)S(1)}, f32[8,128]{1,0:T(8,128)S(1)}) custom-call(s32[1,2]{1,0:T(1,128)S(1)} %add_bitcast_fusion.place_ref, bf16[2048,768]{1,0:T(8,128)(2,1)S(1)} %bitcast.16, bf16[2048,768]{1,0:T(8,128)(2,1)} %collective-permute-done.sib_hbm, ...), custom_call_target="tpu_custom_call" | custom-call | flops 3221225472 | bytes 6000000 | tf_op jit(solution)/shard_map/pallas_call | solution.py:296
  109.8 0.0 copy-start.2
  109.8 0.2 collective-permute-start.2
  110.0 0.9 shard_map.53
  110.9 0.1 collective-permute-done.2.taken_ref
  111.0 1.0 shard_map.54
  112.0 0.9 collective-permute-start.3
  112.9 2.0 %collective-permute-start.4 = (f32[40,128]{1,0:T(8,128)S(1)}, f32[40,128]{1,0:T(8,128)S(1)}, u32[]{:S(2)}, u32[]{:S(2)}) collective-permute-start(f32[40,128]{1,0:T(8,128)S(1)} %get-tuple-element.31), channel_id=1, source_target_pairs={{0,1},{1,2},{2,3},{3,0},{4,5},{5,6},{6,7},{7,4},{8,9},{9,10},{10,1... | collective-permute-start | bytes 61448 | tf_op jit(solution)/shard_map/ppermute | solution.py:318
  114.9 0.4 collective-permute-start.5
  115.3 2.1 %collective-permute-done.3.refs_0_ = f32[40,128]{1,0:T(8,128)S(1)} collective-permute-done((f32[40,128]{1,0:T(8,128)S(1)}, f32[40,128]{1,0:T(8,128)S(1)}, u32[]{:S(2)}, u32[]{:S(2)}) %collective-permute-start.3) | collective-permute-done | bytes 20512 | tf_op jit(solution)/shard_map/ppermute | solution.py:318
  117.4 0.0 collective-permute-done.4.refs_1_
  117.4 1.3 collective-permute-done.5.refs_2_
  118.7 14.7 %all_to_all.17 = f32[32,1,128]{2,1,0:T(1,128)S(1)} all-to-all(f32[32,1,128]{2,1,0:T(1,128)S(1)} %bitcast.18), channel_id=1, replica_groups=mesh['y'=4,'z'=8,'core'=2,'x'=4] {'z','y'}, dimensions={0} | all-to-all | bytes 32768 | tf_op jit(solution)/shard_map/all_to_all | solution.py:322
  133.4 0.0 copy-done.2
  133.4 1.6 %shard_map.56 = (f32[1,1024]{1,0:T(1,128)}, f32[1,1024]{1,0:T(1,128)}, f32[2,768]{1,0:T(2,128)}) custom-call(s32[1,2]{1,0:T(1,128)S(1)} %add_bitcast_fusion.place_ref, s32[1,1024]{1,0:T(1,128)S(1)} %bitcast.21, s32[1,1024]{1,0:T(1,128)S(1)} %get-tuple-element.20.rank_ref, f32[32,128]{1,0:T(8,128)S(1)} %bitcast.19, ...), custom_call_target="tpu_custom_call" | custom-call | flops 100000000 | bytes 6000000 | tf_op jit(solution)/shard_map/pallas_call | solution.py:323
  (1 shorter events, 0.0 us)
Async XLA Ops:
  0.6 1.4 %copy-start = (bf16[1024,768]{1,0:T(8,128)(2,1)S(1)}, bf16[1024,768]{1,0:T(8,128)(2,1)}, u32[]{:S(2)}) copy-start(bf16[1024,768]{1,0:T(8,128)(2,1)} %x_hbm.1) | copy-start | bytes 4718596
  2.0 0.7 copy-start.1
  96.2 5.8 %collective-permute-start = (bf16[2048,768]{1,0:T(8,128)(2,1)S(1)}, bf16[2048,768]{1,0:T(8,128)(2,1)}, u32[]{:S(2)}, u32[]{:S(2)}) collective-permute-start(bf16[2048,768]{1,0:T(8,128)(2,1)S(1)} %bitcast.13), channel_id=1, source_target_pairs={{0,4},{4,0},{1,5},{5,1},{2,6},{6,2},{3,7},{7,3},{8,12},{12,8},{9,1... | collective-permute-start | bytes 9437192 | tf_op jit(solution)/shard_map/ppermute | solution.py:286
  99.0 3.0 %collective-permute-start.1 = (f32[3,2048]{1,0:T(4,128)S(1)}, f32[3,2048]{1,0:T(4,128)S(1)}, u32[]{:S(2)}, u32[]{:S(2)}) collective-permute-start(f32[3,2048]{1,0:T(4,128)S(1)} %get-tuple-element.22.info_ref), channel_id=1, source_target_pairs={{0,4},{4,0},{1,5},{5,1},{2,6},{6,2},{3,7},{7,3},{8,12},{12,8},{9,1... | collective-permute-start | bytes 73736 | tf_op jit(solution)/shard_map/ppermute | solution.py:289
  109.8 23.7 %copy-start.2 = (s32[1024,1]{0,1:T(1,128)S(1)}, s32[1024,1]{0,1:T(1,128)}, u32[]{:S(2)}) copy-start(s32[1024,1]{0,1:T(1,128)} %param.3) | copy-start | bytes 12292
  109.8 1.3 collective-permute-start.2
  112.0 5.4 %collective-permute-start.3 = (f32[40,128]{1,0:T(8,128)S(1)}, f32[40,128]{1,0:T(8,128)S(1)}, u32[]{:S(2)}, u32[]{:S(2)}) collective-permute-start(f32[40,128]{1,0:T(8,128)S(1)} %get-tuple-element.30), channel_id=1, source_target_pairs={{0,2},{1,3},{2,0},{3,1},{4,6},{5,7},{6,4},{7,5},{8,10},{9,11},{10,... | collective-permute-start | bytes 61448 | tf_op jit(solution)/shard_map/ppermute | solution.py:318
  112.9 4.5 %collective-permute-start.4 = (f32[40,128]{1,0:T(8,128)S(1)}, f32[40,128]{1,0:T(8,128)S(1)}, u32[]{:S(2)}, u32[]{:S(2)}) collective-permute-start(f32[40,128]{1,0:T(8,128)S(1)} %get-tuple-element.31), channel_id=1, source_target_pairs={{0,1},{1,2},{2,3},{3,0},{4,5},{5,6},{6,7},{7,4},{8,9},{9,10},{10,1... | collective-permute-start | bytes 61448 | tf_op jit(solution)/shard_map/ppermute | solution.py:318
  114.9 3.8 %collective-permute-start.5 = (f32[40,128]{1,0:T(8,128)S(1)}, f32[40,128]{1,0:T(8,128)S(1)}, u32[]{:S(2)}, u32[]{:S(2)}) collective-permute-start(f32[40,128]{1,0:T(8,128)S(1)} %get-tuple-element.32), channel_id=1, source_target_pairs={{0,3},{1,0},{2,1},{3,2},{4,7},{5,4},{6,5},{7,6},{8,11},{9,8},{10,9... | collective-permute-start | bytes 61448 | tf_op jit(solution)/shard_map/ppermute | solution.py:318

commit v11 on v10

--- a/solution.py
+++ b/solution.py
@@ -144,8 +144,8 @@
             sib_hbm.at[rows(k), :], sib_ref.at[k * TILE : (k + 1) * TILE, :], sems.at[k]
         )
 
-    copy(0).start()
-    copy(2).start()
+    for k in range(TILES):
+        copy(k).start()
     for k in range(TILES):
         turned_ref[:, k * TILE : (k + 1) * TILE] = sib_info_ref[0:2, rows(k)]
     total = info_ref[2:3, 0:WIDTH] + sib_info_ref[2:3, 0:WIDTH]
@@ -172,18 +172,12 @@
         return both(i, part(x_ref, j), lanes(info_ref, 0, j), lanes(info_ref, 1, j))
 
     folds, downs = {}, {}
+    folds[1], downs[1] = own(1)
     folds[2], downs[2] = own(2)
+    for k in range(TILES):
+        copy(k).wait()
     give = {}
     for i in range(TILES):
-        if i == 0:
-            copy(0).wait()
-            copy(2).wait()
-            copy(1).start()
-            copy(3).start()
-            folds[1], downs[1] = own(1)
-        if i == 1:
-            copy(1).wait()
-            copy(3).wait()
         fold = folds.get(i)
         for k in (i, (i + 2) % TILES):
             value, down = both(i, part(sib_ref, k), lanes(turned_ref, 0, k), lanes(turned_ref, 1, k))

time: 135 us -> 135 us (level)
  no operation moved by 1% of the time
where the time goes in v11:
time: 135 us
  blocking collectives  104 us (77%)
  Pallas kernels  19.7 us (15%)
  starting transfers between devices  4.27 us (3%)
  waiting for transfers between devices  3.58 us (3%)
  local copies, waits for them, and re-layouts  2.09 us (2%)
    all_to_all x1, blocking collectives, shards(): lax.all_to_all(send.reshape(CHIPS, CAP, WIDTH), chips, 0, 0, tiled=True)  89.4 us
    all_to_all x1, blocking collectives, shards(): back = lax.all_to_all(out, ('z', 'y'), 0, 0, tiled=True)  14.7 us
    pallas_call x1, Pallas kernels, shards(): call(across_kernel, (row, row, row, struct((8, 128), F32)), block / 2, (p...  7.26 us
    pallas_call x1, Pallas kernels, shards(): call(pack_kernel, (struct((SLOTS, WIDTH), BF16), struct((1, ROWS), jnp.in...  4.1 us
    ppermute x3, waiting for transfers between devices, shards(): lax.ppermute(outs[k], 'x', [(i, (i + k) % XS) for i in range(XS)])  3.42 us
    ppermute x3, starting transfers between devices, shards(): lax.ppermute(outs[k], 'x', [(i, (i + k) % XS) for i in range(XS)])  3.27 us
  transfers between devices with their start and end apart: 6, of which 4 were waited for; matrix products, arithmetic and copies ran while one was open for 0% of the time, Pallas kernels for 4%

profile of v11, /device:TPU:2, one launch (start us, length us, event | category | flops | bytes accessed | tf_op | source)
XLA Modules:
  0.0 134.6 jit_solution(6692915336836240295)
XLA Ops:
  0.6 0.0 copy-start
  0.6 1.4 %copy-done = bf16[1024,768]{1,0:T(8,128)(2,1)S(1)} copy-done((bf16[1024,768]{1,0:T(8,128)(2,1)S(1)}, bf16[1024,768]{1,0:T(8,128)(2,1)}, u32[]{:S(2)}) %copy-start) | copy-done | bytes 1572888
  2.0 0.0 copy-start.1
  2.0 0.7 copy-done.1
  2.7 4.1 %shard_map.49 = (bf16[2048,768]{1,0:T(8,128)(2,1)S(1)}, s32[1,1024]{1,0:T(1,128)S(1)}) custom-call(s32[1,1024]{1,0:T(1,128)S(1)} %bitcast.20, bf16[1024,768]{1,0:T(8,128)(2,1)S(1)} %copy-done), custom_call_target="tpu_custom_call" | custom-call | flops 3221225472 | bytes 6000000 | tf_op jit(solution)/shard_map/pallas_call | solution.py:269
  6.8 89.4 %all_to_all.16 = bf16[128,16,768]{2,1,0:T(8,128)(2,1)S(1)} all-to-all(bf16[128,16,768]{2,1,0:T(8,128)(2,1)S(1)} %bitcast.17), channel_id=1, replica_groups=mesh['y'=4,'z'=8,'core'=2,'x'=4] {'z','x','y'}, dimensions={0} | all-to-all | bytes 6291456 | tf_op jit(solution)/shard_map/all_to_all | solution.py:277
  96.2 0.0 collective-permute-start
  96.2 0.1 add_bitcast_fusion.place_ref
  96.3 2.7 %shard_map.50 = (f32[3,2048]{1,0:T(4,128)S(1)}, f32[1,2048]{1,0:T(1,128)S(1)}) custom-call(bf16[2048,768]{1,0:T(8,128)(2,1)S(1)} %bitcast.14), custom_call_target="tpu_custom_call" | custom-call | flops 1610612736 | bytes 6000000 | tf_op jit(solution)/shard_map/pallas_call | solution.py:282
  99.0 0.8 collective-permute-start.1
  99.8 2.2 %shard_map.51.before_ref = f32[1,2048]{1,0:T(1,128)S(1)} custom-call(bf16[2048,768]{1,0:T(8,128)(2,1)S(1)} %bitcast.15, f32[3,2048]{1,0:T(4,128)S(1)} %get-tuple-element.22.info_ref, f32[1,2048]{1,0:T(1,128)S(1)} %get-tuple-element.23.before_ref), custom_call_target="tpu_custom_call" | custom-call | flops 2415919104 | bytes 6000000 | tf_op jit(solution)/shard_map/pallas_call | solution.py:285
  102.0 0.0 collective-permute-done.1.sib_info_ref
  102.0 0.1 collective-permute-done.sib_hbm
  102.0 7.3 %shard_map.52 = (f32[1,2048]{1,0:T(1,128)S(1)}, f32[1,2048]{1,0:T(1,128)S(1)}, f32[1,2048]{1,0:T(1,128)S(1)}, f32[8,128]{1,0:T(8,128)S(1)}) custom-call(s32[1,2]{1,0:T(1,128)S(1)} %add_bitcast_fusion.place_ref, bf16[2048,768]{1,0:T(8,128)(2,1)S(1)} %bitcast.16, bf16[2048,768]{1,0:T(8,128)(2,1)} %collective-permute-done.sib_hbm, ...), custom_call_target="tpu_custom_call" | custom-call | flops 3221225472 | bytes 6000000 | tf_op jit(solution)/shard_map/pallas_call | solution.py:290
  109.3 0.0 copy-start.2
  109.3 0.2 collective-permute-start.2
  109.5 0.9 shard_map.53
  110.5 0.1 collective-permute-done.2.taken_ref
  110.6 1.0 shard_map.54
  111.6 0.9 collective-permute-start.3
  112.5 2.0 %collective-permute-start.4 = (f32[40,128]{1,0:T(8,128)S(1)}, f32[40,128]{1,0:T(8,128)S(1)}, u32[]{:S(2)}, u32[]{:S(2)}) collective-permute-start(f32[40,128]{1,0:T(8,128)S(1)} %get-tuple-element.31), channel_id=1, source_target_pairs={{0,1},{1,2},{2,3},{3,0},{4,5},{5,6},{6,7},{7,4},{8,9},{9,10},{10,1... | collective-permute-start | bytes 61448 | tf_op jit(solution)/shard_map/ppermute | solution.py:312
  114.5 0.4 collective-permute-start.5
  114.8 2.1 %collective-permute-done.3.refs_0_ = f32[40,128]{1,0:T(8,128)S(1)} collective-permute-done((f32[40,128]{1,0:T(8,128)S(1)}, f32[40,128]{1,0:T(8,128)S(1)}, u32[]{:S(2)}, u32[]{:S(2)}) %collective-permute-start.3) | collective-permute-done | bytes 20512 | tf_op jit(solution)/shard_map/ppermute | solution.py:312
  117.0 0.0 collective-permute-done.4.refs_1_
  117.0 1.3 collective-permute-done.5.refs_2_
  118.3 14.7 %all_to_all.17 = f32[32,1,128]{2,1,0:T(1,128)S(1)} all-to-all(f32[32,1,128]{2,1,0:T(1,128)S(1)} %bitcast.18), channel_id=1, replica_groups=mesh['y'=4,'z'=8,'core'=2,'x'=4] {'z','y'}, dimensions={0} | all-to-all | bytes 32768 | tf_op jit(solution)/shard_map/all_to_all | solution.py:316
  133.0 0.0 copy-done.2
  133.0 1.6 %shard_map.56 = (f32[1,1024]{1,0:T(1,128)}, f32[1,1024]{1,0:T(1,128)}, f32[2,768]{1,0:T(2,128)}) custom-call(s32[1,2]{1,0:T(1,128)S(1)} %add_bitcast_fusion.place_ref, s32[1,1024]{1,0:T(1,128)S(1)} %bitcast.21, s32[1,1024]{1,0:T(1,128)S(1)} %get-tuple-element.20.rank_ref, f32[32,128]{1,0:T(8,128)S(1)} %bitcast.19, ...), custom_call_target="tpu_custom_call" | custom-call | flops 100000000 | bytes 6000000 | tf_op jit(solution)/shard_map/pallas_call | solution.py:317
  (1 shorter events, 0.0 us)
Async XLA Ops:
  0.6 1.4 %copy-start = (bf16[1024,768]{1,0:T(8,128)(2,1)S(1)}, bf16[1024,768]{1,0:T(8,128)(2,1)}, u32[]{:S(2)}) copy-start(bf16[1024,768]{1,0:T(8,128)(2,1)} %x_hbm.1) | copy-start | bytes 4718596
  2.0 0.7 copy-start.1
  96.2 5.8 %collective-permute-start = (bf16[2048,768]{1,0:T(8,128)(2,1)S(1)}, bf16[2048,768]{1,0:T(8,128)(2,1)}, u32[]{:S(2)}, u32[]{:S(2)}) collective-permute-start(bf16[2048,768]{1,0:T(8,128)(2,1)S(1)} %bitcast.13), channel_id=1, source_target_pairs={{0,4},{4,0},{1,5},{5,1},{2,6},{6,2},{3,7},{7,3},{8,12},{12,8},{9,1... | collective-permute-start | bytes 9437192 | tf_op jit(solution)/shard_map/ppermute | solution.py:280
  99.0 3.0 %collective-permute-start.1 = (f32[3,2048]{1,0:T(4,128)S(1)}, f32[3,2048]{1,0:T(4,128)S(1)}, u32[]{:S(2)}, u32[]{:S(2)}) collective-permute-start(f32[3,2048]{1,0:T(4,128)S(1)} %get-tuple-element.22.info_ref), channel_id=1, source_target_pairs={{0,4},{4,0},{1,5},{5,1},{2,6},{6,2},{3,7},{7,3},{8,12},{12,8},{9,1... | collective-permute-start | bytes 73736 | tf_op jit(solution)/shard_map/ppermute | solution.py:283
  109.3 23.7 %copy-start.2 = (s32[1024,1]{0,1:T(1,128)S(1)}, s32[1024,1]{0,1:T(1,128)}, u32[]{:S(2)}) copy-start(s32[1024,1]{0,1:T(1,128)} %param.3) | copy-start | bytes 12292
  109.3 1.3 collective-permute-start.2
  111.6 5.4 %collective-permute-start.3 = (f32[40,128]{1,0:T(8,128)S(1)}, f32[40,128]{1,0:T(8,128)S(1)}, u32[]{:S(2)}, u32[]{:S(2)}) collective-permute-start(f32[40,128]{1,0:T(8,128)S(1)} %get-tuple-element.30), channel_id=1, source_target_pairs={{0,2},{1,3},{2,0},{3,1},{4,6},{5,7},{6,4},{7,5},{8,10},{9,11},{10,... | collective-permute-start | bytes 61448 | tf_op jit(solution)/shard_map/ppermute | solution.py:312
  112.5 4.5 %collective-permute-start.4 = (f32[40,128]{1,0:T(8,128)S(1)}, f32[40,128]{1,0:T(8,128)S(1)}, u32[]{:S(2)}, u32[]{:S(2)}) collective-permute-start(f32[40,128]{1,0:T(8,128)S(1)} %get-tuple-element.31), channel_id=1, source_target_pairs={{0,1},{1,2},{2,3},{3,0},{4,5},{5,6},{6,7},{7,4},{8,9},{9,10},{10,1... | collective-permute-start | bytes 61448 | tf_op jit(solution)/shard_map/ppermute | solution.py:312
  114.5 3.8 %collective-permute-start.5 = (f32[40,128]{1,0:T(8,128)S(1)}, f32[40,128]{1,0:T(8,128)S(1)}, u32[]{:S(2)}, u32[]{:S(2)}) collective-permute-start(f32[40,128]{1,0:T(8,128)S(1)} %get-tuple-element.32), channel_id=1, source_target_pairs={{0,3},{1,0},{2,1},{3,2},{4,7},{5,4},{6,5},{7,6},{8,11},{9,8},{10,9... | collective-permute-start | bytes 61448 | tf_op jit(solution)/shard_map/ppermute | solution.py:312

commit v12 on v9

--- a/solution.py
+++ b/solution.py
@@ -36,7 +36,7 @@
 
 
 def chip_of(ids):
-    return ((ids >> 2) & 7) * 16 + (ids & 3) * 4 + (ids >> 5)
+    return (ids & 3) * 32 + ((ids >> 2) & 7) * 4 + (ids >> 5)
 
 
 def eye(n):
@@ -188,16 +188,7 @@
         give_ref[:, rows(k)] = give[k]
 
 
-def spread(source, row):
-    slot = lax.rem(iota((CAP, SLOTS), 1), CAP) == iota((CAP, SLOTS), 0)
-    parts = jnp.concatenate(split3(jnp.where(slot, row, 0.0)), axis=0)
-    lines = lax.dot_general(source, parts, NT, preferred_element_type=F32)
-    return lines[:, 0:CAP] + lines[:, CAP : 2 * CAP] + lines[:, 2 * CAP : 3 * CAP]
-
-
-def centre_kernel(
-    place_ref, after_ref, x_ref, info_ref, sib_info_ref, source_ref, centre_ref, mean_ref
-):
+def centre_kernel(after_ref, x_ref, info_ref, sib_info_ref, centre_ref, mean_ref):
     total = info_ref[2:3, 0:WIDTH] + sib_info_ref[2:3, 0:WIDTH]
     count = info_ref[2:3, WIDTH : WIDTH + 1] + sib_info_ref[2:3, WIDTH : WIDTH + 1]
     mean = total / count
@@ -207,35 +198,41 @@
     parts = jnp.concatenate(split3(total) + (jnp.zeros((13, WIDTH), BF16),), axis=0)
     toward = lax.dot_general(parts, x_ref[...], NT, preferred_element_type=F32)
     toward = toward[0:1] + toward[1:2] + toward[2:3]
-    centre = toward * info_ref[0:1, :] * scale / WIDTH
-    chip = iota((1, SLOTS), 1) // CAP
-    line = (((chip >> 2) - place_ref[0, 0]) & 3) * 32 + (chip >> 4) * 4 + (chip & 3)
-    source = (line == iota((CHIPS, SLOTS), 0)).astype(F32).astype(BF16)
-    source_ref[...] = source
-    centre_ref[...] = spread(source, centre)
-
-
-def spread_kernel(
-    place_ref, best_ref, taken_ref, info_ref, source_ref, centre_ref, mean_ref, *out_refs
-):
+    centre_ref[...] = toward * info_ref[0:1, :] * scale / WIDTH
+
+
+def lines_kernel(place_ref, best_ref, taken_ref, info_ref, centre_ref, mean_ref, *refs):
+    out_refs, near_ref = refs[:XS], refs[XS]
     best = jnp.maximum(best_ref[...], taken_ref[...])
-    near = jnp.maximum(-1.0, best * info_ref[0:1, :] / WIDTH)
-    lines = jnp.concatenate([spread(source_ref[...], near), centre_ref[...]] * XS, axis=1)
-    lines = jnp.where(iota((CHIPS, XS * PAIR), 1) // PAIR == place_ref[0, 0], lines, 0.0)
+    near_ref[...] = jnp.maximum(-1.0, best * info_ref[0:1, :] / WIDTH)
     for k in range(XS):
-        out_refs[k][0:32, :] = lines[32 * k : 32 * (k + 1)]
-        out_refs[k][32:40, :] = mean_ref[...]
+        first = ((place_ref[0, 0] + k) & 3) * TILE
+        for line in range(4):
+            lane = pl.ds(pl.multiple_of(first + line * 128, 128), 128)
+            out_refs[k][line : line + 1, :] = near_ref[:, lane]
+            out_refs[k][4 + line : 5 + line, :] = centre_ref[:, lane]
+        out_refs[k][8:16, :] = mean_ref[...]
 
 
 def merge_kernel(*refs):
-    refs[XS][...] = sum(ref[0:32, :] for ref in refs[:XS])
+    came, out_ref = refs[:XS], refs[XS]
+    group, line = iota((8, 128), 1) // CAP, iota((8, 128), 0)
+    for s in range(4):
+        rows = [ref[4 * t + s : 4 * t + s + 1, :] for ref in came for t in range(2)]
+        value = jnp.concatenate(rows, axis=0)
+        out = jnp.zeros((8, 128), F32)
+        for d in range(8):
+            turned = pltpu.roll(value, CAP * d, 1) if d else value
+            picked = jnp.sum(jnp.where(group == line, turned, 0.0), axis=0, keepdims=True)
+            out = jnp.where(((group - line) & 7) == d, picked, out)
+        out_ref[8 * s : 8 * (s + 1), :] = out
 
 
 def unpack_kernel(place_ref, ids_ref, rank_ref, back_ref, *refs):
     came, (near_ref, centre_ref, mean_ref) = refs[:XS], refs[XS:]
     for k in range(2):
         offset = (place_ref[0, 0] - 2 * place_ref[0, 1] - k) & 3
-        folded = sum(jnp.where(offset == i, ref[32:40, :], 0.0) for i, ref in enumerate(came))
+        folded = sum(jnp.where(offset == i, ref[8:16, :], 0.0) for i, ref in enumerate(came))
         for j in range(WIDTH // 128):
             mean_ref[k : k + 1, j * 128 : (j + 1) * 128] = folded[j : j + 1]
     ids = ids_ref[...]
@@ -244,7 +241,7 @@
     parts = jnp.concatenate(split3(back_ref[...]), axis=1)
     picked = lax.dot_general(parts, onehot, TN, preferred_element_type=F32)
     picked = picked[0:128] + picked[128:256] + picked[256:384]
-    place = (ids & 3) * PAIR + rank_ref[...]
+    place = ((place_ref[0, 0] - ids) & 3) * PAIR + rank_ref[...]
     line = iota((128, ROWS), 0)
     near_ref[...] = jnp.sum(jnp.where(line == place, picked, 0.0), axis=0, keepdims=True)
     centre_ref[...] = jnp.sum(
@@ -280,7 +277,7 @@
         (pltpu.VMEM((ROWS, WIDTH), BF16), pltpu.SemaphoreType.DMA),
         in_specs=[here, pl.BlockSpec(memory_space=pltpu.HBM)],
     )(ids, embeddings)
-    chips = ("z", "x", "y")
+    chips = ("x", "z", "y")
     mine = lax.all_to_all(send.reshape(CHIPS, CAP, WIDTH), chips, 0, 0, tiled=True)
     mine = mine.reshape(SLOTS, WIDTH)
     swap = [(0, 1), (1, 0)]
@@ -293,7 +290,7 @@
     axes = [lax.axis_index("x"), lax.axis_index("core")]
     place = jnp.stack(axes).astype(jnp.int32).reshape(1, 2)
     scalars = pl.BlockSpec(memory_space=pltpu.SMEM)
-    line = struct((40, 128), F32)
+    line = struct((16, 128), F32)
     best, give = call(
         across_kernel,
         (row, row),
@@ -306,15 +303,16 @@
         in_specs=[scalars, here, pl.BlockSpec(memory_space=pltpu.HBM), here, here, here],
     )(place, mine, sib, info, sib_info, best)
     taken = lax.ppermute(give, "core", swap)
-    source, centre, mean = call(
-        centre_kernel,
-        (struct((CHIPS, SLOTS), BF16), struct((CHIPS, CAP), F32), struct((8, 128), F32)),
-        block / 8,
-        in_specs=[scalars] + [here] * 4,
-    )(place, give, mine, info, sib_info)
+    centre, mean = call(
+        centre_kernel, (row, struct((8, 128), F32)), block / 8
+    )(give, mine, info, sib_info)
     outs = call(
-        spread_kernel, (line,) * XS, 1e8, in_specs=[scalars] + [here] * 6
-    )(place, best, taken, info, source, centre, mean)
+        lines_kernel,
+        (line,) * XS,
+        1e7,
+        (pltpu.VMEM((1, SLOTS), F32),),
+        in_specs=[scalars] + [here] * 5,
+    )(place, best, taken, info, centre, mean)
     came = [outs[0]]
     for k in range(1, XS):
         came.append(lax.ppermute(outs[k], "x", [(i, (i + k) % XS) for i in range(XS)]))

time: 136 us -> 134 us (0.985)
  transfers between devices with their start and end apart: 6 -> 6, of which waited for: 3 -> 4; matrix products, arithmetic and copies ran while one was open for 0% -> 0% of each run, Pallas kernels for 5% -> 4%
where the time goes in v12:
time: 134 us
  blocking collectives  104 us (78%)
  Pallas kernels  18.8 us (14%)
  starting transfers between devices  4.73 us (4%)
  waiting for transfers between devices  3.46 us (3%)
  local copies, waits for them, and re-layouts  2.09 us (2%)
    all_to_all x1, blocking collectives, shards(): lax.all_to_all(send.reshape(CHIPS, CAP, WIDTH), chips, 0, 0, tiled=True)  89.5 us
    all_to_all x1, blocking collectives, shards(): back = lax.all_to_all(out, ('z', 'y'), 0, 0, tiled=True)  14.5 us
    pallas_call x1, Pallas kernels, shards(): call(across_kernel, (row, row), block / 2, (pltpu.VMEM((SLOTS, WIDTH), BF...  6.68 us
    pallas_call x1, Pallas kernels, shards(): call(pack_kernel, (struct((SLOTS, WIDTH), BF16), struct((1, ROWS), jnp.in...  4.1 us
    ppermute x3, starting transfers between devices, shards(): lax.ppermute(outs[k], 'x', [(i, (i + k) % XS) for i in range(XS)])  3.73 us
    ppermute x3, waiting for transfers between devices, shards(): lax.ppermute(outs[k], 'x', [(i, (i + k) % XS) for i in range(XS)])  3.3 us
    pallas_call x1, Pallas kernels, shards(): call(diagonal_kernel, (struct((3, SLOTS), F32), row), block / 4)(mine)  2.7 us
  transfers between devices with their start and end apart: 6, of which 4 were waited for; matrix products, arithmetic and copies ran while one was open for 0% of the time, Pallas kernels for 4%

profile of v12, /device:TPU:2, one launch (start us, length us, event | category | flops | bytes accessed | tf_op | source)
XLA Modules:
  0.0 134.0 jit_solution(17584468829440781171)
XLA Ops:
  0.6 0.0 copy-start
  0.6 1.4 %copy-done = bf16[1024,768]{1,0:T(8,128)(2,1)S(1)} copy-done((bf16[1024,768]{1,0:T(8,128)(2,1)S(1)}, bf16[1024,768]{1,0:T(8,128)(2,1)}, u32[]{:S(2)}) %copy-start) | copy-done | bytes 1572888
  2.0 0.0 copy-start.1
  2.0 0.7 copy-done.1
  2.7 4.1 %shard_map.49 = (bf16[2048,768]{1,0:T(8,128)(2,1)S(1)}, s32[1,1024]{1,0:T(1,128)S(1)}) custom-call(s32[1,1024]{1,0:T(1,128)S(1)} %bitcast.21, bf16[1024,768]{1,0:T(8,128)(2,1)S(1)} %copy-done), custom_call_target="tpu_custom_call" | custom-call | flops 3221225472 | bytes 6000000 | tf_op jit(solution)/shard_map/pallas_call | solution.py:273
  6.8 89.5 %all_to_all.16 = bf16[128,16,768]{2,1,0:T(8,128)(2,1)S(1)} all-to-all(bf16[128,16,768]{2,1,0:T(8,128)(2,1)S(1)} %bitcast.18), channel_id=1, replica_groups=mesh['y'=4,'z'=8,'core'=2,'x'=4] {'x','z','y'}, dimensions={0} | all-to-all | bytes 6291456 | tf_op jit(solution)/shard_map/all_to_all | solution.py:281
  96.4 0.0 collective-permute-start
  96.4 0.1 add_bitcast_fusion.place_ref
  96.4 2.7 %shard_map.50 = (f32[3,2048]{1,0:T(4,128)S(1)}, f32[1,2048]{1,0:T(1,128)S(1)}) custom-call(bf16[2048,768]{1,0:T(8,128)(2,1)S(1)} %bitcast.14), custom_call_target="tpu_custom_call" | custom-call | flops 1610612736 | bytes 6000000 | tf_op jit(solution)/shard_map/pallas_call | solution.py:286
  99.1 0.8 collective-permute-start.1
  99.9 2.2 %shard_map.51.before_ref = f32[1,2048]{1,0:T(1,128)S(1)} custom-call(bf16[2048,768]{1,0:T(8,128)(2,1)S(1)} %bitcast.15, f32[3,2048]{1,0:T(4,128)S(1)} %get-tuple-element.20.info_ref, f32[1,2048]{1,0:T(1,128)S(1)} %get-tuple-element.21.before_ref), custom_call_target="tpu_custom_call" | custom-call | flops 2415919104 | bytes 6000000 | tf_op jit(solution)/shard_map/pallas_call | solution.py:289
  102.1 0.0 collective-permute-done.1.sib_info_ref
  102.1 0.1 collective-permute-done.sib_hbm
  102.2 6.7 %shard_map.52 = (f32[1,2048]{1,0:T(1,128)S(1)}, f32[1,2048]{1,0:T(1,128)S(1)}) custom-call(s32[1,2]{1,0:T(1,128)S(1)} %add_bitcast_fusion.place_ref, bf16[2048,768]{1,0:T(8,128)(2,1)S(1)} %bitcast.16, bf16[2048,768]{1,0:T(8,128)(2,1)} %collective-permute-done.sib_hbm, f32[3,2048]{1,0:T(4,128)S(1)} %get-tuple-element.20.info_ref, ...), custom_call_target="tpu_custom_call" | custom-call | flops 3221225472 | bytes 6000000 | tf_op jit(solution)/shard_map/pallas_call | solution.py:294
  108.8 0.0 copy-start.2
  108.9 0.2 collective-permute-start.2
  109.1 0.9 shard_map.53
  110.0 0.1 collective-permute-done.2.taken_ref
  110.1 0.6 shard_map.54
  110.7 0.2 collective-permute-start.3
  110.9 3.2 %collective-permute-start.4 = (f32[16,128]{1,0:T(8,128)S(1)}, f32[16,128]{1,0:T(8,128)S(1)}, u32[]{:S(2)}, u32[]{:S(2)}) collective-permute-start(f32[16,128]{1,0:T(8,128)S(1)} %get-tuple-element.28), channel_id=1, source_target_pairs={{0,2},{1,3},{2,0},{3,1},{4,6},{5,7},{6,4},{7,5},{8,10},{9,11},{10,... | collective-permute-start | bytes 24584 | tf_op jit(solution)/shard_map/ppermute | solution.py:318
  114.1 0.3 collective-permute-start.5
  114.4 0.0 collective-permute-done.3.refs_1_
  114.4 1.6 %collective-permute-done.4.refs_2_ = f32[16,128]{1,0:T(8,128)S(1)} collective-permute-done((f32[16,128]{1,0:T(8,128)S(1)}, f32[16,128]{1,0:T(8,128)S(1)}, u32[]{:S(2)}, u32[]{:S(2)}) %collective-permute-start.4) | collective-permute-done | bytes 8224 | tf_op jit(solution)/shard_map/ppermute | solution.py:318
  116.1 1.7 %collective-permute-done.5.refs_3_ = f32[16,128]{1,0:T(8,128)S(1)} collective-permute-done((f32[16,128]{1,0:T(8,128)S(1)}, f32[16,128]{1,0:T(8,128)S(1)}, u32[]{:S(2)}, u32[]{:S(2)}) %collective-permute-start.5) | collective-permute-done | bytes 8224 | tf_op jit(solution)/shard_map/ppermute | solution.py:318
  117.7 0.1 shard_map.55
  117.8 14.5 %all_to_all.17 = f32[32,1,128]{2,1,0:T(1,128)S(1)} all-to-all(f32[32,1,128]{2,1,0:T(1,128)S(1)} %bitcast.19), channel_id=1, replica_groups=mesh['y'=4,'z'=8,'core'=2,'x'=4] {'z','y'}, dimensions={0} | all-to-all | bytes 32768 | tf_op jit(solution)/shard_map/all_to_all | solution.py:320
  132.4 0.0 copy-done.2
  132.4 1.6 %shard_map.56 = (f32[1,1024]{1,0:T(1,128)}, f32[1,1024]{1,0:T(1,128)}, f32[2,768]{1,0:T(2,128)}) custom-call(s32[1,2]{1,0:T(1,128)S(1)} %add_bitcast_fusion.place_ref, s32[1,1024]{1,0:T(1,128)S(1)} %bitcast.22, s32[1,1024]{1,0:T(1,128)S(1)} %get-tuple-element.18.rank_ref, f32[32,128]{1,0:T(8,128)S(1)} %bitcast.20, f32[16,128]{1,0:T(8,128)S(1)} %get-tuple-element.26.refs_0_, ...), custom_call_target="tpu_custom_call" | custom-call | flops 100000000 | bytes 6000000 | tf_op jit(solution)/shard_map/pallas_call | solution.py:321
Async XLA Ops:
  0.6 1.4 %copy-start = (bf16[1024,768]{1,0:T(8,128)(2,1)S(1)}, bf16[1024,768]{1,0:T(8,128)(2,1)}, u32[]{:S(2)}) copy-start(bf16[1024,768]{1,0:T(8,128)(2,1)} %x_hbm.1) | copy-start | bytes 4718596
  2.0 0.7 copy-start.1
  96.4 5.8 %collective-permute-start = (bf16[2048,768]{1,0:T(8,128)(2,1)S(1)}, bf16[2048,768]{1,0:T(8,128)(2,1)}, u32[]{:S(2)}, u32[]{:S(2)}) collective-permute-start(bf16[2048,768]{1,0:T(8,128)(2,1)S(1)} %bitcast.13), channel_id=1, source_target_pairs={{0,4},{4,0},{1,5},{5,1},{2,6},{6,2},{3,7},{7,3},{8,12},{12,8},{9,1... | collective-permute-start | bytes 9437192 | tf_op jit(solution)/shard_map/ppermute | solution.py:284
  99.1 3.0 %collective-permute-start.1 = (f32[3,2048]{1,0:T(4,128)S(1)}, f32[3,2048]{1,0:T(4,128)S(1)}, u32[]{:S(2)}, u32[]{:S(2)}) collective-permute-start(f32[3,2048]{1,0:T(4,128)S(1)} %get-tuple-element.20.info_ref), channel_id=1, source_target_pairs={{0,4},{4,0},{1,5},{5,1},{2,6},{6,2},{3,7},{7,3},{8,12},{12,8},{9,1... | collective-permute-start | bytes 73736 | tf_op jit(solution)/shard_map/ppermute | solution.py:287
  108.8 23.5 %copy-start.2 = (s32[1024,1]{0,1:T(1,128)S(1)}, s32[1024,1]{0,1:T(1,128)}, u32[]{:S(2)}) copy-start(s32[1024,1]{0,1:T(1,128)} %param.3) | copy-start | bytes 12292
  108.9 1.3 collective-permute-start.2
  110.7 3.7 %collective-permute-start.3 = (f32[16,128]{1,0:T(8,128)S(1)}, f32[16,128]{1,0:T(8,128)S(1)}, u32[]{:S(2)}, u32[]{:S(2)}) collective-permute-start(f32[16,128]{1,0:T(8,128)S(1)} %get-tuple-element.27), channel_id=1, source_target_pairs={{0,1},{1,2},{2,3},{3,0},{4,5},{5,6},{6,7},{7,4},{8,9},{9,10},{10,1... | collective-permute-start | bytes 24584 | tf_op jit(solution)/shard_map/ppermute | solution.py:318
  110.9 5.2 %collective-permute-start.4 = (f32[16,128]{1,0:T(8,128)S(1)}, f32[16,128]{1,0:T(8,128)S(1)}, u32[]{:S(2)}, u32[]{:S(2)}) collective-permute-start(f32[16,128]{1,0:T(8,128)S(1)} %get-tuple-element.28), channel_id=1, source_target_pairs={{0,2},{1,3},{2,0},{3,1},{4,6},{5,7},{6,4},{7,5},{8,10},{9,11},{10,... | collective-permute-start | bytes 24584 | tf_op jit(solution)/shard_map/ppermute | solution.py:318
  114.1 3.7 %collective-permute-start.5 = (f32[16,128]{1,0:T(8,128)S(1)}, f32[16,128]{1,0:T(8,128)S(1)}, u32[]{:S(2)}, u32[]{:S(2)}) collective-permute-start(f32[16,128]{1,0:T(8,128)S(1)} %get-tuple-element.29), channel_id=1, source_target_pairs={{0,3},{1,0},{2,1},{3,2},{4,7},{5,4},{6,5},{7,6},{8,11},{9,8},{10,9... | collective-permute-start | bytes 24584 | tf_op jit(solution)/shard_map/ppermute | solution.py:318

commit v13 on v12

--- a/solution.py
+++ b/solution.py
@@ -97,11 +97,16 @@
 
 
 def diagonal_kernel(x_ref, info_ref, best_ref):
-    live = to_row((x_ref[:, 0:1].astype(F32) < MARK / 2).astype(F32))
-    weights = jnp.broadcast_to(live, (8, SLOTS)).astype(BF16)
-    totals = jnp.dot(weights, x_ref[...], preferred_element_type=F32)
+    first = x_ref[:, 0:1].astype(F32)
+    live = to_row((first < MARK / 2).astype(F32))
     info_ref[1:2, :] = jnp.where(live > 0, 0.0, LOW)
-    info_ref[2:3, 0:WIDTH] = totals[0:1]
+    total = jnp.zeros((8, WIDTH), F32)
+    for i in range(TILES):
+        rows = part(x_ref, i).astype(F32)
+        total = total + jnp.sum(rows.reshape(TILE // 8, 8, WIDTH), axis=0)
+    total = jnp.sum(total, axis=0, keepdims=True)
+    lead = jnp.sum(jnp.where(first < MARK / 2, first, 0.0), axis=0, keepdims=True)
+    info_ref[2:3, 0:WIDTH] = jnp.where(iota((1, WIDTH), 1) == 0, lead, total)
     count = jnp.sum(live, axis=1, keepdims=True)
     info_ref[2:3, WIDTH:] = jnp.broadcast_to(count, (1, SLOTS - WIDTH))
     for i in range(TILES):
@@ -119,7 +124,7 @@
     for i in range(TILES - 2):
         inv = to_column(lanes(info_ref, 0, i))
         bias = to_column(lanes(info_ref, 1, i))
-        for j in range(i + 1, TILES - i):
+        for j in range(i + 1, TILES):
             dots = lax.dot_general(part(x_ref, i), part(x_ref, j), NT, preferred_element_type=F32)
             fold = fold_lanes(dots * lanes(info_ref, 0, j) + lanes(info_ref, 1, j))
             fold_ref[...] = fold if j == i + 1 else jnp.maximum(fold_ref[...], fold)
@@ -156,12 +161,8 @@
         down = jnp.max(dots * columns[i][0] + columns[i][1], axis=0, keepdims=True)
         return fold_lanes(dots * row + bias), down
 
-    def own(i):
-        j = TILES - 1
-        return both(i, part(x_ref, j), lanes(info_ref, 0, j), lanes(info_ref, 1, j))
-
-    folds, downs = {}, {}
-    folds[2], downs[2] = own(2)
+    j = TILES - 1
+    last, own = both(2, part(x_ref, j), lanes(info_ref, 0, j), lanes(info_ref, 1, j))
     give = {}
     for i in range(TILES):
         if i == 0:
@@ -169,11 +170,10 @@
             copy(2).wait()
             copy(1).start()
             copy(3).start()
-            folds[1], downs[1] = own(1)
         if i == 1:
             copy(1).wait()
             copy(3).wait()
-        fold = folds.get(i)
+        fold = last if i == 2 else None
         for k in (i, (i + 2) % TILES):
             value, down = both(i, part(sib_ref, k), lanes(turned_ref, 0, k), lanes(turned_ref, 1, k))
             fold = value if fold is None else jnp.maximum(fold, value)
@@ -182,7 +182,7 @@
             lanes(before_ref, 0, i), to_row(jnp.max(fold, axis=1, keepdims=True))
         )
         if i == TILES - 1:
-            best = jnp.maximum(best, jnp.maximum(downs[1], downs[2]))
+            best = jnp.maximum(best, own)
         best_ref[:, i * TILE : (i + 1) * TILE] = best
     for k in range(TILES):
         give_ref[:, rows(k)] = give[k]

time: 134 us -> 135 us (level)
  transfers between devices with their start and end apart: 6 -> 6, of which waited for: 4 -> 3; matrix products, arithmetic and copies ran while one was open for 0% -> 0% of each run, Pallas kernels for 4% -> 5%
where the time goes in v13:
time: 135 us
  blocking collectives  104 us (77%)
  Pallas kernels  19.6 us (15%)
  starting transfers between devices  4.62 us (3%)
  waiting for transfers between devices  3.51 us (3%)
  local copies, waits for them, and re-layouts  2.09 us (2%)
    all_to_all x1, blocking collectives, shards(): lax.all_to_all(send.reshape(CHIPS, CAP, WIDTH), chips, 0, 0, tiled=True)  89.5 us
    all_to_all x1, blocking collectives, shards(): back = lax.all_to_all(out, ('z', 'y'), 0, 0, tiled=True)  14.5 us
    pallas_call x1, Pallas kernels, shards(): call(across_kernel, (row, row), block / 2, (pltpu.VMEM((SLOTS, WIDTH), BF...  7.01 us
    pallas_call x1, Pallas kernels, shards(): call(pack_kernel, (struct((SLOTS, WIDTH), BF16), struct((1, ROWS), jnp.in...  4.1 us
    ppermute x3, starting transfers between devices, shards(): lax.ppermute(outs[k], 'x', [(i, (i + k) % XS) for i in range(XS)])  3.73 us
    ppermute x3, waiting for transfers between devices, shards(): lax.ppermute(outs[k], 'x', [(i, (i + k) % XS) for i in range(XS)])  3.29 us
    pallas_call x1, Pallas kernels, shards(): call(diagonal_kernel, (struct((3, SLOTS), F32), row), block / 4)(mine)  2.71 us
  transfers between devices with their start and end apart: 6, of which 3 were waited for; matrix products, arithmetic and copies ran while one was open for 0% of the time, Pallas kernels for 5%

profile of v13, /device:TPU:2, one launch (start us, length us, event | category | flops | bytes accessed | tf_op | source)
XLA Modules:
  0.0 134.7 jit_solution(15361596279452745216)
XLA Ops:
  0.6 0.0 copy-start
  0.6 1.4 %copy-done = bf16[1024,768]{1,0:T(8,128)(2,1)S(1)} copy-done((bf16[1024,768]{1,0:T(8,128)(2,1)S(1)}, bf16[1024,768]{1,0:T(8,128)(2,1)}, u32[]{:S(2)}) %copy-start) | copy-done | bytes 1572888
  2.0 0.0 copy-start.1
  2.0 0.7 copy-done.1
  2.7 4.1 %shard_map.49 = (bf16[2048,768]{1,0:T(8,128)(2,1)S(1)}, s32[1,1024]{1,0:T(1,128)S(1)}) custom-call(s32[1,1024]{1,0:T(1,128)S(1)} %bitcast.21, bf16[1024,768]{1,0:T(8,128)(2,1)S(1)} %copy-done), custom_call_target="tpu_custom_call" | custom-call | flops 3221225472 | bytes 6000000 | tf_op jit(solution)/shard_map/pallas_call | solution.py:273
  6.8 89.5 %all_to_all.16 = bf16[128,16,768]{2,1,0:T(8,128)(2,1)S(1)} all-to-all(bf16[128,16,768]{2,1,0:T(8,128)(2,1)S(1)} %bitcast.18), channel_id=1, replica_groups=mesh['y'=4,'z'=8,'core'=2,'x'=4] {'x','z','y'}, dimensions={0} | all-to-all | bytes 6291456 | tf_op jit(solution)/shard_map/all_to_all | solution.py:281
  96.4 0.0 collective-permute-start
  96.4 0.1 add_bitcast_fusion.place_ref
  96.4 2.7 %shard_map.50 = (f32[3,2048]{1,0:T(4,128)S(1)}, f32[1,2048]{1,0:T(1,128)S(1)}) custom-call(bf16[2048,768]{1,0:T(8,128)(2,1)S(1)} %bitcast.14), custom_call_target="tpu_custom_call" | custom-call | flops 1610612736 | bytes 6000000 | tf_op jit(solution)/shard_map/pallas_call | solution.py:286
  99.2 0.8 collective-permute-start.1
  99.9 2.6 %shard_map.51.before_ref = f32[1,2048]{1,0:T(1,128)S(1)} custom-call(bf16[2048,768]{1,0:T(8,128)(2,1)S(1)} %bitcast.15, f32[3,2048]{1,0:T(4,128)S(1)} %get-tuple-element.20.info_ref, f32[1,2048]{1,0:T(1,128)S(1)} %get-tuple-element.21.before_ref), custom_call_target="tpu_custom_call" | custom-call | flops 2415919104 | bytes 6000000 | tf_op jit(solution)/shard_map/pallas_call | solution.py:289
  102.6 0.0 collective-permute-done.1.sib_info_ref
  102.6 0.0 collective-permute-done.sib_hbm
  102.6 7.0 %shard_map.52 = (f32[1,2048]{1,0:T(1,128)S(1)}, f32[1,2048]{1,0:T(1,128)S(1)}) custom-call(s32[1,2]{1,0:T(1,128)S(1)} %add_bitcast_fusion.place_ref, bf16[2048,768]{1,0:T(8,128)(2,1)S(1)} %bitcast.16, bf16[2048,768]{1,0:T(8,128)(2,1)} %collective-permute-done.sib_hbm, f32[3,2048]{1,0:T(4,128)S(1)} %get-tuple-element.20.info_ref, ...), custom_call_target="tpu_custom_call" | custom-call | flops 3221225472 | bytes 6000000 | tf_op jit(solution)/shard_map/pallas_call | solution.py:294
  109.6 0.0 copy-start.2
  109.6 0.1 collective-permute-start.2
  109.7 0.9 shard_map.53
  110.7 0.2 collective-permute-done.2.taken_ref
  110.9 0.6 shard_map.54
  111.4 0.2 collective-permute-start.3
  111.6 3.2 %collective-permute-start.4 = (f32[16,128]{1,0:T(8,128)S(1)}, f32[16,128]{1,0:T(8,128)S(1)}, u32[]{:S(2)}, u32[]{:S(2)}) collective-permute-start(f32[16,128]{1,0:T(8,128)S(1)} %get-tuple-element.28), channel_id=1, source_target_pairs={{0,2},{1,3},{2,0},{3,1},{4,6},{5,7},{6,4},{7,5},{8,10},{9,11},{10,... | collective-permute-start | bytes 24584 | tf_op jit(solution)/shard_map/ppermute | solution.py:318
  114.8 0.4 collective-permute-start.5
  115.2 0.0 collective-permute-done.3.refs_1_
  115.2 1.6 %collective-permute-done.4.refs_2_ = f32[16,128]{1,0:T(8,128)S(1)} collective-permute-done((f32[16,128]{1,0:T(8,128)S(1)}, f32[16,128]{1,0:T(8,128)S(1)}, u32[]{:S(2)}, u32[]{:S(2)}) %collective-permute-start.4) | collective-permute-done | bytes 8224 | tf_op jit(solution)/shard_map/ppermute | solution.py:318
  116.8 1.7 %collective-permute-done.5.refs_3_ = f32[16,128]{1,0:T(8,128)S(1)} collective-permute-done((f32[16,128]{1,0:T(8,128)S(1)}, f32[16,128]{1,0:T(8,128)S(1)}, u32[]{:S(2)}, u32[]{:S(2)}) %collective-permute-start.5) | collective-permute-done | bytes 8224 | tf_op jit(solution)/shard_map/ppermute | solution.py:318
  118.5 0.1 shard_map.55
  118.6 14.5 %all_to_all.17 = f32[32,1,128]{2,1,0:T(1,128)S(1)} all-to-all(f32[32,1,128]{2,1,0:T(1,128)S(1)} %bitcast.19), channel_id=1, replica_groups=mesh['y'=4,'z'=8,'core'=2,'x'=4] {'z','y'}, dimensions={0} | all-to-all | bytes 32768 | tf_op jit(solution)/shard_map/all_to_all | solution.py:320
  133.1 0.0 copy-done.2
  133.1 1.6 %shard_map.56 = (f32[1,1024]{1,0:T(1,128)}, f32[1,1024]{1,0:T(1,128)}, f32[2,768]{1,0:T(2,128)}) custom-call(s32[1,2]{1,0:T(1,128)S(1)} %add_bitcast_fusion.place_ref, s32[1,1024]{1,0:T(1,128)S(1)} %bitcast.22, s32[1,1024]{1,0:T(1,128)S(1)} %get-tuple-element.18.rank_ref, f32[32,128]{1,0:T(8,128)S(1)} %bitcast.20, f32[16,128]{1,0:T(8,128)S(1)} %get-tuple-element.26.refs_0_, ...), custom_call_target="tpu_custom_call" | custom-call | flops 100000000 | bytes 6000000 | tf_op jit(solution)/shard_map/pallas_call | solution.py:321
Async XLA Ops:
  0.6 1.4 %copy-start = (bf16[1024,768]{1,0:T(8,128)(2,1)S(1)}, bf16[1024,768]{1,0:T(8,128)(2,1)}, u32[]{:S(2)}) copy-start(bf16[1024,768]{1,0:T(8,128)(2,1)} %x_hbm.1) | copy-start | bytes 4718596
  2.0 0.7 copy-start.1
  96.4 6.2 %collective-permute-start = (bf16[2048,768]{1,0:T(8,128)(2,1)S(1)}, bf16[2048,768]{1,0:T(8,128)(2,1)}, u32[]{:S(2)}, u32[]{:S(2)}) collective-permute-start(bf16[2048,768]{1,0:T(8,128)(2,1)S(1)} %bitcast.13), channel_id=1, source_target_pairs={{0,4},{4,0},{1,5},{5,1},{2,6},{6,2},{3,7},{7,3},{8,12},{12,8},{9,1... | collective-permute-start | bytes 9437192 | tf_op jit(solution)/shard_map/ppermute | solution.py:284
  99.2 3.4 %collective-permute-start.1 = (f32[3,2048]{1,0:T(4,128)S(1)}, f32[3,2048]{1,0:T(4,128)S(1)}, u32[]{:S(2)}, u32[]{:S(2)}) collective-permute-start(f32[3,2048]{1,0:T(4,128)S(1)} %get-tuple-element.20.info_ref), channel_id=1, source_target_pairs={{0,4},{4,0},{1,5},{5,1},{2,6},{6,2},{3,7},{7,3},{8,12},{12,8},{9,1... | collective-permute-start | bytes 73736 | tf_op jit(solution)/shard_map/ppermute | solution.py:287
  109.6 23.5 %copy-start.2 = (s32[1024,1]{0,1:T(1,128)S(1)}, s32[1024,1]{0,1:T(1,128)}, u32[]{:S(2)}) copy-start(s32[1024,1]{0,1:T(1,128)} %param.3) | copy-start | bytes 12292
  109.6 1.3 collective-permute-start.2
  111.4 3.7 %collective-permute-start.3 = (f32[16,128]{1,0:T(8,128)S(1)}, f32[16,128]{1,0:T(8,128)S(1)}, u32[]{:S(2)}, u32[]{:S(2)}) collective-permute-start(f32[16,128]{1,0:T(8,128)S(1)} %get-tuple-element.27), channel_id=1, source_target_pairs={{0,1},{1,2},{2,3},{3,0},{4,5},{5,6},{6,7},{7,4},{8,9},{9,10},{10,1... | collective-permute-start | bytes 24584 | tf_op jit(solution)/shard_map/ppermute | solution.py:318
  111.6 5.2 %collective-permute-start.4 = (f32[16,128]{1,0:T(8,128)S(1)}, f32[16,128]{1,0:T(8,128)S(1)}, u32[]{:S(2)}, u32[]{:S(2)}) collective-permute-start(f32[16,128]{1,0:T(8,128)S(1)} %get-tuple-element.28), channel_id=1, source_target_pairs={{0,2},{1,3},{2,0},{3,1},{4,6},{5,7},{6,4},{7,5},{8,10},{9,11},{10,... | collective-permute-start | bytes 24584 | tf_op jit(solution)/shard_map/ppermute | solution.py:318
  114.8 3.7 %collective-permute-start.5 = (f32[16,128]{1,0:T(8,128)S(1)}, f32[16,128]{1,0:T(8,128)S(1)}, u32[]{:S(2)}, u32[]{:S(2)}) collective-permute-start(f32[16,128]{1,0:T(8,128)S(1)} %get-tuple-element.29), channel_id=1, source_target_pairs={{0,3},{1,0},{2,1},{3,2},{4,7},{5,4},{6,5},{7,6},{8,11},{9,8},{10,9... | collective-permute-start | bytes 24584 | tf_op jit(solution)/shard_map/ppermute | solution.py:318

commit v14 on v12

--- a/solution.py
+++ b/solution.py
@@ -130,10 +130,10 @@
 
 
 def across_kernel(
-    place_ref, x_ref, sib_hbm, info_ref, sib_info_ref, before_ref,
+    x_ref, sib_hbm, info_ref, sib_info_ref, before_ref,
     best_ref, give_ref, sib_ref, turned_ref, sems,
 ):
-    core = place_ref[0, 1]
+    core = lax.axis_index("core")
 
     def rows(k):
         return pl.ds(pl.multiple_of(((core + k) & 3) * TILE, TILE), TILE)
@@ -201,12 +201,12 @@
     centre_ref[...] = toward * info_ref[0:1, :] * scale / WIDTH
 
 
-def lines_kernel(place_ref, best_ref, taken_ref, info_ref, centre_ref, mean_ref, *refs):
+def lines_kernel(best_ref, taken_ref, info_ref, centre_ref, mean_ref, *refs):
     out_refs, near_ref = refs[:XS], refs[XS]
     best = jnp.maximum(best_ref[...], taken_ref[...])
     near_ref[...] = jnp.maximum(-1.0, best * info_ref[0:1, :] / WIDTH)
     for k in range(XS):
-        first = ((place_ref[0, 0] + k) & 3) * TILE
+        first = ((lax.axis_index("x") + k) & 3) * TILE
         for line in range(4):
             lane = pl.ds(pl.multiple_of(first + line * 128, 128), 128)
             out_refs[k][line : line + 1, :] = near_ref[:, lane]
@@ -228,10 +228,11 @@
         out_ref[8 * s : 8 * (s + 1), :] = out
 
 
-def unpack_kernel(place_ref, ids_ref, rank_ref, back_ref, *refs):
+def unpack_kernel(ids_ref, rank_ref, back_ref, *refs):
     came, (near_ref, centre_ref, mean_ref) = refs[:XS], refs[XS:]
+    x, core = lax.axis_index("x"), lax.axis_index("core")
     for k in range(2):
-        offset = (place_ref[0, 0] - 2 * place_ref[0, 1] - k) & 3
+        offset = (x - 2 * core - k) & 3
         folded = sum(jnp.where(offset == i, ref[8:16, :], 0.0) for i, ref in enumerate(came))
         for j in range(WIDTH // 128):
             mean_ref[k : k + 1, j * 128 : (j + 1) * 128] = folded[j : j + 1]
@@ -241,7 +242,7 @@
     parts = jnp.concatenate(split3(back_ref[...]), axis=1)
     picked = lax.dot_general(parts, onehot, TN, preferred_element_type=F32)
     picked = picked[0:128] + picked[128:256] + picked[256:384]
-    place = ((place_ref[0, 0] - ids) & 3) * PAIR + rank_ref[...]
+    place = ((x - ids) & 3) * PAIR + rank_ref[...]
     line = iota((128, ROWS), 0)
     near_ref[...] = jnp.sum(jnp.where(line == place, picked, 0.0), axis=0, keepdims=True)
     centre_ref[...] = jnp.sum(
@@ -287,9 +288,6 @@
     sib_info = lax.ppermute(info, "core", swap)
     fold = pltpu.VMEM((TILE, 128), F32)
     best = call(own_kernel, row, block * 3 / 8, (fold,))(mine, info, best)
-    axes = [lax.axis_index("x"), lax.axis_index("core")]
-    place = jnp.stack(axes).astype(jnp.int32).reshape(1, 2)
-    scalars = pl.BlockSpec(memory_space=pltpu.SMEM)
     line = struct((16, 128), F32)
     best, give = call(
         across_kernel,
@@ -300,8 +298,8 @@
             pltpu.VMEM((2, SLOTS), F32),
             pltpu.SemaphoreType.DMA((TILES,)),
         ),
-        in_specs=[scalars, here, pl.BlockSpec(memory_space=pltpu.HBM), here, here, here],
-    )(place, mine, sib, info, sib_info, best)
+        in_specs=[here, pl.BlockSpec(memory_space=pltpu.HBM), here, here, here],
+    )(mine, sib, info, sib_info, best)
     taken = lax.ppermute(give, "core", swap)
     centre, mean = call(
         centre_kernel, (row, struct((8, 128), F32)), block / 8
@@ -311,8 +309,7 @@
         (line,) * XS,
         1e7,
         (pltpu.VMEM((1, SLOTS), F32),),
-        in_specs=[scalars] + [here] * 5,
-    )(place, best, taken, info, centre, mean)
+    )(best, taken, info, centre, mean)
     came = [outs[0]]
     for k in range(1, XS):
         came.append(lax.ppermute(outs[k], "x", [(i, (i + k) % XS) for i in range(XS)]))
@@ -322,8 +319,7 @@
         unpack_kernel,
         (struct((1, ROWS), F32), struct((1, ROWS), F32), struct((2, WIDTH), F32)),
         1e8,
-        in_specs=[scalars] + [here] * (3 + XS),
-    )(place, ids, rank, back, *came)
+    )(ids, rank, back, *came)
     return near.reshape(ROWS), centre.reshape(ROWS), means
 
 

time: 134 us -> 133 us (level)
  Pallas kernels: 18.8 us -> 17.4 us
  transfers between devices with their start and end apart: 6 -> 6, of which waited for: 4 -> 3; matrix products, arithmetic and copies ran while one was open for 0% -> 0% of each run, Pallas kernels for 4% -> 5%
where the time goes in v14:
time: 133 us; the launch traced here: 132 us
  blocking collectives  104 us (78%)
  Pallas kernels  17.4 us (13%)
  starting transfers between devices  4.62 us (3%)
  waiting for transfers between devices  3.51 us (3%)
  local copies, waits for them, and re-layouts  2.09 us (2%)
    all_to_all x1, blocking collectives, shards(): lax.all_to_all(send.reshape(CHIPS, CAP, WIDTH), chips, 0, 0, tiled=True)  89.5 us
    all_to_all x1, blocking collectives, shards(): back = lax.all_to_all(out, ('z', 'y'), 0, 0, tiled=True)  14.5 us
    pallas_call x1, Pallas kernels, shards(): call(across_kernel, (row, row), block / 2, (pltpu.VMEM((SLOTS, WIDTH), BF...  6.05 us
    pallas_call x1, Pallas kernels, shards(): call(pack_kernel, (struct((SLOTS, WIDTH), BF16), struct((1, ROWS), jnp.in...  4.1 us
    ppermute x3, starting transfers between devices, shards(): lax.ppermute(outs[k], 'x', [(i, (i + k) % XS) for i in range(XS)])  3.73 us
    ppermute x3, waiting for transfers between devices, shards(): lax.ppermute(outs[k], 'x', [(i, (i + k) % XS) for i in range(XS)])  3.3 us
    pallas_call x1, Pallas kernels, shards(): call(diagonal_kernel, (struct((3, SLOTS), F32), row), block / 4)(mine)  2.81 us
  transfers between devices with their start and end apart: 6, of which 3 were waited for; matrix products, arithmetic and copies ran while one was open for 0% of the time, Pallas kernels for 5%

profile of v14, /device:TPU:2, one launch (start us, length us, event | category | flops | bytes accessed | tf_op | source)
XLA Modules:
  0.0 132.4 jit_solution(7098474074247969673)
XLA Ops:
  0.6 0.0 copy-start
  0.6 1.4 %copy-done = bf16[1024,768]{1,0:T(8,128)(2,1)S(1)} copy-done((bf16[1024,768]{1,0:T(8,128)(2,1)S(1)}, bf16[1024,768]{1,0:T(8,128)(2,1)}, u32[]{:S(2)}) %copy-start) | copy-done | bytes 1572888
  2.0 0.0 copy-start.1
  2.0 0.7 copy-done.1
  2.7 4.1 %shard_map.49 = (bf16[2048,768]{1,0:T(8,128)(2,1)S(1)}, s32[1,1024]{1,0:T(1,128)S(1)}) custom-call(s32[1,1024]{1,0:T(1,128)S(1)} %bitcast.17, bf16[1024,768]{1,0:T(8,128)(2,1)S(1)} %copy-done), custom_call_target="tpu_custom_call" | custom-call | flops 3221225472 | bytes 6000000 | tf_op jit(solution)/shard_map/pallas_call | solution.py:274
  6.8 89.5 %all_to_all.16 = bf16[128,16,768]{2,1,0:T(8,128)(2,1)S(1)} all-to-all(bf16[128,16,768]{2,1,0:T(8,128)(2,1)S(1)} %bitcast.14), channel_id=1, replica_groups=mesh['y'=4,'z'=8,'core'=2,'x'=4] {'x','z','y'}, dimensions={0} | all-to-all | bytes 6291456 | tf_op jit(solution)/shard_map/all_to_all | solution.py:282
  96.4 0.0 collective-permute-start
  96.4 2.8 %shard_map.50 = (f32[3,2048]{1,0:T(4,128)S(1)}, f32[1,2048]{1,0:T(1,128)S(1)}) custom-call(bf16[2048,768]{1,0:T(8,128)(2,1)S(1)} %bitcast.10), custom_call_target="tpu_custom_call" | custom-call | flops 1610612736 | bytes 6000000 | tf_op jit(solution)/shard_map/pallas_call | solution.py:287
  99.2 0.8 collective-permute-start.1
  100.0 2.3 %shard_map.51.before_ref = f32[1,2048]{1,0:T(1,128)S(1)} custom-call(bf16[2048,768]{1,0:T(8,128)(2,1)S(1)} %bitcast.11, f32[3,2048]{1,0:T(4,128)S(1)} %get-tuple-element.20.info_ref, f32[1,2048]{1,0:T(1,128)S(1)} %get-tuple-element.21.before_ref), custom_call_target="tpu_custom_call" | custom-call | flops 2415919104 | bytes 6000000 | tf_op jit(solution)/shard_map/pallas_call | solution.py:290
  102.3 0.0 collective-permute-done.1.sib_info_ref
  102.3 0.0 collective-permute-done.sib_hbm
  102.3 6.1 %shard_map.52 = (f32[1,2048]{1,0:T(1,128)S(1)}, f32[1,2048]{1,0:T(1,128)S(1)}) custom-call(bf16[2048,768]{1,0:T(8,128)(2,1)S(1)} %bitcast.12, bf16[2048,768]{1,0:T(8,128)(2,1)S(1)} %collective-permute-done.sib_hbm, f32[3,2048]{1,0:T(4,128)S(1)} %get-tuple-element.20.info_ref, f32[3,2048]{1,0:T(4,128)S(1)} %collective-permute-done.1.sib_info_ref, ...), custom_call_target="tpu_custom_call" | custom-call | flops 3221225472 | bytes 6000000 | tf_op jit(solution)/shard_map/pallas_call | solution.py:292
  108.4 0.0 copy-start.2
  108.4 0.1 collective-permute-start.2
  108.5 0.9 shard_map.53
  109.4 0.2 collective-permute-done.2.taken_ref
  109.7 0.2 collective-permute-start.3
  109.9 3.2 %collective-permute-start.4 = (f32[16,128]{1,0:T(8,128)S(1)}, f32[16,128]{1,0:T(8,128)S(1)}, u32[]{:S(2)}, u32[]{:S(2)}) collective-permute-start(f32[16,128]{1,0:T(8,128)S(1)} %get-tuple-element.28), channel_id=1, source_target_pairs={{0,2},{1,3},{2,0},{3,1},{4,6},{5,7},{6,4},{7,5},{8,10},{9,11},{10,... | collective-permute-start | bytes 24584 | tf_op jit(solution)/shard_map/ppermute | solution.py:315
  113.0 0.4 collective-permute-start.5
  113.4 0.0 collective-permute-done.3.refs_1_
  113.4 1.6 %collective-permute-done.4.refs_2_ = f32[16,128]{1,0:T(8,128)S(1)} collective-permute-done((f32[16,128]{1,0:T(8,128)S(1)}, f32[16,128]{1,0:T(8,128)S(1)}, u32[]{:S(2)}, u32[]{:S(2)}) %collective-permute-start.4) | collective-permute-done | bytes 8224 | tf_op jit(solution)/shard_map/ppermute | solution.py:315
  115.0 1.7 %collective-permute-done.5.refs_3_ = f32[16,128]{1,0:T(8,128)S(1)} collective-permute-done((f32[16,128]{1,0:T(8,128)S(1)}, f32[16,128]{1,0:T(8,128)S(1)}, u32[]{:S(2)}, u32[]{:S(2)}) %collective-permute-start.5) | collective-permute-done | bytes 8224 | tf_op jit(solution)/shard_map/ppermute | solution.py:315
  116.7 0.1 shard_map.55
  116.8 14.5 %all_to_all.17 = f32[32,1,128]{2,1,0:T(1,128)S(1)} all-to-all(f32[32,1,128]{2,1,0:T(1,128)S(1)} %bitcast.15), channel_id=1, replica_groups=mesh['y'=4,'z'=8,'core'=2,'x'=4] {'z','y'}, dimensions={0} | all-to-all | bytes 32768 | tf_op jit(solution)/shard_map/all_to_all | solution.py:317
  131.3 0.0 copy-done.2
  131.3 1.0 shard_map.56
  (1 shorter events, 0.0 us)
Async XLA Ops:
  0.6 1.4 %copy-start = (bf16[1024,768]{1,0:T(8,128)(2,1)S(1)}, bf16[1024,768]{1,0:T(8,128)(2,1)}, u32[]{:S(2)}) copy-start(bf16[1024,768]{1,0:T(8,128)(2,1)} %x_hbm.1) | copy-start | bytes 4718596
  2.0 0.7 copy-start.1
  96.4 5.9 %collective-permute-start = (bf16[2048,768]{1,0:T(8,128)(2,1)S(1)}, bf16[2048,768]{1,0:T(8,128)(2,1)S(1)}, u32[]{:S(2)}, u32[]{:S(2)}) collective-permute-start(bf16[2048,768]{1,0:T(8,128)(2,1)S(1)} %bitcast.9), channel_id=1, source_target_pairs={{0,4},{4,0},{1,5},{5,1},{2,6},{6,2},{3,7},{7,3},{8,12},{12,8},{9,1... | collective-permute-start | bytes 9437192 | tf_op jit(solution)/shard_map/ppermute | solution.py:285
  99.2 3.1 %collective-permute-start.1 = (f32[3,2048]{1,0:T(4,128)S(1)}, f32[3,2048]{1,0:T(4,128)S(1)}, u32[]{:S(2)}, u32[]{:S(2)}) collective-permute-start(f32[3,2048]{1,0:T(4,128)S(1)} %get-tuple-element.20.info_ref), channel_id=1, source_target_pairs={{0,4},{4,0},{1,5},{5,1},{2,6},{6,2},{3,7},{7,3},{8,12},{12,8},{9,1... | collective-permute-start | bytes 73736 | tf_op jit(solution)/shard_map/ppermute | solution.py:288
  108.4 23.0 %copy-start.2 = (s32[1024,1]{0,1:T(1,128)S(1)}, s32[1024,1]{0,1:T(1,128)}, u32[]{:S(2)}) copy-start(s32[1024,1]{0,1:T(1,128)} %param.3) | copy-start | bytes 12292
  108.4 1.3 collective-permute-start.2
  109.7 3.7 %collective-permute-start.3 = (f32[16,128]{1,0:T(8,128)S(1)}, f32[16,128]{1,0:T(8,128)S(1)}, u32[]{:S(2)}, u32[]{:S(2)}) collective-permute-start(f32[16,128]{1,0:T(8,128)S(1)} %get-tuple-element.27), channel_id=1, source_target_pairs={{0,1},{1,2},{2,3},{3,0},{4,5},{5,6},{6,7},{7,4},{8,9},{9,10},{10,1... | collective-permute-start | bytes 24584 | tf_op jit(solution)/shard_map/ppermute | solution.py:315
  109.9 5.2 %collective-permute-start.4 = (f32[16,128]{1,0:T(8,128)S(1)}, f32[16,128]{1,0:T(8,128)S(1)}, u32[]{:S(2)}, u32[]{:S(2)}) collective-permute-start(f32[16,128]{1,0:T(8,128)S(1)} %get-tuple-element.28), channel_id=1, source_target_pairs={{0,2},{1,3},{2,0},{3,1},{4,6},{5,7},{6,4},{7,5},{8,10},{9,11},{10,... | collective-permute-start | bytes 24584 | tf_op jit(solution)/shard_map/ppermute | solution.py:315
  113.0 3.7 %collective-permute-start.5 = (f32[16,128]{1,0:T(8,128)S(1)}, f32[16,128]{1,0:T(8,128)S(1)}, u32[]{:S(2)}, u32[]{:S(2)}) collective-permute-start(f32[16,128]{1,0:T(8,128)S(1)} %get-tuple-element.29), channel_id=1, source_target_pairs={{0,3},{1,0},{2,1},{3,2},{4,7},{5,4},{6,5},{7,6},{8,11},{9,8},{10,9... | collective-permute-start | bytes 24584 | tf_op jit(solution)/shard_map/ppermute | solution.py:315

commit v15 on v14

--- a/solution.py
+++ b/solution.py
@@ -74,9 +74,7 @@
     return ref[row : row + 1, i * TILE : (i + 1) * TILE]
 
 
-def pack_kernel(ids_ref, x_hbm, send_ref, rank_ref, x_ref, sem):
-    copy = pltpu.make_async_copy(x_hbm, x_ref, sem)
-    copy.start()
+def rank_kernel(ids_ref, rank_ref, slot_ref):
     chip = chip_of(ids_ref[...])
     same = iota((CHIPS, ROWS), 0) == chip
     onehot = same.astype(F32).astype(BF16)
@@ -84,9 +82,12 @@
     earlier = jnp.dot(onehot, before, preferred_element_type=F32)
     rank = jnp.sum(jnp.where(same, earlier, 0.0), axis=0, keepdims=True).astype(jnp.int32)
     rank_ref[...] = rank
-    position = chip * CAP + rank
+    slot_ref[...] = chip * CAP + rank
+
+
+def pack_kernel(slot_ref, x_ref, send_ref):
+    position = slot_ref[...]
     step = 256
-    copy.wait()
     for start in range(0, SLOTS, step):
         pick = (iota((step, ROWS), 0) + start == position).astype(F32)
         live = jnp.sum(pick, axis=1, keepdims=True)
@@ -271,13 +272,11 @@
     ids = cluster_ids.reshape(1, ROWS)
     block = 2 * SLOTS * SLOTS * WIDTH
     here = pl.BlockSpec(memory_space=pltpu.VMEM)
-    send, rank = call(
-        pack_kernel,
-        (struct((SLOTS, WIDTH), BF16), struct((1, ROWS), jnp.int32)),
-        2 * SLOTS * ROWS * WIDTH,
-        (pltpu.VMEM((ROWS, WIDTH), BF16), pltpu.SemaphoreType.DMA),
-        in_specs=[here, pl.BlockSpec(memory_space=pltpu.HBM)],
-    )(ids, embeddings)
+    whole = struct((1, ROWS), jnp.int32)
+    rank, slot = call(rank_kernel, (whole, whole), 3e10)(ids)
+    send = call(pack_kernel, struct((SLOTS, WIDTH), BF16), 2 * SLOTS * ROWS * WIDTH)(
+        slot, embeddings
+    )
     chips = ("x", "z", "y")
     mine = lax.all_to_all(send.reshape(CHIPS, CAP, WIDTH), chips, 0, 0, tiled=True)
     mine = mine.reshape(SLOTS, WIDTH)

time: 133 us -> 132 us (level)
    pallas_call x1 -> x2, Pallas kernels: 4.1 us -> 4.07 us  [the longest x1 3.61 us: shards(): call(pack_kernel, struct((SLOTS, WIDTH), BF16), 2 * SLOTS * ROWS * WIDTH)]
where the time goes in v15:
time: 132 us
  blocking collectives  104 us (79%)
  Pallas kernels  17.4 us (13%)
  starting transfers between devices  4.63 us (4%)
  waiting for transfers between devices  3.5 us (3%)
  local copies, waits for them, and re-layouts  1.63 us (1%)
    all_to_all x1, blocking collectives, shards(): lax.all_to_all(send.reshape(CHIPS, CAP, WIDTH), chips, 0, 0, tiled=True)  89.5 us
    all_to_all x1, blocking collectives, shards(): back = lax.all_to_all(out, ('z', 'y'), 0, 0, tiled=True)  14.5 us
    pallas_call x1, Pallas kernels, shards(): call(across_kernel, (row, row), block / 2, (pltpu.VMEM((SLOTS, WIDTH), BF...  6.05 us
    ppermute x3, starting transfers between devices, shards(): lax.ppermute(outs[k], 'x', [(i, (i + k) % XS) for i in range(XS)])  3.73 us
    pallas_call x1, Pallas kernels, shards(): call(pack_kernel, struct((SLOTS, WIDTH), BF16), 2 * SLOTS * ROWS * WIDTH)  3.61 us
    ppermute x3, waiting for transfers between devices, shards(): lax.ppermute(outs[k], 'x', [(i, (i + k) % XS) for i in range(XS)])  3.31 us
    pallas_call x1, Pallas kernels, shards(): call(diagonal_kernel, (struct((3, SLOTS), F32), row), block / 4)(mine)  2.81 us
  transfers between devices with their start and end apart: 6, of which 3 were waited for; matrix products, arithmetic and copies ran while one was open for 0% of the time, Pallas kernels for 5%

profile of v15, /device:TPU:2, one launch (start us, length us, event | category | flops | bytes accessed | tf_op | source)
XLA Modules:
  0.0 131.9 jit_solution(10354150765362660537)
XLA Ops:
  0.6 0.0 copy-start.1
  0.6 0.7 copy-done.1
  1.3 0.0 copy-start
  1.3 0.5 shard_map.49
  1.8 0.9 copy-done
  2.7 3.6 %shard_map.50 = bf16[2048,768]{1,0:T(8,128)(2,1)S(1)} custom-call(s32[1,1024]{1,0:T(1,128)S(1)} %get-tuple-element.19.slot_ref, bf16[1024,768]{1,0:T(8,128)(2,1)S(1)} %copy-done), custom_call_target="tpu_custom_call" | custom-call | flops 3221225472 | bytes 6000000 | tf_op jit(solution)/shard_map/pallas_call | solution.py:277
  6.3 89.5 %all_to_all.16 = bf16[128,16,768]{2,1,0:T(8,128)(2,1)S(1)} all-to-all(bf16[128,16,768]{2,1,0:T(8,128)(2,1)S(1)} %bitcast.14), channel_id=1, replica_groups=mesh['y'=4,'z'=8,'core'=2,'x'=4] {'x','z','y'}, dimensions={0} | all-to-all | bytes 6291456 | tf_op jit(solution)/shard_map/all_to_all | solution.py:281
  95.9 0.0 collective-permute-start
  95.9 2.8 %shard_map.51 = (f32[3,2048]{1,0:T(4,128)S(1)}, f32[1,2048]{1,0:T(1,128)S(1)}) custom-call(bf16[2048,768]{1,0:T(8,128)(2,1)S(1)} %bitcast.10), custom_call_target="tpu_custom_call" | custom-call | flops 1610612736 | bytes 6000000 | tf_op jit(solution)/shard_map/pallas_call | solution.py:286
  98.7 0.8 collective-permute-start.1
  99.5 2.3 %shard_map.52.before_ref = f32[1,2048]{1,0:T(1,128)S(1)} custom-call(bf16[2048,768]{1,0:T(8,128)(2,1)S(1)} %bitcast.11, f32[3,2048]{1,0:T(4,128)S(1)} %get-tuple-element.20.info_ref, f32[1,2048]{1,0:T(1,128)S(1)} %get-tuple-element.21.before_ref), custom_call_target="tpu_custom_call" | custom-call | flops 2415919104 | bytes 6000000 | tf_op jit(solution)/shard_map/pallas_call | solution.py:289
  101.8 0.0 collective-permute-done.1.sib_info_ref
  101.8 0.0 collective-permute-done.sib_hbm
  101.8 6.0 %shard_map.53 = (f32[1,2048]{1,0:T(1,128)S(1)}, f32[1,2048]{1,0:T(1,128)S(1)}) custom-call(bf16[2048,768]{1,0:T(8,128)(2,1)S(1)} %bitcast.12, bf16[2048,768]{1,0:T(8,128)(2,1)S(1)} %collective-permute-done.sib_hbm, f32[3,2048]{1,0:T(4,128)S(1)} %get-tuple-element.20.info_ref, f32[3,2048]{1,0:T(4,128)S(1)} %collective-permute-done.1.sib_info_ref, ...), custom_call_target="tpu_custom_call" | custom-call | flops 3221225472 | bytes 6000000 | tf_op jit(solution)/shard_map/pallas_call | solution.py:291
  107.9 0.0 copy-start.2
  107.9 0.1 collective-permute-start.2
  108.0 0.9 shard_map.54
  108.9 0.2 collective-permute-done.2.taken_ref
  109.2 0.2 collective-permute-start.3
  109.4 3.2 %collective-permute-start.4 = (f32[16,128]{1,0:T(8,128)S(1)}, f32[16,128]{1,0:T(8,128)S(1)}, u32[]{:S(2)}, u32[]{:S(2)}) collective-permute-start(f32[16,128]{1,0:T(8,128)S(1)} %get-tuple-element.28), channel_id=1, source_target_pairs={{0,2},{1,3},{2,0},{3,1},{4,6},{5,7},{6,4},{7,5},{8,10},{9,11},{10,... | collective-permute-start | bytes 24584 | tf_op jit(solution)/shard_map/ppermute | solution.py:314
  112.5 0.3 collective-permute-start.5
  112.9 0.0 collective-permute-done.3.refs_1_
  112.9 1.6 %collective-permute-done.4.refs_2_ = f32[16,128]{1,0:T(8,128)S(1)} collective-permute-done((f32[16,128]{1,0:T(8,128)S(1)}, f32[16,128]{1,0:T(8,128)S(1)}, u32[]{:S(2)}, u32[]{:S(2)}) %collective-permute-start.4) | collective-permute-done | bytes 8224 | tf_op jit(solution)/shard_map/ppermute | solution.py:314
  114.5 1.7 %collective-permute-done.5.refs_3_ = f32[16,128]{1,0:T(8,128)S(1)} collective-permute-done((f32[16,128]{1,0:T(8,128)S(1)}, f32[16,128]{1,0:T(8,128)S(1)}, u32[]{:S(2)}, u32[]{:S(2)}) %collective-permute-start.5) | collective-permute-done | bytes 8224 | tf_op jit(solution)/shard_map/ppermute | solution.py:314
  116.2 0.1 shard_map.56
  116.3 14.5 %all_to_all.17 = f32[32,1,128]{2,1,0:T(1,128)S(1)} all-to-all(f32[32,1,128]{2,1,0:T(1,128)S(1)} %bitcast.15), channel_id=1, replica_groups=mesh['y'=4,'z'=8,'core'=2,'x'=4] {'z','y'}, dimensions={0} | all-to-all | bytes 32768 | tf_op jit(solution)/shard_map/all_to_all | solution.py:316
  130.8 0.0 copy-done.2
  130.8 1.0 shard_map.57
  (1 shorter events, 0.0 us)
Async XLA Ops:
  0.6 0.7 copy-start.1
  1.3 1.4 %copy-start = (bf16[1024,768]{1,0:T(8,128)(2,1)S(1)}, bf16[1024,768]{1,0:T(8,128)(2,1)}, u32[]{:S(2)}) copy-start(bf16[1024,768]{1,0:T(8,128)(2,1)} %x_ref.1) | copy-start | bytes 4718596
  95.9 5.9 %collective-permute-start = (bf16[2048,768]{1,0:T(8,128)(2,1)S(1)}, bf16[2048,768]{1,0:T(8,128)(2,1)S(1)}, u32[]{:S(2)}, u32[]{:S(2)}) collective-permute-start(bf16[2048,768]{1,0:T(8,128)(2,1)S(1)} %bitcast.9), channel_id=1, source_target_pairs={{0,4},{4,0},{1,5},{5,1},{2,6},{6,2},{3,7},{7,3},{8,12},{12,8},{9,1... | collective-permute-start | bytes 9437192 | tf_op jit(solution)/shard_map/ppermute | solution.py:284
  98.7 3.1 %collective-permute-start.1 = (f32[3,2048]{1,0:T(4,128)S(1)}, f32[3,2048]{1,0:T(4,128)S(1)}, u32[]{:S(2)}, u32[]{:S(2)}) collective-permute-start(f32[3,2048]{1,0:T(4,128)S(1)} %get-tuple-element.20.info_ref), channel_id=1, source_target_pairs={{0,4},{4,0},{1,5},{5,1},{2,6},{6,2},{3,7},{7,3},{8,12},{12,8},{9,1... | collective-permute-start | bytes 73736 | tf_op jit(solution)/shard_map/ppermute | solution.py:287
  107.9 23.0 %copy-start.2 = (s32[1024,1]{0,1:T(1,128)S(1)}, s32[1024,1]{0,1:T(1,128)}, u32[]{:S(2)}) copy-start(s32[1024,1]{0,1:T(1,128)} %param.3) | copy-start | bytes 12292
  107.9 1.3 collective-permute-start.2
  109.2 3.7 %collective-permute-start.3 = (f32[16,128]{1,0:T(8,128)S(1)}, f32[16,128]{1,0:T(8,128)S(1)}, u32[]{:S(2)}, u32[]{:S(2)}) collective-permute-start(f32[16,128]{1,0:T(8,128)S(1)} %get-tuple-element.27), channel_id=1, source_target_pairs={{0,1},{1,2},{2,3},{3,0},{4,5},{5,6},{6,7},{7,4},{8,9},{9,10},{10,1... | collective-permute-start | bytes 24584 | tf_op jit(solution)/shard_map/ppermute | solution.py:314
  109.4 5.2 %collective-permute-start.4 = (f32[16,128]{1,0:T(8,128)S(1)}, f32[16,128]{1,0:T(8,128)S(1)}, u32[]{:S(2)}, u32[]{:S(2)}) collective-permute-start(f32[16,128]{1,0:T(8,128)S(1)} %get-tuple-element.28), channel_id=1, source_target_pairs={{0,2},{1,3},{2,0},{3,1},{4,6},{5,7},{6,4},{7,5},{8,10},{9,11},{10,... | collective-permute-start | bytes 24584 | tf_op jit(solution)/shard_map/ppermute | solution.py:314
  112.5 3.7 %collective-permute-start.5 = (f32[16,128]{1,0:T(8,128)S(1)}, f32[16,128]{1,0:T(8,128)S(1)}, u32[]{:S(2)}, u32[]{:S(2)}) collective-permute-start(f32[16,128]{1,0:T(8,128)S(1)} %get-tuple-element.29), channel_id=1, source_target_pairs={{0,3},{1,0},{2,1},{3,2},{4,7},{5,4},{6,5},{7,6},{8,11},{9,8},{10,9... | collective-permute-start | bytes 24584 | tf_op jit(solution)/shard_map/ppermute | solution.py:314

commit v16 on v15

--- a/solution.py
+++ b/solution.py
@@ -74,8 +74,8 @@
     return ref[row : row + 1, i * TILE : (i + 1) * TILE]
 
 
-def rank_kernel(ids_ref, rank_ref, slot_ref):
-    chip = chip_of(ids_ref[...])
+def rank_kernel(chip_ref, rank_ref, slot_ref):
+    chip = chip_ref[...]
     same = iota((CHIPS, ROWS), 0) == chip
     onehot = same.astype(F32).astype(BF16)
     before = (iota((ROWS, ROWS), 0) < iota((ROWS, ROWS), 1)).astype(F32).astype(BF16)
@@ -115,7 +115,7 @@
         best_ref[:, i * TILE : (i + 1) * TILE] = to_row(best)
 
 
-def own_kernel(x_ref, info_ref, before_ref, best_ref, fold_ref):
+def own_kernel(x_ref, info_ref, before_ref, best_ref):
     best_ref[...] = before_ref[...]
     for i in range(TILES - 2):
         inv = to_column(lanes(info_ref, 0, i))
@@ -123,10 +123,10 @@
         for j in range(i + 1, TILES - i):
             dots = lax.dot_general(part(x_ref, i), part(x_ref, j), NT, preferred_element_type=F32)
             fold = fold_lanes(dots * lanes(info_ref, 0, j) + lanes(info_ref, 1, j))
-            fold_ref[...] = fold if j == i + 1 else jnp.maximum(fold_ref[...], fold)
+            best = fold if j == i + 1 else jnp.maximum(best, fold)
             down = jnp.max(dots * inv + bias, axis=0, keepdims=True)
             best_ref[:, j * TILE : (j + 1) * TILE] = jnp.maximum(lanes(best_ref, 0, j), down)
-        best = to_row(jnp.max(fold_ref[...], axis=1, keepdims=True))
+        best = to_row(jnp.max(best, axis=1, keepdims=True))
         best_ref[:, i * TILE : (i + 1) * TILE] = jnp.maximum(lanes(best_ref, 0, i), best)
 
 
@@ -273,7 +273,7 @@
     block = 2 * SLOTS * SLOTS * WIDTH
     here = pl.BlockSpec(memory_space=pltpu.VMEM)
     whole = struct((1, ROWS), jnp.int32)
-    rank, slot = call(rank_kernel, (whole, whole), 3e10)(ids)
+    rank, slot = call(rank_kernel, (whole, whole), 3e10)(chip_of(ids))
     send = call(pack_kernel, struct((SLOTS, WIDTH), BF16), 2 * SLOTS * ROWS * WIDTH)(
         slot, embeddings
     )
@@ -285,8 +285,7 @@
     row = struct((1, SLOTS), F32)
     info, best = call(diagonal_kernel, (struct((3, SLOTS), F32), row), block / 4)(mine)
     sib_info = lax.ppermute(info, "core", swap)
-    fold = pltpu.VMEM((TILE, 128), F32)
-    best = call(own_kernel, row, block * 3 / 8, (fold,))(mine, info, best)
+    best = call(own_kernel, row, block / 4)(mine, info, best)
     line = struct((16, 128), F32)
     best, give = call(
         across_kernel,

time: 132 us -> 132 us (level)
  no operation moved by 1% of the time
where the time goes in v16:
time: 132 us
  blocking collectives  104 us (79%)
  Pallas kernels  17.4 us (13%)
  starting transfers between devices  4.63 us (4%)
  waiting for transfers between devices  3.51 us (3%)
    all_to_all x1, blocking collectives, shards(): lax.all_to_all(send.reshape(CHIPS, CAP, WIDTH), chips, 0, 0, tiled=True)  89.5 us
    all_to_all x1, blocking collectives, shards(): back = lax.all_to_all(out, ('z', 'y'), 0, 0, tiled=True)  14.5 us
    pallas_call x1, Pallas kernels, shards(): call(across_kernel, (row, row), block / 2, (pltpu.VMEM((SLOTS, WIDTH), BF...  6.04 us
    ppermute x3, starting transfers between devices, shards(): lax.ppermute(outs[k], 'x', [(i, (i + k) % XS) for i in range(XS)])  3.73 us
    pallas_call x1, Pallas kernels, shards(): call(pack_kernel, struct((SLOTS, WIDTH), BF16), 2 * SLOTS * ROWS * WIDTH)  3.61 us
    ppermute x3, waiting for transfers between devices, shards(): lax.ppermute(outs[k], 'x', [(i, (i + k) % XS) for i in range(XS)])  3.32 us
    pallas_call x1, Pallas kernels, shards(): call(diagonal_kernel, (struct((3, SLOTS), F32), row), block / 4)(mine)  2.81 us
  transfers between devices with their start and end apart: 6, of which 3 were waited for; matrix products, arithmetic and copies ran while one was open for 0% of the time, Pallas kernels for 5%

profile of v16, /device:TPU:2, one launch (start us, length us, event | category | flops | bytes accessed | tf_op | source)
XLA Modules:
  0.0 131.9 jit_solution(17451622844754227809)
XLA Ops:
  0.6 0.7 shift-right-arithmetic_add_fusion.chip_ref
  1.3 0.0 copy-start.1
  1.3 0.5 shard_map.49
  1.8 0.9 copy-done.1
  2.7 3.6 %shard_map.50 = bf16[2048,768]{1,0:T(8,128)(2,1)S(1)} custom-call(s32[1,1024]{1,0:T(1,128)S(1)} %get-tuple-element.19.slot_ref, bf16[1024,768]{1,0:T(8,128)(2,1)S(1)} %copy-done.1), custom_call_target="tpu_custom_call" | custom-call | flops 3221225472 | bytes 6000000 | tf_op jit(solution)/shard_map/pallas_call | solution.py:277
  6.4 89.5 %all_to_all.16 = bf16[128,16,768]{2,1,0:T(8,128)(2,1)S(1)} all-to-all(bf16[128,16,768]{2,1,0:T(8,128)(2,1)S(1)} %bitcast.15), channel_id=1, replica_groups=mesh['y'=4,'z'=8,'core'=2,'x'=4] {'x','z','y'}, dimensions={0} | all-to-all | bytes 6291456 | tf_op jit(solution)/shard_map/all_to_all | solution.py:281
  95.9 0.0 collective-permute-start
  95.9 2.8 %shard_map.51 = (f32[3,2048]{1,0:T(4,128)S(1)}, f32[1,2048]{1,0:T(1,128)S(1)}) custom-call(bf16[2048,768]{1,0:T(8,128)(2,1)S(1)} %bitcast.11), custom_call_target="tpu_custom_call" | custom-call | flops 1610612736 | bytes 6000000 | tf_op jit(solution)/shard_map/pallas_call | solution.py:286
  98.7 0.8 collective-permute-start.1
  99.5 2.3 %shard_map.52.before_ref = f32[1,2048]{1,0:T(1,128)S(1)} custom-call(bf16[2048,768]{1,0:T(8,128)(2,1)S(1)} %bitcast.12, f32[3,2048]{1,0:T(4,128)S(1)} %get-tuple-element.20.info_ref, f32[1,2048]{1,0:T(1,128)S(1)} %get-tuple-element.21.before_ref), custom_call_target="tpu_custom_call" | custom-call | flops 1610612736 | bytes 6000000 | tf_op jit(solution)/shard_map/pallas_call | solution.py:288
  101.8 0.0 collective-permute-done.1.sib_info_ref
  101.8 0.0 collective-permute-done.sib_hbm
  101.8 6.0 %shard_map.53 = (f32[1,2048]{1,0:T(1,128)S(1)}, f32[1,2048]{1,0:T(1,128)S(1)}) custom-call(bf16[2048,768]{1,0:T(8,128)(2,1)S(1)} %bitcast.13, bf16[2048,768]{1,0:T(8,128)(2,1)S(1)} %collective-permute-done.sib_hbm, f32[3,2048]{1,0:T(4,128)S(1)} %get-tuple-element.20.info_ref, f32[3,2048]{1,0:T(4,128)S(1)} %collective-permute-done.1.sib_info_ref, ...), custom_call_target="tpu_custom_call" | custom-call | flops 3221225472 | bytes 6000000 | tf_op jit(solution)/shard_map/pallas_call | solution.py:290
  107.9 0.0 copy-start
  107.9 0.1 collective-permute-start.2
  108.0 0.9 shard_map.54
  109.0 0.2 collective-permute-done.2.taken_ref
  109.2 0.2 collective-permute-start.3
  109.4 3.2 %collective-permute-start.4 = (f32[16,128]{1,0:T(8,128)S(1)}, f32[16,128]{1,0:T(8,128)S(1)}, u32[]{:S(2)}, u32[]{:S(2)}) collective-permute-start(f32[16,128]{1,0:T(8,128)S(1)} %get-tuple-element.28), channel_id=1, source_target_pairs={{0,2},{1,3},{2,0},{3,1},{4,6},{5,7},{6,4},{7,5},{8,10},{9,11},{10,... | collective-permute-start | bytes 24584 | tf_op jit(solution)/shard_map/ppermute | solution.py:313
  112.6 0.3 collective-permute-start.5
  112.9 0.0 collective-permute-done.3.refs_1_
  112.9 1.7 %collective-permute-done.4.refs_2_ = f32[16,128]{1,0:T(8,128)S(1)} collective-permute-done((f32[16,128]{1,0:T(8,128)S(1)}, f32[16,128]{1,0:T(8,128)S(1)}, u32[]{:S(2)}, u32[]{:S(2)}) %collective-permute-start.4) | collective-permute-done | bytes 8224 | tf_op jit(solution)/shard_map/ppermute | solution.py:313
  114.6 1.6 %collective-permute-done.5.refs_3_ = f32[16,128]{1,0:T(8,128)S(1)} collective-permute-done((f32[16,128]{1,0:T(8,128)S(1)}, f32[16,128]{1,0:T(8,128)S(1)}, u32[]{:S(2)}, u32[]{:S(2)}) %collective-permute-start.5) | collective-permute-done | bytes 8224 | tf_op jit(solution)/shard_map/ppermute | solution.py:313
  116.2 0.1 shard_map.56
  116.3 14.5 %all_to_all.17 = f32[32,1,128]{2,1,0:T(1,128)S(1)} all-to-all(f32[32,1,128]{2,1,0:T(1,128)S(1)} %bitcast.16), channel_id=1, replica_groups=mesh['y'=4,'z'=8,'core'=2,'x'=4] {'z','y'}, dimensions={0} | all-to-all | bytes 32768 | tf_op jit(solution)/shard_map/all_to_all | solution.py:315
  130.9 0.0 copy-done
  130.9 1.0 shard_map.57
  (1 shorter events, 0.0 us)
Async XLA Ops:
  1.3 1.4 %copy-start.1 = (bf16[1024,768]{1,0:T(8,128)(2,1)S(1)}, bf16[1024,768]{1,0:T(8,128)(2,1)}, u32[]{:S(2)}) copy-start(bf16[1024,768]{1,0:T(8,128)(2,1)} %x_ref.1) | copy-start | bytes 4718596
  95.9 5.9 %collective-permute-start = (bf16[2048,768]{1,0:T(8,128)(2,1)S(1)}, bf16[2048,768]{1,0:T(8,128)(2,1)S(1)}, u32[]{:S(2)}, u32[]{:S(2)}) collective-permute-start(bf16[2048,768]{1,0:T(8,128)(2,1)S(1)} %bitcast.10), channel_id=1, source_target_pairs={{0,4},{4,0},{1,5},{5,1},{2,6},{6,2},{3,7},{7,3},{8,12},{12,8},{9,1... | collective-permute-start | bytes 9437192 | tf_op jit(solution)/shard_map/ppermute | solution.py:284
  98.7 3.1 %collective-permute-start.1 = (f32[3,2048]{1,0:T(4,128)S(1)}, f32[3,2048]{1,0:T(4,128)S(1)}, u32[]{:S(2)}, u32[]{:S(2)}) collective-permute-start(f32[3,2048]{1,0:T(4,128)S(1)} %get-tuple-element.20.info_ref), channel_id=1, source_target_pairs={{0,4},{4,0},{1,5},{5,1},{2,6},{6,2},{3,7},{7,3},{8,12},{12,8},{9,1... | collective-permute-start | bytes 73736 | tf_op jit(solution)/shard_map/ppermute | solution.py:287
  107.9 23.0 %copy-start = (s32[1024,1]{0,1:T(1,128)S(1)}, s32[1024,1]{0,1:T(1,128)}, u32[]{:S(2)}) copy-start(s32[1024,1]{0,1:T(1,128)} %param.3) | copy-start | bytes 12292
  107.9 1.3 collective-permute-start.2
  109.2 3.7 %collective-permute-start.3 = (f32[16,128]{1,0:T(8,128)S(1)}, f32[16,128]{1,0:T(8,128)S(1)}, u32[]{:S(2)}, u32[]{:S(2)}) collective-permute-start(f32[16,128]{1,0:T(8,128)S(1)} %get-tuple-element.27), channel_id=1, source_target_pairs={{0,1},{1,2},{2,3},{3,0},{4,5},{5,6},{6,7},{7,4},{8,9},{9,10},{10,1... | collective-permute-start | bytes 24584 | tf_op jit(solution)/shard_map/ppermute | solution.py:313
  109.4 5.2 %collective-permute-start.4 = (f32[16,128]{1,0:T(8,128)S(1)}, f32[16,128]{1,0:T(8,128)S(1)}, u32[]{:S(2)}, u32[]{:S(2)}) collective-permute-start(f32[16,128]{1,0:T(8,128)S(1)} %get-tuple-element.28), channel_id=1, source_target_pairs={{0,2},{1,3},{2,0},{3,1},{4,6},{5,7},{6,4},{7,5},{8,10},{9,11},{10,... | collective-permute-start | bytes 24584 | tf_op jit(solution)/shard_map/ppermute | solution.py:313
  112.6 3.7 %collective-permute-start.5 = (f32[16,128]{1,0:T(8,128)S(1)}, f32[16,128]{1,0:T(8,128)S(1)}, u32[]{:S(2)}, u32[]{:S(2)}) collective-permute-start(f32[16,128]{1,0:T(8,128)S(1)} %get-tuple-element.29), channel_id=1, source_target_pairs={{0,3},{1,0},{2,1},{3,2},{4,7},{5,4},{6,5},{7,6},{8,11},{9,8},{10,9... | collective-permute-start | bytes 24584 | tf_op jit(solution)/shard_map/ppermute | solution.py:313

commit v17 on v16

--- a/solution.py
+++ b/solution.py
@@ -273,7 +273,7 @@
     block = 2 * SLOTS * SLOTS * WIDTH
     here = pl.BlockSpec(memory_space=pltpu.VMEM)
     whole = struct((1, ROWS), jnp.int32)
-    rank, slot = call(rank_kernel, (whole, whole), 3e10)(chip_of(ids))
+    rank, slot = call(rank_kernel, (whole, whole), 1e9)(chip_of(ids))
     send = call(pack_kernel, struct((SLOTS, WIDTH), BF16), 2 * SLOTS * ROWS * WIDTH)(
         slot, embeddings
     )

time: 132 us -> 131 us (level)
  no operation moved by 1% of the time
where the time goes in v17:
time: 131 us
  blocking collectives  104 us (79%)
  Pallas kernels  17.4 us (13%)
  starting transfers between devices  4.63 us (4%)
  waiting for transfers between devices  3.51 us (3%)
    all_to_all x1, blocking collectives, shards(): lax.all_to_all(send.reshape(CHIPS, CAP, WIDTH), chips, 0, 0, tiled=True)  89.5 us
    all_to_all x1, blocking collectives, shards(): back = lax.all_to_all(out, ('z', 'y'), 0, 0, tiled=True)  14.5 us
    pallas_call x1, Pallas kernels, shards(): call(across_kernel, (row, row), block / 2, (pltpu.VMEM((SLOTS, WIDTH), BF...  6.04 us
    ppermute x3, starting transfers between devices, shards(): lax.ppermute(outs[k], 'x', [(i, (i + k) % XS) for i in range(XS)])  3.73 us
    pallas_call x1, Pallas kernels, shards(): call(pack_kernel, struct((SLOTS, WIDTH), BF16), 2 * SLOTS * ROWS * WIDTH)  3.61 us
    ppermute x3, waiting for transfers between devices, shards(): lax.ppermute(outs[k], 'x', [(i, (i + k) % XS) for i in range(XS)])  3.32 us
    pallas_call x1, Pallas kernels, shards(): call(diagonal_kernel, (struct((3, SLOTS), F32), row), block / 4)(mine)  2.81 us
  transfers between devices with their start and end apart: 6, of which 3 were waited for; matrix products, arithmetic and copies ran while one was open for 0% of the time, Pallas kernels for 5%

profile of v17, /device:TPU:2, one launch (start us, length us, event | category | flops | bytes accessed | tf_op | source)
XLA Modules:
  0.0 131.2 jit_solution(8874618797138795082)
XLA Ops:
  0.6 0.0 copy-start.1
  0.6 0.8 shift-right-arithmetic_add_fusion.chip_ref
  1.5 0.5 shard_map.49
  1.9 0.1 copy-done.1
  2.1 3.6 %shard_map.50 = bf16[2048,768]{1,0:T(8,128)(2,1)S(1)} custom-call(s32[1,1024]{1,0:T(1,128)S(1)} %get-tuple-element.19.slot_ref, bf16[1024,768]{1,0:T(8,128)(2,1)S(1)} %copy-done.1), custom_call_target="tpu_custom_call" | custom-call | flops 3221225472 | bytes 6000000 | tf_op jit(solution)/shard_map/pallas_call | solution.py:277
  5.7 89.5 %all_to_all.16 = bf16[128,16,768]{2,1,0:T(8,128)(2,1)S(1)} all-to-all(bf16[128,16,768]{2,1,0:T(8,128)(2,1)S(1)} %bitcast.15), channel_id=1, replica_groups=mesh['y'=4,'z'=8,'core'=2,'x'=4] {'x','z','y'}, dimensions={0} | all-to-all | bytes 6291456 | tf_op jit(solution)/shard_map/all_to_all | solution.py:281
  95.2 0.0 collective-permute-start
  95.2 2.8 %shard_map.51 = (f32[3,2048]{1,0:T(4,128)S(1)}, f32[1,2048]{1,0:T(1,128)S(1)}) custom-call(bf16[2048,768]{1,0:T(8,128)(2,1)S(1)} %bitcast.11), custom_call_target="tpu_custom_call" | custom-call | flops 1610612736 | bytes 6000000 | tf_op jit(solution)/shard_map/pallas_call | solution.py:286
  98.0 0.8 collective-permute-start.1
  98.8 2.3 %shard_map.52.before_ref = f32[1,2048]{1,0:T(1,128)S(1)} custom-call(bf16[2048,768]{1,0:T(8,128)(2,1)S(1)} %bitcast.12, f32[3,2048]{1,0:T(4,128)S(1)} %get-tuple-element.20.info_ref, f32[1,2048]{1,0:T(1,128)S(1)} %get-tuple-element.21.before_ref), custom_call_target="tpu_custom_call" | custom-call | flops 1610612736 | bytes 6000000 | tf_op jit(solution)/shard_map/pallas_call | solution.py:288
  101.1 0.0 collective-permute-done.1.sib_info_ref
  101.1 0.0 collective-permute-done.sib_hbm
  101.1 6.0 %shard_map.53 = (f32[1,2048]{1,0:T(1,128)S(1)}, f32[1,2048]{1,0:T(1,128)S(1)}) custom-call(bf16[2048,768]{1,0:T(8,128)(2,1)S(1)} %bitcast.13, bf16[2048,768]{1,0:T(8,128)(2,1)S(1)} %collective-permute-done.sib_hbm, f32[3,2048]{1,0:T(4,128)S(1)} %get-tuple-element.20.info_ref, f32[3,2048]{1,0:T(4,128)S(1)} %collective-permute-done.1.sib_info_ref, ...), custom_call_target="tpu_custom_call" | custom-call | flops 3221225472 | bytes 6000000 | tf_op jit(solution)/shard_map/pallas_call | solution.py:290
  107.2 0.0 copy-start
  107.2 0.1 collective-permute-start.2
  107.3 0.9 shard_map.54
  108.3 0.2 collective-permute-done.2.taken_ref
  108.5 0.2 collective-permute-start.3
  108.7 3.2 %collective-permute-start.4 = (f32[16,128]{1,0:T(8,128)S(1)}, f32[16,128]{1,0:T(8,128)S(1)}, u32[]{:S(2)}, u32[]{:S(2)}) collective-permute-start(f32[16,128]{1,0:T(8,128)S(1)} %get-tuple-element.28), channel_id=1, source_target_pairs={{0,2},{1,3},{2,0},{3,1},{4,6},{5,7},{6,4},{7,5},{8,10},{9,11},{10,... | collective-permute-start | bytes 24584 | tf_op jit(solution)/shard_map/ppermute | solution.py:313
  111.9 0.3 collective-permute-start.5
  112.2 0.0 collective-permute-done.3.refs_1_
  112.2 1.7 %collective-permute-done.4.refs_2_ = f32[16,128]{1,0:T(8,128)S(1)} collective-permute-done((f32[16,128]{1,0:T(8,128)S(1)}, f32[16,128]{1,0:T(8,128)S(1)}, u32[]{:S(2)}, u32[]{:S(2)}) %collective-permute-start.4) | collective-permute-done | bytes 8224 | tf_op jit(solution)/shard_map/ppermute | solution.py:313
  113.9 1.6 %collective-permute-done.5.refs_3_ = f32[16,128]{1,0:T(8,128)S(1)} collective-permute-done((f32[16,128]{1,0:T(8,128)S(1)}, f32[16,128]{1,0:T(8,128)S(1)}, u32[]{:S(2)}, u32[]{:S(2)}) %collective-permute-start.5) | collective-permute-done | bytes 8224 | tf_op jit(solution)/shard_map/ppermute | solution.py:313
  115.5 0.1 shard_map.56
  115.7 14.5 %all_to_all.17 = f32[32,1,128]{2,1,0:T(1,128)S(1)} all-to-all(f32[32,1,128]{2,1,0:T(1,128)S(1)} %bitcast.16), channel_id=1, replica_groups=mesh['y'=4,'z'=8,'core'=2,'x'=4] {'z','y'}, dimensions={0} | all-to-all | bytes 32768 | tf_op jit(solution)/shard_map/all_to_all | solution.py:315
  130.2 0.0 copy-done
  130.2 1.0 shard_map.57
  (1 shorter events, 0.0 us)
Async XLA Ops:
  0.6 1.4 %copy-start.1 = (bf16[1024,768]{1,0:T(8,128)(2,1)S(1)}, bf16[1024,768]{1,0:T(8,128)(2,1)}, u32[]{:S(2)}) copy-start(bf16[1024,768]{1,0:T(8,128)(2,1)} %x_ref.1) | copy-start | bytes 4718596
  95.2 5.9 %collective-permute-start = (bf16[2048,768]{1,0:T(8,128)(2,1)S(1)}, bf16[2048,768]{1,0:T(8,128)(2,1)S(1)}, u32[]{:S(2)}, u32[]{:S(2)}) collective-permute-start(bf16[2048,768]{1,0:T(8,128)(2,1)S(1)} %bitcast.10), channel_id=1, source_target_pairs={{0,4},{4,0},{1,5},{5,1},{2,6},{6,2},{3,7},{7,3},{8,12},{12,8},{9,1... | collective-permute-start | bytes 9437192 | tf_op jit(solution)/shard_map/ppermute | solution.py:284
  98.0 3.1 %collective-permute-start.1 = (f32[3,2048]{1,0:T(4,128)S(1)}, f32[3,2048]{1,0:T(4,128)S(1)}, u32[]{:S(2)}, u32[]{:S(2)}) collective-permute-start(f32[3,2048]{1,0:T(4,128)S(1)} %get-tuple-element.20.info_ref), channel_id=1, source_target_pairs={{0,4},{4,0},{1,5},{5,1},{2,6},{6,2},{3,7},{7,3},{8,12},{12,8},{9,1... | collective-permute-start | bytes 73736 | tf_op jit(solution)/shard_map/ppermute | solution.py:287
  107.2 23.0 %copy-start = (s32[1024,1]{0,1:T(1,128)S(1)}, s32[1024,1]{0,1:T(1,128)}, u32[]{:S(2)}) copy-start(s32[1024,1]{0,1:T(1,128)} %param.3) | copy-start | bytes 12292
  107.2 1.3 collective-permute-start.2
  108.5 3.7 %collective-permute-start.3 = (f32[16,128]{1,0:T(8,128)S(1)}, f32[16,128]{1,0:T(8,128)S(1)}, u32[]{:S(2)}, u32[]{:S(2)}) collective-permute-start(f32[16,128]{1,0:T(8,128)S(1)} %get-tuple-element.27), channel_id=1, source_target_pairs={{0,1},{1,2},{2,3},{3,0},{4,5},{5,6},{6,7},{7,4},{8,9},{9,10},{10,1... | collective-permute-start | bytes 24584 | tf_op jit(solution)/shard_map/ppermute | solution.py:313
  108.7 5.2 %collective-permute-start.4 = (f32[16,128]{1,0:T(8,128)S(1)}, f32[16,128]{1,0:T(8,128)S(1)}, u32[]{:S(2)}, u32[]{:S(2)}) collective-permute-start(f32[16,128]{1,0:T(8,128)S(1)} %get-tuple-element.28), channel_id=1, source_target_pairs={{0,2},{1,3},{2,0},{3,1},{4,6},{5,7},{6,4},{7,5},{8,10},{9,11},{10,... | collective-permute-start | bytes 24584 | tf_op jit(solution)/shard_map/ppermute | solution.py:313
  111.9 3.7 %collective-permute-start.5 = (f32[16,128]{1,0:T(8,128)S(1)}, f32[16,128]{1,0:T(8,128)S(1)}, u32[]{:S(2)}, u32[]{:S(2)}) collective-permute-start(f32[16,128]{1,0:T(8,128)S(1)} %get-tuple-element.29), channel_id=1, source_target_pairs={{0,3},{1,0},{2,1},{3,2},{4,7},{5,4},{6,5},{7,6},{8,11},{9,8},{10,9... | collective-permute-start | bytes 24584 | tf_op jit(solution)/shard_map/ppermute | solution.py:313
